TPU v7x, 32 devices: a whole 2x2x4 slice. The times are simulated.
32 devices in a mesh: ctx: 8 (over z, y), head: 4 (over x, core).
Axes of the slice: x: 2, y: 2, z: 4, core: 2. Of those that a mesh axis runs over, the one named last changes fastest.
Arguments:
- queries: bfloat16 [4096, 32, 128], P(('ctx', 'head')), may hold values from -1.796875 to 1.796875
- key_vectors: bfloat16 [4096, 32, 128], P(('ctx', 'head')), may hold values from -1.796875 to 1.796875
- value_vectors: bfloat16 [4096, 32, 128], P(('ctx', 'head')), may hold values from -9.9 to 9.9
- output_grad: bfloat16 [4096, 32, 128], P(('ctx', 'head')), may hold values from -9.9 to 9.9
- decay_rate: float32 [32], replicated, may hold values from 0 to 1, as said below
- norm_gain: float32 [32, 128], replicated, may hold values from 0.25 to 1.75
Outputs:
- normed: bfloat16 [4096, 32, 128], P(('ctx', 'head'))
- query_gradient: bfloat16 [4096, 32, 128], P(('ctx', 'head'))
- grad_keys: bfloat16 [4096, 32, 128], P(('ctx', 'head'))
- value_gradient: bfloat16 [4096, 32, 128], P(('ctx', 'head'))
Inputs may be any that keep to these rules, and one draw needn't show every extreme that they name: `decay_rate`: each head's rate is positive; a head's state is multiplied by exp(-rate) at every position.
All inputs are finite; a program needn't handle non-finite values.
Results may differ from a plain program's by a relative error of at most 0.012.
Values may be sent and summed in bfloat16 or wider, within the bound.
No kernel may reach another device: no remote copies, remote signals or barrier semaphores. Data moves between devices by JAX's collectives and lax.ppermute only.
A program may use at most 128 MiB of HBM per device.

v0:
```python
import jax
import jax.numpy as jnp
from jax import lax
from jax.sharding import PartitionSpec as P


def row_rates_here(head_rates, head_size, piece_rows):
    all_rates = jnp.repeat(head_rates, head_size)
    return lax.dynamic_slice_in_dim(all_rates, lax.axis_index("ctx") * piece_rows, piece_rows, 0)


def local_chain(spread_rows, rates_here, span_length, forward):
    row_decay = jnp.exp(-rates_here * span_length)[:, None]

    def carry_step(state, piece):
        return (row_decay * state + piece.astype(jnp.float32), state)

    empty_rows = jnp.zeros(spread_rows.shape[1:], jnp.float32)
    final_rows, carried_rows = lax.scan(carry_step, empty_rows, spread_rows, reverse=not forward)
    return carried_rows


def carry_states(stretch_states, head_rates, length, forward):
    group_size = stretch_states.shape[0]
    heads_here = stretch_states.shape[1]
    head_size = stretch_states.shape[2]
    stretch_order = jnp.arange(group_size).astype(jnp.float32)
    if forward:
        place_in = stretch_order
    else:
        place_in = group_size - 1.0 - stretch_order
    states_float = stretch_states.astype(jnp.float32)
    fold_weights = jnp.exp(-head_rates[None, :] * length * (group_size - 1.0 - place_in)[:, None])
    block_state = jnp.einsum(
        "kh,khde->hde", fold_weights, states_float, precision=lax.Precision.HIGHEST
    ).astype(jnp.bfloat16)
    span_length = length * group_size
    total_rows = heads_here * head_size
    piece_rows = total_rows // lax.axis_size("ctx")
    flat_rows = block_state.reshape(1, total_rows, head_size)
    rates_here = row_rates_here(head_rates, head_size, piece_rows)
    if forward:
        spread_rows = lax.all_to_all(flat_rows, "ctx", split_axis=1, concat_axis=0, tiled=True)
        carried_rows = local_chain(spread_rows, rates_here, span_length, True)
        carried = (
            lax.all_to_all(
                carried_rows.astype(jnp.bfloat16), "ctx", split_axis=0, concat_axis=1, tiled=True
            )
            .astype(carried_rows.dtype)
            .reshape(heads_here, head_size, head_size)
        )
    else:
        spread_rows = lax.all_to_all(flat_rows, "ctx", split_axis=1, concat_axis=0, tiled=True)
        carried_rows = local_chain(spread_rows, rates_here, span_length, False)
        carried = (
            lax.all_to_all(
                carried_rows.astype(jnp.bfloat16), "ctx", split_axis=0, concat_axis=1, tiled=True
            )
            .astype(carried_rows.dtype)
            .reshape(heads_here, head_size, head_size)
        )
    lead_decay = jnp.exp(-head_rates[None, :] * length * place_in[:, None])
    stretch_gap = place_in[:, None] - 1.0 - place_in[None, :]
    inner_weights = jnp.where(
        (stretch_gap >= 0)[:, :, None],
        jnp.exp(-head_rates[None, None, :] * length * jnp.maximum(stretch_gap, 0.0)[:, :, None]),
        0.0,
    )
    spread = lead_decay[:, :, None, None] * carried[None] + jnp.einsum(
        "kqh,qhde->khde", inner_weights, states_float, precision=lax.Precision.HIGHEST
    )
    return spread.astype(jnp.bfloat16)


def local(queries, key_vectors, value_vectors, output_grad, decay_rate, norm_gain):
    group_size = lax.axis_size("head")
    heads_group = decay_rate.shape[0] // group_size
    first_head = lax.axis_index("head") * heads_group
    group_rates = lax.dynamic_slice_in_dim(decay_rate, first_head, heads_group, 0)
    head_size = queries.shape[2]
    query_block, key_block, value_block, grad_block = (
        lax.all_to_all(queries, "head", split_axis=1, concat_axis=0, tiled=True),
        lax.all_to_all(key_vectors, "head", split_axis=1, concat_axis=0, tiled=True),
        lax.all_to_all(value_vectors, "head", split_axis=1, concat_axis=0, tiled=True),
        lax.all_to_all(output_grad, "head", split_axis=1, concat_axis=0, tiled=True),
    )
    length = query_block.shape[0] // group_size
    stretch_shape = (group_size, length, heads_group, head_size)
    query_stretches = query_block.reshape(stretch_shape)
    key_stretches = key_block.reshape(stretch_shape)
    value_stretches = value_block.reshape(stretch_shape)
    grad_stretches = grad_block.reshape(stretch_shape)
    head_gains = lax.dynamic_slice_in_dim(norm_gain, first_head, heads_group, 0)
    steps = jnp.arange(length).astype(jnp.float32)
    offset = steps[:, None] - steps[None, :]
    decay_weight_mask = jnp.where(
        offset[None] >= 0,
        jnp.exp(-group_rates[:, None, None] * jnp.maximum(offset, 0.0)[None]),
        0.0,
    )
    per_head_decay = jnp.exp(-group_rates[None, :] * (steps[:, None] + 1.0))[None, :, :, None]
    trailing_decay = jnp.exp(-group_rates[None, :] * (length - 1.0 - steps[:, None]))[
        None, :, :, None
    ]
    key_decayed = (key_stretches.astype(jnp.float32) * trailing_decay).astype(jnp.bfloat16)
    local_state = jnp.einsum(
        "kjhd,kjhe->khde", key_decayed, value_stretches, preferred_element_type=jnp.float32
    ).astype(jnp.bfloat16)
    incoming_portion = carry_states(local_state, group_rates, length, True)
    scores = jnp.einsum(
        "kihd,kjhd->khij", query_stretches, key_stretches, preferred_element_type=jnp.float32
    )
    attention_matrix = (scores * decay_weight_mask[None]).astype(jnp.bfloat16)
    output_rows = jnp.einsum(
        "khij,kjhe->kihe", attention_matrix, value_stretches, preferred_element_type=jnp.float32
    )
    output_rows = output_rows + per_head_decay * jnp.einsum(
        "kihd,khde->kihe", query_stretches, incoming_portion, preferred_element_type=jnp.float32
    )
    inv_rms = lax.rsqrt(jnp.mean(output_rows * output_rows, axis=-1, keepdims=True) + 1e-06)
    unit_rows = output_rows * inv_rms
    gain_float = head_gains[None, None]
    normed = (unit_rows * gain_float).astype(jnp.bfloat16)
    scaled = gain_float * grad_stretches.astype(jnp.float32)
    grad_out = (
        inv_rms * (scaled - unit_rows * jnp.mean(scaled * unit_rows, axis=-1, keepdims=True))
    ).astype(jnp.bfloat16)
    query_with_decay = (query_stretches.astype(jnp.float32) * per_head_decay).astype(jnp.bfloat16)
    state_gradient = jnp.einsum(
        "kihd,kihe->khde", query_with_decay, grad_out, preferred_element_type=jnp.float32
    ).astype(jnp.bfloat16)
    later_portion = carry_states(state_gradient, group_rates, length, False)
    score_gradient = (
        jnp.einsum("kihe,kjhe->khij", grad_out, value_stretches, preferred_element_type=jnp.float32)
        * decay_weight_mask[None]
    ).astype(jnp.bfloat16)
    query_gradient = jnp.einsum(
        "khij,kjhd->kihd", score_gradient, key_stretches, preferred_element_type=jnp.float32
    )
    query_gradient = query_gradient + per_head_decay * jnp.einsum(
        "kihe,khde->kihd", grad_out, incoming_portion, preferred_element_type=jnp.float32
    )
    grad_keys = jnp.einsum(
        "khij,kihd->kjhd", score_gradient, query_stretches, preferred_element_type=jnp.float32
    )
    grad_keys = grad_keys + trailing_decay * jnp.einsum(
        "kjhe,khde->kjhd", value_stretches, later_portion, preferred_element_type=jnp.float32
    )
    value_gradient = jnp.einsum(
        "khij,kihe->kjhe", attention_matrix, grad_out, preferred_element_type=jnp.float32
    )
    value_gradient = value_gradient + trailing_decay * jnp.einsum(
        "kjhd,khde->kjhe", key_stretches, later_portion, preferred_element_type=jnp.float32
    )
    results = (
        normed,
        query_gradient.astype(jnp.bfloat16),
        grad_keys.astype(jnp.bfloat16),
        value_gradient.astype(jnp.bfloat16),
    )
    flat_shape = (group_size * length, heads_group, head_size)
    returned = (
        lax.all_to_all(
            results[0].reshape(flat_shape), "head", split_axis=0, concat_axis=1, tiled=True
        ),
        lax.all_to_all(
            results[1].reshape(flat_shape), "head", split_axis=0, concat_axis=1, tiled=True
        ),
        lax.all_to_all(
            results[2].reshape(flat_shape), "head", split_axis=0, concat_axis=1, tiled=True
        ),
        lax.all_to_all(
            results[3].reshape(flat_shape), "head", split_axis=0, concat_axis=1, tiled=True
        ),
    )
    return returned


def solution(mesh):
    in_specs = (
        P(("ctx", "head"), None, None),
        P(("ctx", "head"), None, None),
        P(("ctx", "head"), None, None),
        P(("ctx", "head"), None, None),
        P(),
        P(),
    )
    out_specs = (
        P(("ctx", "head"), None, None),
        P(("ctx", "head"), None, None),
        P(("ctx", "head"), None, None),
        P(("ctx", "head"), None, None),
    )
    return jax.shard_map(local, mesh=mesh, in_specs=in_specs, out_specs=out_specs, check_vma=False)
```

profile of v0, /device:TPU:0, one launch (start us, length us, event | category | flops | bytes accessed | tf_op | source)
XLA Modules:
  0.0 225.5 jit_solution(12125105259696826864)
XLA Ops:
  3.4 4.3 %all-to-all-start.1 = ((bf16[128,32,128]{2,0,1:T(8,128)(2,1)}), bf16[128,32,128]{2,0,1:T(8,128)(2,1)S(1)}, u32[]{:S(2)}, u32[]{:S(2)}) async-start(bf16[128,32,128]{2,0,1:T(8,128)(2,1)} %copy.87), calls=%async_computation.1 | async-start | bytes 2097152 | tf_op jit(solution)/shard_map/all_to_all | solution.py:83
  15.0 7.1 %all-to-all-done.1 = bf16[128,32,128]{2,0,1:T(8,128)(2,1)S(1)} async-done(((bf16[128,32,128]{2,0,1:T(8,128)(2,1)}), bf16[128,32,128]{2,0,1:T(8,128)(2,1)S(1)}, u32[]{:S(2)}, u32[]{:S(2)}) %all-to-all-start.1) | async-done | bytes 1048608 | tf_op jit(solution)/shard_map/all_to_all | solution.py:83
  27.2 12.9 %all-to-all-done.2 = bf16[128,32,128]{2,0,1:T(8,128)(2,1)S(1)} async-done(((bf16[128,32,128]{2,0,1:T(8,128)(2,1)}), bf16[128,32,128]{2,0,1:T(8,128)(2,1)S(1)}, u32[]{:S(2)}, u32[]{:S(2)}) %all-to-all-start.2) | async-done | bytes 1048608 | tf_op jit(solution)/shard_map/all_to_all | solution.py:84
  46.9 6.6 %all-to-all-start.3 = ((bf16[8,2,8192]{2,1,0:T(2,128)(2,1)}), bf16[8,2,8192]{2,1,0:T(2,128)(2,1)S(1)}, u32[]{:S(2)}, u32[]{:S(2)}) async-start(bf16[8,2,8192]{2,1,0:T(2,128)(2,1)} %reshape.428), calls=%async_computation.3 | async-start | bytes 524288 | tf_op jit(solution)/shard_map/all_to_all | solution.py:43
  55.0 7.1 %all-to-all-done.3 = bf16[8,2,8192]{2,1,0:T(2,128)(2,1)S(1)} async-done(((bf16[8,2,8192]{2,1,0:T(2,128)(2,1)}), bf16[8,2,8192]{2,1,0:T(2,128)(2,1)S(1)}, u32[]{:S(2)}, u32[]{:S(2)}) %all-to-all-start.3) | async-done | bytes 262176 | tf_op jit(solution)/shard_map/all_to_all | solution.py:43
  68.5 7.2 %while.30 = (s32[]{:T(128)}, f32[128,128]{1,0:T(8,128)S(1)}, bf16[8,128,128]{2,1,0:T(8,128)(2,1)S(1)}, f32[128,1]{0,1:T(1,128)}, bf16[8,128,128]{2,1,0:T(8,128)(2,1)}, /*index=5*/s32[]{:T(128)}, s32[]{:T(128)}) while((s32[]{:T(128)}, f32[128,128]{1,0:T(8,128)S(1)}, bf16[8,128,128]{2,1,0:T(8,128)(2,1)S(1)}, f32[128,1]{0,1:T(1,128)}, ...), condition=%wide.region_1.2_spmd.clone, body=%wide.region_0.1_spmd.clone.sunk | while | flops 81923 | bytes 262760 | solution.py:19
  75.7 4.4 %all-to-all-done = bf16[128,32,128]{2,0,1:T(8,128)(2,1)S(1)} async-done(((bf16[128,32,128]{2,0,1:T(8,128)(2,1)}), bf16[128,32,128]{2,0,1:T(8,128)(2,1)S(1)}, u32[]{:S(2)}, u32[]{:S(2)}) %all-to-all-start) | async-done | bytes 1048608 | tf_op jit(solution)/shard_map/all_to_all | solution.py:82
  80.1 3.6 %all-to-all-start.4 = ((bf16[8,128,128]{2,1,0:T(8,128)(2,1)}), bf16[8,128,128]{2,1,0:T(8,128)(2,1)S(1)}, u32[]{:S(2)}, u32[]{:S(2)}) async-start(bf16[8,128,128]{2,1,0:T(8,128)(2,1)} %copy-done.19), calls=%async_computation.4 | async-start | bytes 524288 | tf_op jit(solution)/shard_map/all_to_all | solution.py:46
  88.4 4.1 %all-to-all-done.4 = bf16[8,128,128]{2,1,0:T(8,128)(2,1)S(1)} async-done(((bf16[8,128,128]{2,1,0:T(8,128)(2,1)}), bf16[8,128,128]{2,1,0:T(8,128)(2,1)S(1)}, u32[]{:S(2)}, u32[]{:S(2)}) %all-to-all-start.4) | async-done | bytes 262176 | tf_op jit(solution)/shard_map/all_to_all | solution.py:46
  92.5 4.4 %all-to-all-start.6 = ((bf16[128,32,128]{2,0,1:T(8,128)(2,1)}), bf16[128,32,128]{2,0,1:T(8,128)(2,1)}, u32[]{:S(2)}, u32[]{:S(2)}) async-start(bf16[128,32,128]{2,0,1:T(8,128)(2,1)} %copy.95), calls=%async_computation.6 | async-start | bytes 2097152 | tf_op jit(solution)/shard_map/all_to_all | solution.py:85
  97.1 3.7 %fusion.14 = bf16[4,8,128,128]{3,0,2,1:T(4,128)(2,1)S(1)} fusion(f32[8,128,128]{2,1,0:T(8,128)S(1)} %convert_element_type.168, f32[4,8]{0,1:T(8,128)S(1)} %copy-done.28, bf16[4,8,128,128]{3,2,1,0:T(8,128)(2,1)} %copy-done.17, f32[4,4]{1,0:T(4,128)S(1)} %copy-done.30, f32[8]{0:T(128)S(1)} %copy-done.32, pred[4,4]{1,0:T(4,128)(4,1)S(1)} %copy-done.45), kind=kOutput, calls=%fused_computation.25 | convolution fusion | flops 26738944 | bytes 2621680 | tf_op jit(solution)/shard_map/kqh,qhde->khde/dot_general | solution.py:69
  102.7 8.6 %all-to-all-done.6 = bf16[128,32,128]{2,0,1:T(8,128)(2,1)} async-done(((bf16[128,32,128]{2,0,1:T(8,128)(2,1)}), bf16[128,32,128]{2,0,1:T(8,128)(2,1)}, u32[]{:S(2)}, u32[]{:S(2)}) %all-to-all-start.6) | async-done | bytes 1048608 | tf_op jit(solution)/shard_map/all_to_all | solution.py:85
  125.3 3.6 %all-to-all-start.8 = ((bf16[8,2,8192]{2,1,0:T(2,128)(2,1)}), bf16[8,2,8192]{2,1,0:T(2,128)(2,1)S(1)}, u32[]{:S(2)}, u32[]{:S(2)}) async-start(bf16[8,2,8192]{2,1,0:T(2,128)(2,1)} %reshape.430), calls=%async_computation.8 | async-start | bytes 524288 | tf_op jit(solution)/shard_map/all_to_all | solution.py:53
  133.7 3.9 %all-to-all-done.8 = bf16[8,2,8192]{2,1,0:T(2,128)(2,1)S(1)} async-done(((bf16[8,2,8192]{2,1,0:T(2,128)(2,1)}), bf16[8,2,8192]{2,1,0:T(2,128)(2,1)S(1)}, u32[]{:S(2)}, u32[]{:S(2)}) %all-to-all-start.8) | async-done | bytes 262176 | tf_op jit(solution)/shard_map/all_to_all | solution.py:53
  137.7 4.2 %all-to-all-start.5 = ((bf16[512,8,128]{2,1,0:T(8,128)(2,1)}), bf16[512,8,128]{2,1,0:T(8,128)(2,1)}, u32[]{:S(2)}, u32[]{:S(2)}) async-start(bf16[512,8,128]{2,1,0:T(8,128)(2,1)} %bitcast.182), calls=%async_computation.5 | async-start | bytes 2097152 | tf_op jit(solution)/shard_map/all_to_all | solution.py:163
  144.7 7.2 %while.31 = (s32[]{:T(128)}, f32[128,128]{1,0:T(8,128)S(1)}, bf16[8,128,128]{2,1,0:T(8,128)(2,1)S(1)}, f32[128,1]{0,1:T(1,128)S(1)}, bf16[8,128,128]{2,1,0:T(8,128)(2,1)}, /*index=5*/s32[]{:T(128)}, s32[]{:T(128)}, s32[]{:T(128)}) while((s32[]{:T(128)}, f32[128,128]{1,0:T(8,128)S(1)}, bf16[8,128,128]{2,1,0:T(8,128)(2,1)S(1)}, ...), condition=%wide.region_5.6_spmd.clone, body=%wide.region_4.5_spmd.clone.sunk | while | flops 81924 | bytes 262780 | solution.py:19
  151.9 4.5 %all-to-all-done.5 = bf16[512,8,128]{2,1,0:T(8,128)(2,1)} async-done(((bf16[512,8,128]{2,1,0:T(8,128)(2,1)}), bf16[512,8,128]{2,1,0:T(8,128)(2,1)}, u32[]{:S(2)}, u32[]{:S(2)}) %all-to-all-start.5) | async-done | bytes 1048608 | tf_op jit(solution)/shard_map/all_to_all | solution.py:163
  156.5 3.6 %all-to-all-start.9 = ((bf16[8,128,128]{2,1,0:T(8,128)(2,1)}), bf16[8,128,128]{2,1,0:T(8,128)(2,1)S(1)}, u32[]{:S(2)}, u32[]{:S(2)}) async-start(bf16[8,128,128]{2,1,0:T(8,128)(2,1)} %copy-done.18), calls=%async_computation.9 | async-start | bytes 524288 | tf_op jit(solution)/shard_map/all_to_all | solution.py:56
  164.4 4.4 %all-to-all-done.9 = bf16[8,128,128]{2,1,0:T(8,128)(2,1)S(1)} async-done(((bf16[8,128,128]{2,1,0:T(8,128)(2,1)}), bf16[8,128,128]{2,1,0:T(8,128)(2,1)S(1)}, u32[]{:S(2)}, u32[]{:S(2)}) %all-to-all-start.9) | async-done | bytes 262176 | tf_op jit(solution)/shard_map/all_to_all | solution.py:56
  168.8 4.3 %all-to-all-start.7 = ((bf16[512,8,128]{2,1,0:T(8,128)(2,1)}), bf16[512,8,128]{2,1,0:T(8,128)(2,1)}, u32[]{:S(2)}, u32[]{:S(2)}) async-start(bf16[512,8,128]{2,1,0:T(8,128)(2,1)} %bitcast.183), calls=%async_computation.7 | async-start | bytes 2097152 | tf_op jit(solution)/shard_map/all_to_all | solution.py:166
  180.4 7.2 %all-to-all-done.7 = bf16[512,8,128]{2,1,0:T(8,128)(2,1)} async-done(((bf16[512,8,128]{2,1,0:T(8,128)(2,1)}), bf16[512,8,128]{2,1,0:T(8,128)(2,1)}, u32[]{:S(2)}, u32[]{:S(2)}) %all-to-all-start.7) | async-done | bytes 1048608 | tf_op jit(solution)/shard_map/all_to_all | solution.py:166
  187.6 4.2 %all-to-all-start.10 = ((bf16[512,8,128]{2,1,0:T(8,128)(2,1)}), bf16[512,8,128]{2,1,0:T(8,128)(2,1)}, u32[]{:S(2)}, u32[]{:S(2)}) async-start(bf16[512,8,128]{2,1,0:T(8,128)(2,1)} %bitcast.184), calls=%async_computation.10 | async-start | bytes 2097152 | tf_op jit(solution)/shard_map/all_to_all | solution.py:169
  195.3 11.0 %all-to-all-done.10 = bf16[512,8,128]{2,1,0:T(8,128)(2,1)} async-done(((bf16[512,8,128]{2,1,0:T(8,128)(2,1)}), bf16[512,8,128]{2,1,0:T(8,128)(2,1)}, u32[]{:S(2)}, u32[]{:S(2)}) %all-to-all-start.10) | async-done | bytes 1048608 | tf_op jit(solution)/shard_map/all_to_all | solution.py:169
  217.0 7.3 %all-to-all-done.11 = bf16[512,8,128]{2,1,0:T(8,128)(2,1)S(1)} async-done(((bf16[512,8,128]{2,1,0:T(8,128)(2,1)}), bf16[512,8,128]{2,1,0:T(8,128)(2,1)S(1)}, u32[]{:S(2)}, u32[]{:S(2)}) %all-to-all-start.11) | async-done | bytes 1048608 | tf_op jit(solution)/shard_map/all_to_all | solution.py:172
  (198 shorter events, 98.3 us)
Async XLA Ops:
  0.6 12.4 %copy-start = (f32[32,128]{1,0:T(8,128)S(1)}, f32[32,128]{1,0:T(8,128)}, u32[]{:S(2)}) copy-start(f32[32,128]{1,0:T(8,128)} %param.15) | copy-start | bytes 49156
  3.4 18.8 %all-to-all-start.1 = ((bf16[128,32,128]{2,0,1:T(8,128)(2,1)}), bf16[128,32,128]{2,0,1:T(8,128)(2,1)S(1)}, u32[]{:S(2)}, u32[]{:S(2)}) async-start(bf16[128,32,128]{2,0,1:T(8,128)(2,1)} %copy.87), calls=%async_computation.1 | async-start | bytes 2097152 | tf_op jit(solution)/shard_map/all_to_all | solution.py:83
  7.7 18.7 %copy-start.34 = (f32[4]{0:T(128)}, f32[4]{0:T(128)S(1)}, u32[]{:S(2)}) copy-start(f32[4]{0:T(128)S(1)} %broadcast_subtract_fusion.3) | copy-start | bytes 52
  7.7 18.7 %copy-start.36 = (f32[4]{0:T(128)}, f32[4]{0:T(128)S(1)}, u32[]{:S(2)}) copy-start(f32[4]{0:T(128)S(1)} %iota_convert_fusion) | copy-start | bytes 52
  8.2 18.2 %copy-start.31 = (f32[8]{0:T(128)}, f32[8]{0:T(128)S(1)}, u32[]{:S(2)}) copy-start(f32[8]{0:T(128)S(1)} %get-tuple-element.192) | copy-start | bytes 100
  15.0 25.8 %copy-start.21 = (f32[128,8]{0,1:T(8,128)}, f32[128,8]{0,1:T(8,128)S(1)}, u32[]{:S(2)}) copy-start(f32[128,8]{0,1:T(8,128)S(1)} %get-tuple-element.199) | copy-start | bytes 12292
  22.2 18.0 %all-to-all-start.2 = ((bf16[128,32,128]{2,0,1:T(8,128)(2,1)}), bf16[128,32,128]{2,0,1:T(8,128)(2,1)S(1)}, u32[]{:S(2)}, u32[]{:S(2)}) async-start(bf16[128,32,128]{2,0,1:T(8,128)(2,1)} %copy.88), calls=%async_computation.2 | async-start | bytes 2097152 | tf_op jit(solution)/shard_map/all_to_all | solution.py:84
  27.1 15.8 %copy-start.25 = (f32[4,8]{0,1:T(8,128)}, f32[4,8]{0,1:T(8,128)S(1)}, u32[]{:S(2)}) copy-start(f32[4,8]{0,1:T(8,128)S(1)} %get-tuple-element.197) | copy-start | bytes 388
  42.9 10.6 %copy-start.37 = (f32[4]{0:T(128)S(1)}, f32[4]{0:T(128)}, u32[]{:S(2)}) copy-start(f32[4]{0:T(128)} %copy-done.36) | copy-start | bytes 52
  42.9 10.6 %copy-start.44 = (f32[4]{0:T(128)S(1)}, f32[4]{0:T(128)}, u32[]{:S(2)}) copy-start(f32[4]{0:T(128)} %copy-done.43) | copy-start | bytes 52
  42.9 11.2 %copy-start.39 = (f32[8]{0:T(128)S(1)}, f32[8]{0:T(128)}, u32[]{:S(2)}) copy-start(f32[8]{0:T(128)} %copy-done.38) | copy-start | bytes 100
  46.9 15.3 %all-to-all-start.3 = ((bf16[8,2,8192]{2,1,0:T(2,128)(2,1)}), bf16[8,2,8192]{2,1,0:T(2,128)(2,1)S(1)}, u32[]{:S(2)}, u32[]{:S(2)}) async-start(bf16[8,2,8192]{2,1,0:T(2,128)(2,1)} %reshape.428), calls=%async_computation.3 | async-start | bytes 524288 | tf_op jit(solution)/shard_map/all_to_all | solution.py:43
  62.2 18.0 %all-to-all-start = ((bf16[128,32,128]{2,0,1:T(8,128)(2,1)}), bf16[128,32,128]{2,0,1:T(8,128)(2,1)S(1)}, u32[]{:S(2)}, u32[]{:S(2)}) async-start(bf16[128,32,128]{2,0,1:T(8,128)(2,1)} %copy.86), calls=%async_computation | async-start | bytes 2097152 | tf_op jit(solution)/shard_map/all_to_all | solution.py:82
  80.1 20.6 %copy-start.1 = (bf16[128,32,128]{2,0,1:T(8,128)(2,1)}, bf16[128,32,128]{2,0,1:T(8,128)(2,1)S(1)}, u32[]{:S(2)}) copy-start(bf16[128,32,128]{2,0,1:T(8,128)(2,1)S(1)} %all-to-all-done) | copy-start | bytes 3145732
  80.1 12.4 %all-to-all-start.4 = ((bf16[8,128,128]{2,1,0:T(8,128)(2,1)}), bf16[8,128,128]{2,1,0:T(8,128)(2,1)S(1)}, u32[]{:S(2)}, u32[]{:S(2)}) async-start(bf16[8,128,128]{2,1,0:T(8,128)(2,1)} %copy-done.19), calls=%async_computation.4 | async-start | bytes 524288 | tf_op jit(solution)/shard_map/all_to_all | solution.py:46
  92.5 18.8 %all-to-all-start.6 = ((bf16[128,32,128]{2,0,1:T(8,128)(2,1)}), bf16[128,32,128]{2,0,1:T(8,128)(2,1)}, u32[]{:S(2)}, u32[]{:S(2)}) async-start(bf16[128,32,128]{2,0,1:T(8,128)(2,1)} %copy.95), calls=%async_computation.6 | async-start | bytes 2097152 | tf_op jit(solution)/shard_map/all_to_all | solution.py:85
  125.3 12.4 %all-to-all-start.8 = ((bf16[8,2,8192]{2,1,0:T(2,128)(2,1)}), bf16[8,2,8192]{2,1,0:T(2,128)(2,1)S(1)}, u32[]{:S(2)}, u32[]{:S(2)}) async-start(bf16[8,2,8192]{2,1,0:T(2,128)(2,1)} %reshape.430), calls=%async_computation.8 | async-start | bytes 524288 | tf_op jit(solution)/shard_map/all_to_all | solution.py:53
  133.7 11.0 %copy-start.24 = (f32[128,1]{0,1:T(1,128)S(1)}, f32[128,1]{0,1:T(1,128)}, u32[]{:S(2)}) copy-start(f32[128,1]{0,1:T(1,128)} %get-tuple-element.336) | copy-start | bytes 1540
  137.7 18.8 %all-to-all-start.5 = ((bf16[512,8,128]{2,1,0:T(8,128)(2,1)}), bf16[512,8,128]{2,1,0:T(8,128)(2,1)}, u32[]{:S(2)}, u32[]{:S(2)}) async-start(bf16[512,8,128]{2,1,0:T(8,128)(2,1)} %bitcast.182), calls=%async_computation.5 | async-start | bytes 2097152 | tf_op jit(solution)/shard_map/all_to_all | solution.py:163
  156.5 12.4 %all-to-all-start.9 = ((bf16[8,128,128]{2,1,0:T(8,128)(2,1)}), bf16[8,128,128]{2,1,0:T(8,128)(2,1)S(1)}, u32[]{:S(2)}, u32[]{:S(2)}) async-start(bf16[8,128,128]{2,1,0:T(8,128)(2,1)} %copy-done.18), calls=%async_computation.9 | async-start | bytes 524288 | tf_op jit(solution)/shard_map/all_to_all | solution.py:56
  168.8 18.8 %all-to-all-start.7 = ((bf16[512,8,128]{2,1,0:T(8,128)(2,1)}), bf16[512,8,128]{2,1,0:T(8,128)(2,1)}, u32[]{:S(2)}, u32[]{:S(2)}) async-start(bf16[512,8,128]{2,1,0:T(8,128)(2,1)} %bitcast.183), calls=%async_computation.7 | async-start | bytes 2097152 | tf_op jit(solution)/shard_map/all_to_all | solution.py:166
  178.7 13.1 %copy-start.5 = (bf16[4,8,128,128]{3,2,1,0:T(8,128)(2,1)S(1)}, bf16[4,8,128,128]{3,2,1,0:T(8,128)(2,1)}, u32[]{:S(2)}) copy-start(bf16[4,8,128,128]{3,2,1,0:T(8,128)(2,1)} %copy-done.4) | copy-start | bytes 3145732
  187.6 18.8 %all-to-all-start.10 = ((bf16[512,8,128]{2,1,0:T(8,128)(2,1)}), bf16[512,8,128]{2,1,0:T(8,128)(2,1)}, u32[]{:S(2)}, u32[]{:S(2)}) async-start(bf16[512,8,128]{2,1,0:T(8,128)(2,1)} %bitcast.184), calls=%async_computation.10 | async-start | bytes 2097152 | tf_op jit(solution)/shard_map/all_to_all | solution.py:169
  206.4 18.0 %all-to-all-start.11 = ((bf16[512,8,128]{2,1,0:T(8,128)(2,1)}), bf16[512,8,128]{2,1,0:T(8,128)(2,1)S(1)}, u32[]{:S(2)}, u32[]{:S(2)}) async-start(bf16[512,8,128]{2,1,0:T(8,128)(2,1)} %bitcast.49), calls=%async_computation.11 | async-start | bytes 2097152 | tf_op jit(solution)/shard_map/all_to_all | solution.py:172
  (34 other events, 149.7 us)
where the time goes:
time: 228 us; the launch traced here: 225 us
  waiting for transfers between devices  82.7 us (36%)
  starting transfers between devices  49.4 us (22%)
  local copies, waits for them, and re-layouts  35.2 us (15%)
  other arithmetic  30.6 us (13%)
  matrix products  25.7 us (11%)
    unnamed x103, local copies, waits for them, and re-layouts  16.7 us
    add x16, other arithmetic, carry_step(): return (row_decay * state + piece.astype(jnp.float32), state)  13.6 us
    all_to_all x1, waiting for transfers between devices, local(): lax.all_to_all(value_vectors, 'head', split_axis=1, concat_axis=0, tiled=...  12.9 us
    all_to_all x2, waiting for transfers between devices, carry_states(): lax.all_to_all(flat_rows, 'ctx', split_axis=1, concat_axis=0, tiled=True)  11.1 us
    all_to_all x1, waiting for transfers between devices, local(): lax.all_to_all(results[2].reshape(flat_shape), 'head', split_axis=0, conc...  11 us
    all_to_all x2, starting transfers between devices, carry_states(): lax.all_to_all(flat_rows, 'ctx', split_axis=1, concat_axis=0, tiled=True)  10.1 us
    all_to_all x1, waiting for transfers between devices, local(): lax.all_to_all(output_grad, 'head', split_axis=1, concat_axis=0, tiled=True)  8.61 us
    all_to_all x2, waiting for transfers between devices, carry_states(): lax.all_to_all(carried_rows.astype(jnp.bfloat16), 'ctx', split_axis=0, co...  8.49 us
  transfers between devices with their start and end apart: 12, of which 12 were waited for; matrix products, arithmetic and copies ran while one was open for 29% of the time, Pallas kernels for 0%

commit v1 on v0

v1 whole, which is shorter than its diff:
```python
import functools
import jax
import jax.numpy as jnp
from jax import lax
from jax.experimental import pallas as pl
from jax.experimental.pallas import tpu as pltpu
from jax.sharding import PartitionSpec as P

AXES = ("ctx", "head")
F32 = jnp.float32
BF16 = jnp.bfloat16
VMEM_LIMIT = 48 * 1024 * 1024


def dot(a, b, dims):
    return lax.dot_general(a, b, (dims, ((), ())), preferred_element_type=F32)


AB = ((1,), (0,))
ABT = ((1,), (1,))
ATB = ((0,), (0,))


def decay(rate, steps):
    return jnp.exp(-rate * steps)


def positions(shape):
    return lax.broadcasted_iota(jnp.int32, shape, 0).astype(F32)


def causal_weights(rate, length):
    row = lax.broadcasted_iota(jnp.int32, (length, length), 0)
    col = lax.broadcasted_iota(jnp.int32, (length, length), 1)
    offset = (row - col).astype(F32)
    return jnp.where(offset >= 0, jnp.exp(-rate * jnp.maximum(offset, 0.0)), 0.0)


def split_heads(block_ref, scratch):
    length, heads, size = block_ref.shape
    scratch[...] = block_ref[...].astype(F32).reshape(length * heads, size)


def one_head(scratch, h, length, heads):
    return scratch[pl.ds(h, length, stride=heads), :]


def join_heads(scratch, out_ref):
    out_ref[...] = scratch[...].reshape(out_ref.shape).astype(out_ref.dtype)


def local_kernel(meta, k_ref, v_ref, rate_ref, kt_ref, vt_ref, s_ref, ks, vs):
    length, heads, size = k_ref.shape
    split_heads(k_ref, ks)
    split_heads(v_ref, vs)
    first = meta[0] * heads
    tail_steps = length - 1.0 - positions((length, size))
    for h in range(heads):
        key = one_head(ks, h, length, heads)
        value = one_head(vs, h, length, heads).astype(BF16)
        kt_ref[h] = key.astype(BF16)
        vt_ref[h] = value
        rate = rate_ref[pl.ds(first + h, 1), :]
        key_decayed = (key * decay(rate, tail_steps)).astype(BF16)
        s_ref[h] = dot(key_decayed, value, ATB).astype(BF16)


def attention_kernel(meta, q_ref, g_ref, kt_ref, vt_ref, rate_ref, qt_ref, gt_ref, a_ref, o_ref, qs, gs):
    length, heads, size = q_ref.shape
    split_heads(q_ref, qs)
    split_heads(g_ref, gs)
    first = meta[0] * heads
    for h in range(heads):
        query = one_head(qs, h, length, heads).astype(BF16)
        qt_ref[h] = query
        gt_ref[h] = one_head(gs, h, length, heads).astype(BF16)
        rate = rate_ref[pl.ds(first + h, 1), :]
        scores = dot(query, kt_ref[h], ABT)
        attention = (scores * causal_weights(rate, length)).astype(BF16)
        a_ref[h] = attention
        o_ref[h] = dot(attention, vt_ref[h], AB)


def norm_kernel(meta, qt_ref, gt_ref, o_ref, in_ref, rate_ref, gain_ref, n_ref, go_ref, sg_ref):
    heads, length, size = qt_ref.shape
    first = meta[0] * heads
    head_steps = positions((length, size)) + 1.0
    for h in range(heads):
        rate = rate_ref[pl.ds(first + h, 1), :]
        gain = gain_ref[pl.ds(first + h, 1), :]
        head_decay = decay(rate, head_steps)
        query = qt_ref[h]
        out = o_ref[h] + head_decay * dot(query, in_ref[h], AB)
        inv_rms = lax.rsqrt(jnp.mean(out * out, axis=-1, keepdims=True) + 1e-06)
        unit = out * inv_rms
        n_ref[h] = (unit * gain).astype(BF16)
        scaled = gain * gt_ref[h].astype(F32)
        grad_out = (inv_rms * (scaled - unit * jnp.mean(scaled * unit, axis=-1, keepdims=True))).astype(BF16)
        go_ref[h] = grad_out
        query_decayed = (query.astype(F32) * head_decay).astype(BF16)
        sg_ref[h] = dot(query_decayed, grad_out, ATB).astype(BF16)


def grad_kernel(meta, qt_ref, kt_ref, vt_ref, a_ref, go_ref, in_ref, n_ref, rate_ref, *rest):
    n_out, dq_out, dk_ref, dv_ref, ns, ds = rest[-6:]
    heads, length, size = qt_ref.shape
    first = meta[0] * heads
    head_steps = positions((length, size)) + 1.0
    for h in range(heads):
        rate = rate_ref[pl.ds(first + h, 1), :]
        grad_out = go_ref[h]
        grad_scores = (dot(grad_out, vt_ref[h], ABT) * causal_weights(rate, length)).astype(BF16)
        through_state = dot(grad_out, in_ref[h], ABT)
        ds[pl.ds(h, length, stride=heads), :] = (
            dot(grad_scores, kt_ref[h], AB) + decay(rate, head_steps) * through_state
        )
        ns[pl.ds(h, length, stride=heads), :] = n_ref[h].astype(F32)
        dk_ref[h] = dot(grad_scores, qt_ref[h], ATB)
        dv_ref[h] = dot(a_ref[h], grad_out, ATB)
    join_heads(ns, n_out)
    join_heads(ds, dq_out)


def later_kernel(meta, kt_ref, vt_ref, later_ref, dk_ref, dv_ref, rate_ref, *rest):
    dk_out, dv_out, ks, vs = rest[-4:]
    heads, length, size = kt_ref.shape
    first = meta[0] * heads
    tail_steps = length - 1.0 - positions((length, size))
    for h in range(heads):
        tail = decay(rate_ref[pl.ds(first + h, 1), :], tail_steps)
        later = later_ref[h]
        ks[pl.ds(h, length, stride=heads), :] = dk_ref[h] + tail * dot(vt_ref[h], later, ABT)
        vs[pl.ds(h, length, stride=heads), :] = dv_ref[h] + tail * dot(kt_ref[h], later, AB)
    join_heads(ks, dk_out)
    join_heads(vs, dv_out)


def row_weight(rate, span, steps):
    weight = jnp.exp(-rate * (span * jnp.maximum(steps, 0).astype(F32)))
    return jnp.where(steps >= 0, weight, 0.0)


def fold_kernel(group, next_group, span, meta, rate_ref, *refs):
    states, parts = refs[:group], refs[group:]
    heads = parts[0].shape[0]
    for k in range(next_group):
        start = (meta[2] ^ k) * heads
        for i in range(heads):
            rate = rate_ref[pl.ds(meta[0] + start + i, 1), :]
            total = None
            for j in range(group):
                weight = row_weight(rate, span, group - 1 - (meta[1] ^ j))
                term = weight * states[j][start + i].astype(F32)
                total = term if total is None else total + term
            parts[k][i] = total.astype(BF16)


def spread_kernel(group, next_group, top, span, meta, rate_ref, *refs):
    states, ahead, outs = refs[:group], refs[group:-group], refs[-group:]
    heads = states[0].shape[0]
    part_heads = heads if top else heads // next_group
    for k in range(1 if top else next_group):
        start = 0 if top else (meta[2] ^ k) * part_heads
        for i in range(part_heads):
            rate = rate_ref[pl.ds(meta[0] + start + i, 1), :]
            if top:
                before = None
                for j in range(1, next_group):
                    weight = row_weight(rate, span * group, meta[2] - 1 - (meta[2] ^ j))
                    term = weight * ahead[j - 1][i].astype(F32)
                    before = term if before is None else before + term
            else:
                before = ahead[k][i].astype(F32)
            own = [states[j][start + i].astype(F32) for j in range(group)]
            for j in range(group):
                place = meta[1] ^ j
                total = row_weight(rate, span, place) * before
                for q in range(group):
                    if q != j:
                        total = total + row_weight(rate, span, place - 1 - (meta[1] ^ q)) * own[q]
                outs[j][start + i] = total.astype(BF16)


def call(body, meta, inputs, outputs, scratch=(), aliases=None, flops=0, name=None):
    def spec(shape, block):
        if block == "any":
            return pl.BlockSpec(memory_space=pl.ANY)
        if block is None:
            return pl.BlockSpec(shape, lambda i, m: (0,) * len(shape))
        return pl.BlockSpec(block, lambda i, m: (0, m[0], 0))

    nbytes = sum(a.size * a.dtype.itemsize for a, _ in inputs)
    nbytes += sum(s.size * s.dtype.itemsize for s, _ in outputs)
    return pl.pallas_call(
        body,
        grid_spec=pltpu.PrefetchScalarGridSpec(
            num_scalar_prefetch=1,
            grid=(1,),
            in_specs=[spec(a.shape, b) for a, b in inputs],
            out_specs=[spec(s.shape, b) for s, b in outputs],
            scratch_shapes=list(scratch),
        ),
        out_shape=[s for s, _ in outputs],
        input_output_aliases=aliases or {},
        compiler_params=pltpu.CompilerParams(vmem_limit_bytes=VMEM_LIMIT),
        cost_estimate=pl.CostEstimate(flops=flops, bytes_accessed=nbytes, transcendentals=0),
        name=name,
    )(meta, *[a for a, _ in inputs])


def level_sizes(devices):
    sizes = [2]
    left = devices // 2
    while left > 8:
        sizes.append(4)
        left //= 4
    return sizes + [left]


def swap(array, distance, devices):
    return lax.ppermute(array, AXES, [(i, i ^ distance) for i in range(devices)])


def carry_states(kept, sent, index, devices, rates, first_head, length, forward):
    sizes = level_sizes(devices)
    state = kept.shape[1:]
    places, lows = [], []
    low = 1
    for size in sizes:
        places.append((index // low) % size)
        lows.append(low)
        low *= size

    def weigh_place(level):
        return places[level] if forward else places[level] ^ (sizes[level] - 1)

    def climb(level, parts, first):
        group, next_group = sizes[level], sizes[level + 1]
        top = level + 2 == len(sizes)
        span = float(length * lows[level])
        states = [parts[0]] + [swap(parts[k], k * lows[level], devices) for k in range(1, group)]
        heads = parts[0].shape[0]
        part_heads = heads if top else heads // next_group
        next_place = 0 if top else places[level + 1]
        meta = jnp.stack([first, weigh_place(level), next_place + 0 * first]).astype(jnp.int32)
        count = 1 if top else next_group
        folded = call(
            functools.partial(fold_kernel, group, count, span),
            meta,
            [(rates, None)] + [(s, None) for s in states],
            [(jax.ShapeDtypeStruct((part_heads,) + state, BF16), None)] * count,
            name="fold_states",
        )
        if top:
            distance = lows[level + 1]
            ahead = [swap(folded[0], k * distance, devices) for k in range(1, next_group)]
            next_meta = weigh_place(level + 1)
        else:
            ahead = climb(level + 1, folded, first + next_place * part_heads)
            next_meta = next_place
        meta = jnp.stack([first, weigh_place(level), next_meta]).astype(jnp.int32)
        outs = call(
            functools.partial(spread_kernel, group, next_group, top, span),
            meta,
            [(rates, None)] + [(s, None) for s in states] + [(a, None) for a in ahead],
            [(jax.ShapeDtypeStruct((heads,) + state, BF16), None)] * group,
            name="spread_states",
        )
        return [outs[0]] + [swap(outs[k], k * lows[level], devices) for k in range(1, group)]

    return climb(0, [kept, sent], first_head)


def local(devices, queries, key_vectors, value_vectors, output_grad, decay_rate, norm_gain):
    length, heads, size = queries.shape
    half = heads // 2
    index = lax.axis_index("ctx") * lax.axis_size("head") + lax.axis_index("head")
    core = index % 2
    rates = jnp.broadcast_to(decay_rate[:, None], (heads, size))
    block = (length, half, size)
    per_head = (half, length, size)
    states = (half, size, size)

    def shaped(shape, dtype=BF16):
        return (jax.ShapeDtypeStruct(shape, dtype), None)

    def flat():
        return pltpu.VMEM((length * half, size), F32)

    def whole():
        return (jax.ShapeDtypeStruct(queries.shape, BF16), block)

    unit = 2 * half * length * size * size
    metas = [jnp.reshape(core, (1,)).astype(jnp.int32), jnp.reshape(1 - core, (1,)).astype(jnp.int32)]

    keys, values, local_states = [None, None], [None, None], [None, None]
    for s in (1, 0):
        keys[s], values[s], local_states[s] = call(
            local_kernel,
            metas[s],
            [(key_vectors, block), (value_vectors, block), (rates, None)],
            [shaped(per_head), shaped(per_head), shaped(states)],
            [flat(), flat()],
            flops=unit,
            name="local_states",
        )
    incoming = carry_states(
        local_states[0], local_states[1], index, devices, rates, core * half, length, True
    )
    query, grad, attention, inner = [None, None], [None, None], [None, None], [None, None]
    for s in (0, 1):
        query[s], grad[s], attention[s], inner[s] = call(
            attention_kernel,
            metas[s],
            [(queries, block), (output_grad, block), (keys[s], None), (values[s], None), (rates, None)],
            [shaped(per_head), shaped(per_head), shaped((half, length, length)), shaped(per_head, F32)],
            [flat(), flat()],
            flops=2 * unit,
            name="attention",
        )
    normed, grad_out, state_grad = [None, None], [None, None], [None, None]
    for s in (0, 1):
        normed[s], grad_out[s], state_grad[s] = call(
            norm_kernel,
            metas[s],
            [
                (query[s], None),
                (grad[s], None),
                (inner[s], None),
                (incoming[s], None),
                (rates, None),
                (norm_gain, None),
            ],
            [shaped(per_head), shaped(per_head), shaped(states)],
            flops=2 * unit,
            name="norm",
        )
    later = carry_states(
        state_grad[1], state_grad[0], index, devices, rates, (1 - core) * half, length, False
    )
    normed_out, query_out, key_part, value_part = None, None, [None, None], [None, None]
    for s in (0, 1):
        inputs = [
            (query[s], None),
            (keys[s], None),
            (values[s], None),
            (attention[s], None),
            (grad_out[s], None),
            (incoming[s], None),
            (normed[s], None),
            (rates, None),
        ]
        aliases = {}
        if s:
            aliases = {1 + len(inputs): 0, 2 + len(inputs): 1}
            inputs += [(normed_out, "any"), (query_out, "any")]
        normed_out, query_out, key_part[s], value_part[s] = call(
            grad_kernel,
            metas[s],
            inputs,
            [whole(), whole(), shaped(per_head, F32), shaped(per_head, F32)],
            [flat(), flat()],
            aliases,
            flops=5 * unit,
            name="stretch_gradients",
        )
    key_out, value_out = None, None
    for s in (1, 0):
        inputs = [
            (keys[s], None),
            (values[s], None),
            (later[1 - s], None),
            (key_part[s], None),
            (value_part[s], None),
            (rates, None),
        ]
        aliases = {}
        if s == 0:
            aliases = {1 + len(inputs): 0, 2 + len(inputs): 1}
            inputs += [(key_out, "any"), (value_out, "any")]
        key_out, value_out = call(
            later_kernel,
            metas[s],
            inputs,
            [whole(), whole()],
            [flat(), flat()],
            aliases,
            flops=2 * unit,
            name="later_gradients",
        )
    return normed_out, query_out, key_out, value_out


def solution(mesh):
    devices = mesh.shape["ctx"] * mesh.shape["head"]
    spread = P(AXES, None, None)
    return jax.shard_map(
        functools.partial(local, devices),
        mesh=mesh,
        in_specs=(spread, spread, spread, spread, P(), P()),
        out_specs=(spread, spread, spread, spread),
        check_vma=False,
    )
```

time: 228 us -> 123 us (0.54)
  Pallas kernels: 0 us -> 48.3 us
  waiting for transfers between devices: 82.7 us -> 37.3 us
  other arithmetic: 30.6 us -> 0.46 us
  matrix products: 25.7 us -> 0 us
  starting transfers between devices: 49.4 us -> 24.4 us
  local copies, waits for them, and re-layouts: 35.2 us -> 10.9 us
    all_to_all x12 -> x0, waiting for transfers between devices: 82.7 us -> none  [the longest x1 12.9 us: local(): lax.all_to_all(value_vectors, 'head', split_axis=1, concat_axis=0, tiled=...]
    all_to_all x12 -> x0, starting transfers between devices: 49.4 us -> none  [the longest x2 10.1 us: carry_states(): lax.all_to_all(flat_rows, 'ctx', split_axis=1, concat_axis=0, tiled=True)]
    pallas_call x0 -> x18, Pallas kernels: none -> 48.3 us  [call(): pl.pallas_call(body, grid_spec=pltpu.PrefetchScalarGridSpec(num_scalar_pr...]
    ppermute x0 -> x22, waiting for transfers between devices: none -> 37.3 us  [swap(): lax.ppermute(array, AXES, [(i, i ^ distance) for i in range(devices)])]
    dot_general x16 -> x0, matrix products: 25.7 us -> none  [the longest x2 6.09 us: carry_states(): jnp.einsum('kqh,qhde->khde', inner_weights, states_float, precision=lax.P...]
    ppermute x0 -> x22, starting transfers between devices: none -> 24.4 us  [swap(): lax.ppermute(array, AXES, [(i, i ^ distance) for i in range(devices)])]
    add x16 -> x0, other arithmetic: 13.6 us -> none  [carry_step(): return (row_decay * state + piece.astype(jnp.float32), state)]
    all_to_all x4 -> x0, local copies, waits for them, and re-layouts: 8.27 us -> none  [the longest x1 2.37 us: local(): lax.all_to_all(results[0].reshape(flat_shape), 'head', split_axis=0, conc...]
  transfers between devices with their start and end apart: 12 -> 22, of which waited for: 12 -> 11; matrix products, arithmetic and copies ran while one was open for 29% -> 0% of each run, Pallas kernels for 0% -> 21%
where the time goes in v1:
time: 123 us; the launch traced here: 122 us
  Pallas kernels  48.3 us (39%)
  waiting for transfers between devices  37.3 us (30%)
  starting transfers between devices  24.4 us (20%)
  local copies, waits for them, and re-layouts  10.9 us (9%)
    pallas_call x18, Pallas kernels, call(): pl.pallas_call(body, grid_spec=pltpu.PrefetchScalarGridSpec(num_scalar_pr...  48.3 us
    ppermute x22, waiting for transfers between devices, swap(): lax.ppermute(array, AXES, [(i, i ^ distance) for i in range(devices)])  37.3 us
    ppermute x22, starting transfers between devices, swap(): lax.ppermute(array, AXES, [(i, i ^ distance) for i in range(devices)])  24.4 us
    unnamed x62, local copies, waits for them, and re-layouts  10.8 us
  transfers between devices with their start and end apart: 22, of which 11 were waited for; matrix products, arithmetic and copies ran while one was open for 0% of the time, Pallas kernels for 21%

profile of v1, /device:TPU:0, one launch (start us, length us, event | category | flops | bytes accessed | tf_op | source)
XLA Modules:
  0.0 122.4 jit_solution(9335440770763868423)
XLA Ops:
  8.6 2.4 %fold_states.4 = (bf16[4,128,128]{2,1,0:T(8,128)(2,1)S(1)}, bf16[4,128,128]{2,1,0:T(8,128)(2,1)}, bf16[4,128,128]{2,1,0:T(8,128)(2,1)}, bf16[4,128,128]{2,1,0:T(8,128)(2,1)}) custom-call(s32[3]{0:T(128)S(1)} %add_add_fusion.meta, f32[32,128]{1,0:T(8,128)S(1)} %broadcast_in_dim.2.rate_ref, bf16[16,128,128]{2,1,0:T(8,128)(2,1)S(1)} %get-tuple-element.62.refs_0_, ...), custom_call_target="tpu_custom_call" | custom-call | bytes 1589248 | tf_op jit(solution)/shard_map/fold_states/pallas_call | solution.py:194
  11.5 2.5 %collective-permute-start.1 = (bf16[4,128,128]{2,1,0:T(8,128)(2,1)}, bf16[4,128,128]{2,1,0:T(8,128)(2,1)S(1)}, u32[]{:S(2)}, u32[]{:S(2)}) collective-permute-start(bf16[4,128,128]{2,1,0:T(8,128)(2,1)} %get-tuple-element.65), channel_id=1, source_target_pairs={{0,2},{1,3},{2,0},{3,1},{4,6},{5,7},{6,4},{7,5},{8,10},{9,11},{10,... | collective-permute-start | bytes 393224 | tf_op jit(solution)/shard_map/ppermute | solution.py:221
  15.6 2.9 %collective-permute-done.1.refs_1_ = bf16[4,128,128]{2,1,0:T(8,128)(2,1)S(1)} collective-permute-done((bf16[4,128,128]{2,1,0:T(8,128)(2,1)}, bf16[4,128,128]{2,1,0:T(8,128)(2,1)S(1)}, u32[]{:S(2)}, u32[]{:S(2)}) %collective-permute-start.1) | collective-permute-done | bytes 131104 | tf_op jit(solution)/shard_map/ppermute | solution.py:221
  18.5 4.2 %collective-permute-done.2.refs_2_ = bf16[4,128,128]{2,1,0:T(8,128)(2,1)S(1)} collective-permute-done((bf16[4,128,128]{2,1,0:T(8,128)(2,1)}, bf16[4,128,128]{2,1,0:T(8,128)(2,1)S(1)}, u32[]{:S(2)}, u32[]{:S(2)}) %collective-permute-start.2) | collective-permute-done | bytes 131104 | tf_op jit(solution)/shard_map/ppermute | solution.py:221
  22.7 2.2 %fold_states.5 = bf16[4,128,128]{2,1,0:T(8,128)(2,1)} custom-call(s32[3]{0:T(128)S(1)} %pad_add_fusion.1.meta, f32[32,128]{1,0:T(8,128)S(1)} %broadcast_in_dim.2.rate_ref, bf16[4,128,128]{2,1,0:T(8,128)(2,1)S(1)} %get-tuple-element.64.refs_0_, bf16[4,128,128]{2,1,0:T(8,128)(2,1)S(1)} %collective-permute-done.1.refs_1_, ...), custom_call_target="tpu_custom_call" | custom-call | bytes 671744 | tf_op jit(solution)/shard_map/fold_states/pallas_call | solution.py:194
  24.9 3.6 %collective-permute-start.6 = (bf16[4,128,128]{2,1,0:T(8,128)(2,1)}, bf16[4,128,128]{2,1,0:T(8,128)(2,1)}, u32[]{:S(2)}, u32[]{:S(2)}) collective-permute-start(bf16[4,128,128]{2,1,0:T(8,128)(2,1)} %fold_states.5), channel_id=1, source_target_pairs={{0,24},{1,25},{2,26},{3,27},{4,28},{5,29},{6,30},{7,31},{8,16},{9,... | collective-permute-start | bytes 393224 | tf_op jit(solution)/shard_map/ppermute | solution.py:221
  29.4 4.1 %collective-permute-done.6.refs_6_ = bf16[4,128,128]{2,1,0:T(8,128)(2,1)} collective-permute-done((bf16[4,128,128]{2,1,0:T(8,128)(2,1)}, bf16[4,128,128]{2,1,0:T(8,128)(2,1)}, u32[]{:S(2)}, u32[]{:S(2)}) %collective-permute-start.6) | collective-permute-done | bytes 131104 | tf_op jit(solution)/shard_map/ppermute | solution.py:221
  33.5 5.9 %collective-permute-done.5.refs_5_ = bf16[4,128,128]{2,1,0:T(8,128)(2,1)} collective-permute-done((bf16[4,128,128]{2,1,0:T(8,128)(2,1)}, bf16[4,128,128]{2,1,0:T(8,128)(2,1)}, u32[]{:S(2)}, u32[]{:S(2)}) %collective-permute-start.5) | collective-permute-done | bytes 131104 | tf_op jit(solution)/shard_map/ppermute | solution.py:221
  46.3 3.0 %attention.3 = (bf16[16,128,128]{2,1,0:T(8,128)(2,1)S(1)}, bf16[16,128,128]{2,1,0:T(8,128)(2,1)S(1)}, bf16[16,128,128]{2,1,0:T(8,128)(2,1)S(1)}, f32[16,128,128]{2,1,0:T(8,128)S(1)}) custom-call(s32[1]{0:T(128)} %bitcast.2.meta, bf16[128,32,128]{2,1,0:T(8,128)(2,1)S(1)} %copy-done.4, bf16[128,32,128]{2,1,0:T(8,128)(2,1)S(1)} %copy-done.5, ...), custom_call_target="tpu_custom_call" | custom-call | flops 134217728 | bytes 5783552 | tf_op jit(solution)/shard_map/attention/pallas_call | solution.py:194
  50.5 2.9 %spread_states.5 = (bf16[16,128,128]{2,1,0:T(8,128)(2,1)S(1)}, bf16[16,128,128]{2,1,0:T(8,128)(2,1)}) custom-call(s32[3]{0:T(128)S(1)} %copy-done.27, f32[32,128]{1,0:T(8,128)S(1)} %broadcast_in_dim.2.rate_ref, bf16[16,128,128]{2,1,0:T(8,128)(2,1)S(1)} %copy-done.8, bf16[16,128,128]{2,1,0:T(8,128)(2,1)} %collective-permute-done.refs_1_, ...), custom_call_target="tpu_custom_call" | custom-call | bytes 2637824 | tf_op jit(solution)/shard_map/spread_states/pallas_call | solution.py:194
  58.8 3.0 %attention.2 = (bf16[16,128,128]{2,1,0:T(8,128)(2,1)S(1)}, bf16[16,128,128]{2,1,0:T(8,128)(2,1)S(1)}, bf16[16,128,128]{2,1,0:T(8,128)(2,1)S(1)}, f32[16,128,128]{2,1,0:T(8,128)S(1)}) custom-call(s32[1]{0:T(128)} %bitcast.meta, bf16[128,32,128]{2,1,0:T(8,128)(2,1)S(1)} %copy-done.4, bf16[128,32,128]{2,1,0:T(8,128)(2,1)S(1)} %copy-done.6, ...), custom_call_target="tpu_custom_call" | custom-call | flops 134217728 | bytes 5783552 | tf_op jit(solution)/shard_map/attention/pallas_call | solution.py:194
  62.8 2.5 %norm.2 = (bf16[16,128,128]{2,1,0:T(8,128)(2,1)S(1)}, bf16[16,128,128]{2,1,0:T(8,128)(2,1)S(1)}, bf16[16,128,128]{2,1,0:T(8,128)(2,1)S(1)}) custom-call(s32[1]{0:T(128)} %bitcast.meta, bf16[16,128,128]{2,1,0:T(8,128)(2,1)S(1)} %get-tuple-element.58.qt_ref, bf16[16,128,128]{2,1,0:T(8,128)(2,1)S(1)} %get-tuple-element.60.gt_ref, ...), custom_call_target="tpu_custom_call" | custom-call | flops 134217728 | bytes 4227072 | tf_op jit(solution)/shard_map/norm/pallas_call | solution.py:194
  65.3 2.4 %fold_states.6 = (bf16[4,128,128]{2,1,0:T(8,128)(2,1)S(1)}, bf16[4,128,128]{2,1,0:T(8,128)(2,1)}, bf16[4,128,128]{2,1,0:T(8,128)(2,1)}, bf16[4,128,128]{2,1,0:T(8,128)(2,1)}) custom-call(s32[3]{0:T(128)S(1)} %add_add_fusion.1.meta, f32[32,128]{1,0:T(8,128)S(1)} %broadcast_in_dim.2.rate_ref, bf16[16,128,128]{2,1,0:T(8,128)(2,1)S(1)} %get-tuple-element.88.refs_0_, ...), custom_call_target="tpu_custom_call" | custom-call | bytes 1589248 | tf_op jit(solution)/shard_map/fold_states/pallas_call | solution.py:194
  71.3 2.7 %collective-permute-done.12.refs_1_ = bf16[4,128,128]{2,1,0:T(8,128)(2,1)S(1)} collective-permute-done((bf16[4,128,128]{2,1,0:T(8,128)(2,1)}, bf16[4,128,128]{2,1,0:T(8,128)(2,1)S(1)}, u32[]{:S(2)}, u32[]{:S(2)}) %collective-permute-start.12) | collective-permute-done | bytes 131104 | tf_op jit(solution)/shard_map/ppermute | solution.py:221
  74.0 3.1 %collective-permute-done.13.refs_2_ = bf16[4,128,128]{2,1,0:T(8,128)(2,1)S(1)} collective-permute-done((bf16[4,128,128]{2,1,0:T(8,128)(2,1)}, bf16[4,128,128]{2,1,0:T(8,128)(2,1)S(1)}, u32[]{:S(2)}, u32[]{:S(2)}) %collective-permute-start.13) | collective-permute-done | bytes 131104 | tf_op jit(solution)/shard_map/ppermute | solution.py:221
  77.1 2.2 %fold_states.7 = bf16[4,128,128]{2,1,0:T(8,128)(2,1)} custom-call(s32[3]{0:T(128)S(1)} %pad_add_fusion.meta, f32[32,128]{1,0:T(8,128)S(1)} %broadcast_in_dim.2.rate_ref, bf16[4,128,128]{2,1,0:T(8,128)(2,1)S(1)} %get-tuple-element.90.refs_0_, bf16[4,128,128]{2,1,0:T(8,128)(2,1)S(1)} %collective-permute-done.12.refs_1_, ...), custom_call_target="tpu_custom_call" | custom-call | bytes 671744 | tf_op jit(solution)/shard_map/fold_states/pallas_call | solution.py:194
  79.3 2.5 %collective-permute-start.17 = (bf16[4,128,128]{2,1,0:T(8,128)(2,1)}, bf16[4,128,128]{2,1,0:T(8,128)(2,1)}, u32[]{:S(2)}, u32[]{:S(2)}) collective-permute-start(bf16[4,128,128]{2,1,0:T(8,128)(2,1)} %fold_states.7), channel_id=1, source_target_pairs={{0,24},{1,25},{2,26},{3,27},{4,28},{5,29},{6,30},{7,31},{8,16},{9,... | collective-permute-start | bytes 393224 | tf_op jit(solution)/shard_map/ppermute | solution.py:221
  83.8 4.1 %collective-permute-done.17.refs_6_ = bf16[4,128,128]{2,1,0:T(8,128)(2,1)} collective-permute-done((bf16[4,128,128]{2,1,0:T(8,128)(2,1)}, bf16[4,128,128]{2,1,0:T(8,128)(2,1)}, u32[]{:S(2)}, u32[]{:S(2)}) %collective-permute-start.17) | collective-permute-done | bytes 131104 | tf_op jit(solution)/shard_map/ppermute | solution.py:221
  87.9 4.4 %collective-permute-done.16.refs_5_ = bf16[4,128,128]{2,1,0:T(8,128)(2,1)} collective-permute-done((bf16[4,128,128]{2,1,0:T(8,128)(2,1)}, bf16[4,128,128]{2,1,0:T(8,128)(2,1)}, u32[]{:S(2)}, u32[]{:S(2)}) %collective-permute-start.16) | collective-permute-done | bytes 131104 | tf_op jit(solution)/shard_map/ppermute | solution.py:221
  97.9 2.8 %collective-permute-done.18.refs_3_ = bf16[4,128,128]{2,1,0:T(8,128)(2,1)S(1)} collective-permute-done((bf16[4,128,128]{2,1,0:T(8,128)(2,1)S(1)}, bf16[4,128,128]{2,1,0:T(8,128)(2,1)S(1)}, u32[]{:S(2)}, u32[]{:S(2)}) %collective-permute-start.18) | collective-permute-done | bytes 131104 | tf_op jit(solution)/shard_map/ppermute | solution.py:221
  106.2 5.0 %stretch_gradients.2 = (bf16[128,32,128]{2,1,0:T(8,128)(2,1)}, bf16[128,32,128]{2,1,0:T(8,128)(2,1)}, f32[16,128,128]{2,1,0:T(8,128)S(1)}, f32[16,128,128]{2,1,0:T(8,128)S(1)}) custom-call(s32[1]{0:T(128)} %bitcast.2.meta, bf16[16,128,128]{2,1,0:T(8,128)(2,1)S(1)} %copy-done.12, bf16[16,128,128]{2,1,0:T(8,128)(2,1)S(1)} %get-tuple-element.75.kt_ref, ...), custom_call_target="tpu_custom_call" | custom-call | flops 335544320 | bytes 7880704 | tf_op jit(solution)/shard_map/stretch_gradients/pallas_call | solution.py:194
  111.2 6.4 %stretch_gradients.3 = (bf16[128,32,128]{2,1,0:T(8,128)(2,1)}, bf16[128,32,128]{2,1,0:T(8,128)(2,1)}, f32[16,128,128]{2,1,0:T(8,128)S(1)}, f32[16,128,128]{2,1,0:T(8,128)S(1)}) custom-call(s32[1]{0:T(128)} %bitcast.meta, bf16[16,128,128]{2,1,0:T(8,128)(2,1)S(1)} %copy-done.10, ...), custom_call_target="tpu_custom_call", output_to_operand_aliasing={{0}: (9, {}), {1}: (10, {})} | custom-call | flops 335544320 | bytes 9977856 | tf_op jit(solution)/shard_map/stretch_gradients/pallas_call | solution.py:194
  117.6 2.4 %later_gradients.2 = (bf16[128,32,128]{2,1,0:T(8,128)(2,1)}, bf16[128,32,128]{2,1,0:T(8,128)(2,1)}) custom-call(s32[1]{0:T(128)} %bitcast.meta, bf16[16,128,128]{2,1,0:T(8,128)(2,1)S(1)} %get-tuple-element.56.kt_ref, bf16[16,128,128]{2,1,0:T(8,128)(2,1)S(1)} %get-tuple-element.57.vt_ref, bf16[16,128,128]{2,1,0:T(8,128)(2,1)S(1)} %get-tuple-element.101.later_ref, ...), custom_call_target="tpu_custom_call" | custom-call | flops 134217728 | bytes 5783552 | tf_op jit(solution)/shard_map/later_gradients/pallas_call | solution.py:194
  120.0 2.4 %later_gradients.3 = (bf16[128,32,128]{2,1,0:T(8,128)(2,1)}, bf16[128,32,128]{2,1,0:T(8,128)(2,1)}) custom-call(s32[1]{0:T(128)} %bitcast.2.meta, bf16[16,128,128]{2,1,0:T(8,128)(2,1)S(1)} %get-tuple-element.75.kt_ref, bf16[16,128,128]{2,1,0:T(8,128)(2,1)S(1)} %get-tuple-element.76.vt_ref, ...), custom_call_target="tpu_custom_call", output_to_operand_aliasing={{0}: (7, {}), {1}: (8, {})} | custom-call | flops 134217728 | bytes 7880704 | tf_op jit(solution)/shard_map/later_gradients/pallas_call | solution.py:194
  (107 shorter events, 41.6 us)
Async XLA Ops:
  5.7 2.9 %collective-permute-start = (bf16[16,128,128]{2,1,0:T(8,128)(2,1)}, bf16[16,128,128]{2,1,0:T(8,128)(2,1)}, u32[]{:S(2)}, u32[]{:S(2)}) collective-permute-start(bf16[16,128,128]{2,1,0:T(8,128)(2,1)} %get-tuple-element.63), channel_id=1, source_target_pairs={{0,1},{1,0},{2,3},{3,2},{4,5},{5,4},{6,7},{7,6},{8,9},{9,8},{10,11... | collective-permute-start | bytes 1572872 | tf_op jit(solution)/shard_map/ppermute | solution.py:221
  11.5 33.5 %copy-start.4 = (bf16[128,32,128]{2,1,0:T(8,128)(2,1)S(1)}, bf16[128,32,128]{2,1,0:T(8,128)(2,1)}, u32[]{:S(2)}) copy-start(bf16[128,32,128]{2,1,0:T(8,128)(2,1)} %q_ref.3) | copy-start | bytes 3145732
  11.5 7.0 %collective-permute-start.1 = (bf16[4,128,128]{2,1,0:T(8,128)(2,1)}, bf16[4,128,128]{2,1,0:T(8,128)(2,1)S(1)}, u32[]{:S(2)}, u32[]{:S(2)}) collective-permute-start(bf16[4,128,128]{2,1,0:T(8,128)(2,1)} %get-tuple-element.65), channel_id=1, source_target_pairs={{0,2},{1,3},{2,0},{3,1},{4,6},{5,7},{6,4},{7,5},{8,10},{9,11},{10,... | collective-permute-start | bytes 393224 | tf_op jit(solution)/shard_map/ppermute | solution.py:221
  14.0 8.7 %collective-permute-start.2 = (bf16[4,128,128]{2,1,0:T(8,128)(2,1)}, bf16[4,128,128]{2,1,0:T(8,128)(2,1)S(1)}, u32[]{:S(2)}, u32[]{:S(2)}) collective-permute-start(bf16[4,128,128]{2,1,0:T(8,128)(2,1)} %get-tuple-element.66), channel_id=1, source_target_pairs={{0,4},{1,5},{2,6},{3,7},{4,0},{5,1},{6,2},{7,3},{8,12},{9,13},{10,... | collective-permute-start | bytes 393224 | tf_op jit(solution)/shard_map/ppermute | solution.py:221
  15.5 7.1 %collective-permute-start.3 = (bf16[4,128,128]{2,1,0:T(8,128)(2,1)}, bf16[4,128,128]{2,1,0:T(8,128)(2,1)}, u32[]{:S(2)}, u32[]{:S(2)}) collective-permute-start(bf16[4,128,128]{2,1,0:T(8,128)(2,1)} %get-tuple-element.67), channel_id=1, source_target_pairs={{0,6},{1,7},{2,4},{3,5},{4,2},{5,3},{6,0},{7,1},{8,14},{9,15},{10,... | collective-permute-start | bytes 393224 | tf_op jit(solution)/shard_map/ppermute | solution.py:221
  24.9 8.5 %collective-permute-start.6 = (bf16[4,128,128]{2,1,0:T(8,128)(2,1)}, bf16[4,128,128]{2,1,0:T(8,128)(2,1)}, u32[]{:S(2)}, u32[]{:S(2)}) collective-permute-start(bf16[4,128,128]{2,1,0:T(8,128)(2,1)} %fold_states.5), channel_id=1, source_target_pairs={{0,24},{1,25},{2,26},{3,27},{4,28},{5,29},{6,30},{7,31},{8,16},{9,... | collective-permute-start | bytes 393224 | tf_op jit(solution)/shard_map/ppermute | solution.py:221
  28.5 10.9 %collective-permute-start.5 = (bf16[4,128,128]{2,1,0:T(8,128)(2,1)}, bf16[4,128,128]{2,1,0:T(8,128)(2,1)}, u32[]{:S(2)}, u32[]{:S(2)}) collective-permute-start(bf16[4,128,128]{2,1,0:T(8,128)(2,1)} %fold_states.5), channel_id=1, source_target_pairs={{0,16},{1,17},{2,18},{3,19},{4,20},{5,21},{6,22},{7,23},{8,24},{9,... | collective-permute-start | bytes 393224 | tf_op jit(solution)/shard_map/ppermute | solution.py:221
  28.5 10.9 %collective-permute-start.4 = (bf16[4,128,128]{2,1,0:T(8,128)(2,1)}, bf16[4,128,128]{2,1,0:T(8,128)(2,1)}, u32[]{:S(2)}, u32[]{:S(2)}) collective-permute-start(bf16[4,128,128]{2,1,0:T(8,128)(2,1)} %fold_states.5), channel_id=1, source_target_pairs={{0,8},{1,9},{2,10},{3,11},{4,12},{5,13},{6,14},{7,15},{8,0},{9,1},... | collective-permute-start | bytes 393224 | tf_op jit(solution)/shard_map/ppermute | solution.py:221
  41.5 7.9 %collective-permute-start.7 = (bf16[4,128,128]{2,1,0:T(8,128)(2,1)S(1)}, bf16[4,128,128]{2,1,0:T(8,128)(2,1)S(1)}, u32[]{:S(2)}, u32[]{:S(2)}) collective-permute-start(bf16[4,128,128]{2,1,0:T(8,128)(2,1)S(1)} %get-tuple-element.69), channel_id=1, source_target_pairs={{0,2},{1,3},{2,0},{3,1},{4,6},{5,7},{6,4},{7,5},{8,10},{9,11},{10,... | collective-permute-start | bytes 393224 | tf_op jit(solution)/shard_map/ppermute | solution.py:221
  43.3 7.2 %collective-permute-start.8 = (bf16[4,128,128]{2,1,0:T(8,128)(2,1)S(1)}, bf16[4,128,128]{2,1,0:T(8,128)(2,1)S(1)}, u32[]{:S(2)}, u32[]{:S(2)}) collective-permute-start(bf16[4,128,128]{2,1,0:T(8,128)(2,1)S(1)} %get-tuple-element.70), channel_id=1, source_target_pairs={{0,4},{1,5},{2,6},{3,7},{4,0},{5,1},{6,2},{7,3},{8,12},{9,13},{10,... | collective-permute-start | bytes 393224 | tf_op jit(solution)/shard_map/ppermute | solution.py:221
  43.9 6.6 %collective-permute-start.9 = (bf16[4,128,128]{2,1,0:T(8,128)(2,1)S(1)}, bf16[4,128,128]{2,1,0:T(8,128)(2,1)S(1)}, u32[]{:S(2)}, u32[]{:S(2)}) collective-permute-start(bf16[4,128,128]{2,1,0:T(8,128)(2,1)S(1)} %get-tuple-element.71), channel_id=1, source_target_pairs={{0,6},{1,7},{2,4},{3,5},{4,2},{5,3},{6,0},{7,1},{8,14},{9,15},{10,... | collective-permute-start | bytes 393224 | tf_op jit(solution)/shard_map/ppermute | solution.py:221
  53.4 9.4 %collective-permute-start.10 = (bf16[16,128,128]{2,1,0:T(8,128)(2,1)}, bf16[16,128,128]{2,1,0:T(8,128)(2,1)}, u32[]{:S(2)}, u32[]{:S(2)}) collective-permute-start(bf16[16,128,128]{2,1,0:T(8,128)(2,1)} %get-tuple-element.72), channel_id=1, source_target_pairs={{0,1},{1,0},{2,3},{3,2},{4,5},{5,4},{6,7},{7,6},{8,9},{9,8},{10,11... | collective-permute-start | bytes 1572872 | tf_op jit(solution)/shard_map/ppermute | solution.py:221
  57.1 8.1 %collective-permute-start.11 = (bf16[16,128,128]{2,1,0:T(8,128)(2,1)}, bf16[16,128,128]{2,1,0:T(8,128)(2,1)}, u32[]{:S(2)}, u32[]{:S(2)}) collective-permute-start(bf16[16,128,128]{2,1,0:T(8,128)(2,1)} %get-tuple-element.89), channel_id=1, source_target_pairs={{0,1},{1,0},{2,3},{3,2},{4,5},{5,4},{6,7},{7,6},{8,9},{9,8},{10,11... | collective-permute-start | bytes 1572872 | tf_op jit(solution)/shard_map/ppermute | solution.py:221
  67.7 6.3 %collective-permute-start.12 = (bf16[4,128,128]{2,1,0:T(8,128)(2,1)}, bf16[4,128,128]{2,1,0:T(8,128)(2,1)S(1)}, u32[]{:S(2)}, u32[]{:S(2)}) collective-permute-start(bf16[4,128,128]{2,1,0:T(8,128)(2,1)} %get-tuple-element.91), channel_id=1, source_target_pairs={{0,2},{1,3},{2,0},{3,1},{4,6},{5,7},{6,4},{7,5},{8,10},{9,11},{10,... | collective-permute-start | bytes 393224 | tf_op jit(solution)/shard_map/ppermute | solution.py:221
  68.9 8.2 %collective-permute-start.13 = (bf16[4,128,128]{2,1,0:T(8,128)(2,1)}, bf16[4,128,128]{2,1,0:T(8,128)(2,1)S(1)}, u32[]{:S(2)}, u32[]{:S(2)}) collective-permute-start(bf16[4,128,128]{2,1,0:T(8,128)(2,1)} %get-tuple-element.92), channel_id=1, source_target_pairs={{0,4},{1,5},{2,6},{3,7},{4,0},{5,1},{6,2},{7,3},{8,12},{9,13},{10,... | collective-permute-start | bytes 393224 | tf_op jit(solution)/shard_map/ppermute | solution.py:221
  69.5 7.5 %collective-permute-start.14 = (bf16[4,128,128]{2,1,0:T(8,128)(2,1)}, bf16[4,128,128]{2,1,0:T(8,128)(2,1)}, u32[]{:S(2)}, u32[]{:S(2)}) collective-permute-start(bf16[4,128,128]{2,1,0:T(8,128)(2,1)} %get-tuple-element.93), channel_id=1, source_target_pairs={{0,6},{1,7},{2,4},{3,5},{4,2},{5,3},{6,0},{7,1},{8,14},{9,15},{10,... | collective-permute-start | bytes 393224 | tf_op jit(solution)/shard_map/ppermute | solution.py:221
  79.3 8.6 %collective-permute-start.17 = (bf16[4,128,128]{2,1,0:T(8,128)(2,1)}, bf16[4,128,128]{2,1,0:T(8,128)(2,1)}, u32[]{:S(2)}, u32[]{:S(2)}) collective-permute-start(bf16[4,128,128]{2,1,0:T(8,128)(2,1)} %fold_states.7), channel_id=1, source_target_pairs={{0,24},{1,25},{2,26},{3,27},{4,28},{5,29},{6,30},{7,31},{8,16},{9,... | collective-permute-start | bytes 393224 | tf_op jit(solution)/shard_map/ppermute | solution.py:221
  81.8 10.5 %collective-permute-start.16 = (bf16[4,128,128]{2,1,0:T(8,128)(2,1)}, bf16[4,128,128]{2,1,0:T(8,128)(2,1)}, u32[]{:S(2)}, u32[]{:S(2)}) collective-permute-start(bf16[4,128,128]{2,1,0:T(8,128)(2,1)} %fold_states.7), channel_id=1, source_target_pairs={{0,16},{1,17},{2,18},{3,19},{4,20},{5,21},{6,22},{7,23},{8,24},{9,... | collective-permute-start | bytes 393224 | tf_op jit(solution)/shard_map/ppermute | solution.py:221
  81.8 10.5 %collective-permute-start.15 = (bf16[4,128,128]{2,1,0:T(8,128)(2,1)}, bf16[4,128,128]{2,1,0:T(8,128)(2,1)}, u32[]{:S(2)}, u32[]{:S(2)}) collective-permute-start(bf16[4,128,128]{2,1,0:T(8,128)(2,1)} %fold_states.7), channel_id=1, source_target_pairs={{0,8},{1,9},{2,10},{3,11},{4,12},{5,13},{6,14},{7,15},{8,0},{9,1},... | collective-permute-start | bytes 393224 | tf_op jit(solution)/shard_map/ppermute | solution.py:221
  92.3 12.8 %copy-start.22 = (bf16[16,128,128]{2,1,0:T(8,128)(2,1)S(1)}, bf16[16,128,128]{2,1,0:T(8,128)(2,1)}, u32[]{:S(2)}) copy-start(bf16[16,128,128]{2,1,0:T(8,128)(2,1)} %copy-done.21) | copy-start | bytes 1572868
  94.4 6.4 %collective-permute-start.18 = (bf16[4,128,128]{2,1,0:T(8,128)(2,1)S(1)}, bf16[4,128,128]{2,1,0:T(8,128)(2,1)S(1)}, u32[]{:S(2)}, u32[]{:S(2)}) collective-permute-start(bf16[4,128,128]{2,1,0:T(8,128)(2,1)S(1)} %get-tuple-element.95), channel_id=1, source_target_pairs={{0,2},{1,3},{2,0},{3,1},{4,6},{5,7},{6,4},{7,5},{8,10},{9,11},{10,... | collective-permute-start | bytes 393224 | tf_op jit(solution)/shard_map/ppermute | solution.py:221
  94.9 7.8 %collective-permute-start.19 = (bf16[4,128,128]{2,1,0:T(8,128)(2,1)S(1)}, bf16[4,128,128]{2,1,0:T(8,128)(2,1)S(1)}, u32[]{:S(2)}, u32[]{:S(2)}) collective-permute-start(bf16[4,128,128]{2,1,0:T(8,128)(2,1)S(1)} %get-tuple-element.96), channel_id=1, source_target_pairs={{0,4},{1,5},{2,6},{3,7},{4,0},{5,1},{6,2},{7,3},{8,12},{9,13},{10,... | collective-permute-start | bytes 393224 | tf_op jit(solution)/shard_map/ppermute | solution.py:221
  96.4 6.3 %collective-permute-start.20 = (bf16[4,128,128]{2,1,0:T(8,128)(2,1)S(1)}, bf16[4,128,128]{2,1,0:T(8,128)(2,1)S(1)}, u32[]{:S(2)}, u32[]{:S(2)}) collective-permute-start(bf16[4,128,128]{2,1,0:T(8,128)(2,1)S(1)} %get-tuple-element.97), channel_id=1, source_target_pairs={{0,6},{1,7},{2,4},{3,5},{4,2},{5,3},{6,0},{7,1},{8,14},{9,15},{10,... | collective-permute-start | bytes 393224 | tf_op jit(solution)/shard_map/ppermute | solution.py:221
  105.0 15.0 %collective-permute-start.21 = (bf16[16,128,128]{2,1,0:T(8,128)(2,1)S(1)}, bf16[16,128,128]{2,1,0:T(8,128)(2,1)S(1)}, u32[]{:S(2)}, u32[]{:S(2)}) collective-permute-start(bf16[16,128,128]{2,1,0:T(8,128)(2,1)S(1)} %get-tuple-element.98), channel_id=1, source_target_pairs={{0,1},{1,0},{2,3},{3,2},{4,5},{5,4},{6,7},{7,6},{8,9},{9,8},{10,11... | collective-permute-start | bytes 1572872 | tf_op jit(solution)/shard_map/ppermute | solution.py:221
  (29 other events, 69.7 us)

commit v2 on v1

v2 whole, which is shorter than its diff:
```python
import functools
import jax
import jax.numpy as jnp
from jax import lax
from jax.experimental import pallas as pl
from jax.experimental.pallas import tpu as pltpu
from jax.sharding import PartitionSpec as P

AXES = ("ctx", "head")
F32 = jnp.float32
BF16 = jnp.bfloat16
VMEM_LIMIT = 16 * 1024 * 1024
BATCH = 4
CHUNKS = 4


def dot(a, b, dims):
    return lax.dot_general(a, b, (dims, ((), ())), preferred_element_type=F32)


AB = ((1,), (0,))
ABT = ((1,), (1,))
ATB = ((0,), (0,))


def decay(rate, steps):
    return jnp.exp(-rate * steps)


def positions(shape):
    return lax.broadcasted_iota(jnp.int32, shape, 0).astype(F32)


def causal_weights(rate, length):
    row = lax.broadcasted_iota(jnp.int32, (length, length), 0)
    col = lax.broadcasted_iota(jnp.int32, (length, length), 1)
    offset = (row - col).astype(F32)
    return jnp.where(offset >= 0, jnp.exp(-rate * jnp.maximum(offset, 0.0)), 0.0)


def my_index():
    return lax.axis_index("ctx") * lax.axis_size("head") + lax.axis_index("head")


def head_half(own):
    core = my_index() % 2
    return core if own else 1 - core


def split_heads(block_ref, scratch, half, heads):
    length, _, size = block_ref.shape
    start = pl.multiple_of(half * heads, heads)
    scratch[...] = block_ref[:, pl.ds(start, heads), :].astype(F32).reshape(length * heads, size)


def one_head(scratch, h, length, heads):
    return scratch[pl.ds(h, length, stride=heads), :]


def start_output(scratch, stage, out_ref, sems, half):
    length, heads, size = stage.shape
    chunks = sems.shape[0]
    rows = length // chunks
    start = pl.multiple_of(half * heads, heads)
    copies = []
    for c in range(chunks):
        piece = pl.ds(c * rows, rows)
        stage[piece] = scratch[pl.ds(c * rows * heads, rows * heads), :].reshape(rows, heads, size).astype(BF16)
        copy = pltpu.make_async_copy(stage.at[piece], out_ref.at[piece, pl.ds(start, heads), :], sems.at[c])
        copy.start()
        copies.append(copy)
    return copies


def batches(heads, size=BATCH):
    size = min(size, heads)
    return [range(start, start + size) for start in range(0, heads, size)]


def local_kernel(own, k_ref, v_ref, rate_ref, kt_ref, vt_ref, s_ref, kb, vb, ks, vs, sems):
    length, heads, size = kb.shape
    half = head_half(own)
    first = half * heads
    start = pl.multiple_of(first, heads)
    chunks = sems.shape[1]
    rows = length // chunks
    copies = []
    for c in range(chunks):
        piece = pl.ds(c * rows, rows)
        for n, (ref, buffer) in enumerate(((k_ref, kb), (v_ref, vb))):
            copy = pltpu.make_async_copy(ref.at[piece, pl.ds(start, heads), :], buffer.at[piece], sems.at[n, c])
            copy.start()
            copies.append(copy)
    for c in range(chunks):
        piece = pl.ds(c * rows, rows)
        flat = pl.ds(c * rows * heads, rows * heads)
        copies[2 * c].wait()
        ks[flat, :] = kb[piece].astype(F32).reshape(rows * heads, size)
        copies[2 * c + 1].wait()
        vs[flat, :] = vb[piece].astype(F32).reshape(rows * heads, size)
    tail_steps = length - 1.0 - positions((length, size))
    for batch in batches(heads):
        key = [one_head(ks, h, length, heads) for h in batch]
        value = [one_head(vs, h, length, heads).astype(BF16) for h in batch]
        tail = [decay(rate_ref[pl.ds(first + h, 1), :], tail_steps) for h in batch]
        decayed = [(k * t).astype(BF16) for k, t in zip(key, tail)]
        state = [dot(k, v, ATB) for k, v in zip(decayed, value)]
        for i, h in enumerate(batch):
            kt_ref[h] = key[i].astype(BF16)
            vt_ref[h] = value[i]
            s_ref[h] = state[i].astype(BF16)


def attention_kernel(own, q_ref, g_ref, kt_ref, vt_ref, rate_ref, qt_ref, gt_ref, a_ref, o_ref, qs, gs):
    heads, length, size = kt_ref.shape
    half = head_half(own)
    first = half * heads
    split_heads(q_ref, qs, half, heads)
    split_heads(g_ref, gs, half, heads)
    for batch in batches(heads):
        query = [one_head(qs, h, length, heads).astype(BF16) for h in batch]
        scores = [dot(q, kt_ref[h], ABT) for q, h in zip(query, batch)]
        weights = [causal_weights(rate_ref[pl.ds(first + h, 1), :], length) for h in batch]
        attention = [(s * w).astype(BF16) for s, w in zip(scores, weights)]
        inner = [dot(a, vt_ref[h], AB) for a, h in zip(attention, batch)]
        for i, h in enumerate(batch):
            qt_ref[h] = query[i]
            gt_ref[h] = one_head(gs, h, length, heads).astype(BF16)
            a_ref[h] = attention[i]
            o_ref[h] = inner[i]


def norm_kernel(own, qt_ref, gt_ref, o_ref, in_ref, rate_ref, gain_ref, n_ref, go_ref, sg_ref):
    heads, length, size = qt_ref.shape
    first = head_half(own) * heads
    head_steps = positions((length, size)) + 1.0
    for batch in batches(heads):
        through = [dot(qt_ref[h], in_ref[h], AB) for h in batch]
        head_decay = [decay(rate_ref[pl.ds(first + h, 1), :], head_steps) for h in batch]
        out = [o_ref[h] + d * t for h, d, t in zip(batch, head_decay, through)]
        inv_rms = [lax.rsqrt(jnp.mean(o * o, axis=-1, keepdims=True) + 1e-06) for o in out]
        unit = [o * r for o, r in zip(out, inv_rms)]
        gain = [gain_ref[pl.ds(first + h, 1), :] for h in batch]
        scaled = [g * gt_ref[h].astype(F32) for g, h in zip(gain, batch)]
        along = [jnp.mean(s * u, axis=-1, keepdims=True) for s, u in zip(scaled, unit)]
        grad_out = [
            (r * (s - u * m)).astype(BF16) for r, s, u, m in zip(inv_rms, scaled, unit, along)
        ]
        decayed = [(qt_ref[h].astype(F32) * d).astype(BF16) for h, d in zip(batch, head_decay)]
        state = [dot(q, g, ATB) for q, g in zip(decayed, grad_out)]
        for i, h in enumerate(batch):
            n_ref[h] = (unit[i] * gain[i]).astype(BF16)
            go_ref[h] = grad_out[i]
            sg_ref[h] = state[i].astype(BF16)


def grad_kernel(own, qt_ref, kt_ref, vt_ref, a_ref, go_ref, in_ref, n_ref, rate_ref, *rest):
    n_out, dq_out, dk_ref, dv_ref, ns, ds, nb, db, sems = rest[-9:]
    heads, length, size = qt_ref.shape
    half = head_half(own)
    first = half * heads
    head_steps = positions((length, size)) + 1.0
    for h in range(heads):
        ns[pl.ds(h, length, stride=heads), :] = n_ref[h].astype(F32)
    copies = start_output(ns, nb, n_out, sems.at[0], half)
    for batch in batches(heads):
        inner = [dot(go_ref[h], vt_ref[h], ABT) for h in batch]
        through = [dot(go_ref[h], in_ref[h], ABT) for h in batch]
        value = [dot(a_ref[h], go_ref[h], ATB) for h in batch]
        rate = [rate_ref[pl.ds(first + h, 1), :] for h in batch]
        scores = [(s * causal_weights(r, length)).astype(BF16) for s, r in zip(inner, rate)]
        query = [dot(s, kt_ref[h], AB) for s, h in zip(scores, batch)]
        key = [dot(s, qt_ref[h], ATB) for s, h in zip(scores, batch)]
        for i, h in enumerate(batch):
            dv_ref[h] = value[i]
            dk_ref[h] = key[i]
            ds[pl.ds(h, length, stride=heads), :] = query[i] + decay(rate[i], head_steps) * through[i]
    copies += start_output(ds, db, dq_out, sems.at[1], half)
    for copy in copies:
        copy.wait()


def later_kernel(own, kt_ref, vt_ref, later_ref, dk_ref, dv_ref, rate_ref, *rest):
    dk_out, dv_out, ks, vs, kb, vb, sems = rest[-7:]
    heads, length, size = kt_ref.shape
    half = head_half(own)
    first = half * heads
    tail_steps = length - 1.0 - positions((length, size))
    for batch in batches(heads):
        key = [dot(vt_ref[h], later_ref[h], ABT) for h in batch]
        value = [dot(kt_ref[h], later_ref[h], AB) for h in batch]
        for i, h in enumerate(batch):
            tail = decay(rate_ref[pl.ds(first + h, 1), :], tail_steps)
            ks[pl.ds(h, length, stride=heads), :] = dk_ref[h] + tail * key[i]
            vs[pl.ds(h, length, stride=heads), :] = dv_ref[h] + tail * value[i]
    copies = start_output(ks, kb, dk_out, sems.at[0], half)
    copies += start_output(vs, vb, dv_out, sems.at[1], half)
    for copy in copies:
        copy.wait()


def row_weight(rate, span, steps):
    weight = jnp.exp(-rate * (span * jnp.maximum(steps, 0).astype(F32)))
    return jnp.where(steps >= 0, weight, 0.0)


def place_at(sizes, level, forward=True):
    low = 1
    for size in sizes[:level]:
        low *= size
    place = (my_index() // low) % sizes[level]
    return place if forward else place ^ (sizes[level] - 1)


def first_head(sizes, level, heads, forward):
    first, count = 0, heads
    for above in range(level + 1):
        count //= sizes[above]
        place = place_at(sizes, above)
        if above == 0 and not forward:
            place = 1 - place
        first = first + place * count
    return first


def fold_kernel(sizes, level, span, forward, rate_ref, *refs):
    group = sizes[level]
    top = level + 2 == len(sizes)
    states = refs[:group]
    parts = refs[group : group + 1] if top else refs[-sizes[level + 1] :]
    if top:
        parts = refs[-1:]
    heads = parts[0].shape[0]
    first = first_head(sizes, level, rate_ref.shape[0], forward)
    place = place_at(sizes, level, forward)
    weigh = [group - 1 - (place ^ j) for j in range(group)]
    for k in range(len(parts)):
        start = 0 if top else (place_at(sizes, level + 1) ^ k) * heads
        for i in range(heads):
            rate = rate_ref[pl.ds(first + start + i, 1), :]
            total = None
            for j in range(group):
                term = row_weight(rate, span, weigh[j]) * states[j][start + i].astype(F32)
                total = term if total is None else total + term
            parts[k][i] = total.astype(BF16)


def spread_kernel(sizes, level, span, forward, rate_ref, *refs):
    group, next_group = sizes[level], sizes[level + 1]
    top = level + 2 == len(sizes)
    ahead_count = next_group - 1 if top else next_group
    states, ahead, outs = refs[:group], refs[group : group + ahead_count], refs[-group:]
    heads = states[0].shape[0]
    part_heads = heads if top else heads // next_group
    first = first_head(sizes, level, rate_ref.shape[0], forward)
    place = place_at(sizes, level, forward)
    top_place = place_at(sizes, level + 1, forward)
    for k in range(1 if top else next_group):
        start = 0 if top else (place_at(sizes, level + 1) ^ k) * part_heads
        for i in range(part_heads):
            rate = rate_ref[pl.ds(first + start + i, 1), :]
            if top:
                before = None
                for j in range(1, next_group):
                    weight = row_weight(rate, span * group, top_place - 1 - (top_place ^ j))
                    term = weight * ahead[j - 1][i].astype(F32)
                    before = term if before is None else before + term
            else:
                before = ahead[k][i].astype(F32)
            own = [states[j][start + i].astype(F32) for j in range(group)]
            for j in range(group):
                total = row_weight(rate, span, place ^ j) * before
                for q in range(group):
                    if q != j:
                        total = total + row_weight(rate, span, (place ^ j) - 1 - (place ^ q)) * own[q]
                outs[j][start + i] = total.astype(BF16)


WHOLE = pl.BlockSpec(memory_space=pltpu.VMEM)
ANYWHERE = pl.BlockSpec(memory_space=pl.ANY)


def call(body, inputs, outputs, scratch=(), anywhere=(), out_anywhere=(), aliases=None, flops=0, name=None):
    nbytes = sum(a.size * a.dtype.itemsize for a in inputs) + sum(s.size * s.dtype.itemsize for s in outputs)
    return pl.pallas_call(
        body,
        in_specs=[ANYWHERE if n in anywhere else WHOLE for n in range(len(inputs))],
        out_specs=[ANYWHERE if n in out_anywhere else WHOLE for n in range(len(outputs))],
        scratch_shapes=list(scratch),
        out_shape=list(outputs),
        input_output_aliases=aliases or {},
        compiler_params=pltpu.CompilerParams(vmem_limit_bytes=VMEM_LIMIT),
        cost_estimate=pl.CostEstimate(flops=flops, bytes_accessed=nbytes, transcendentals=0),
        name=name,
    )(*inputs)


def level_sizes(devices):
    sizes = [2]
    left = devices // 2
    while left > 8:
        sizes.append(4)
        left //= 4
    return sizes + [left]


def swap(array, distance, devices):
    return lax.ppermute(array, AXES, [(i, i ^ distance) for i in range(devices)])


def carry_states(kept, sent, devices, rates, length, forward, beside):
    sizes = level_sizes(devices)
    state = kept.shape[1:]

    def climb(level, low, parts):
        group, next_group = sizes[level], sizes[level + 1]
        top = level + 2 == len(sizes)
        span = float(length * low)
        states = [parts[0]] + [swap(parts[k], k * low, devices) for k in range(1, group)]
        heads = parts[0].shape[0]
        count = 1 if top else next_group
        part_heads = heads if top else heads // next_group
        extra = list(beside[0]) if level == 1 else []
        inputs = [rates] + states + extra
        folded = call(
            functools.partial(fold_kernel, sizes, level, span, forward),
            inputs,
            [jax.ShapeDtypeStruct((part_heads,) + state, BF16)] * count,
            anywhere=range(1 + group, len(inputs)),
            name="fold_states",
        )
        if top:
            ahead = [swap(folded[0], k * low * group, devices) for k in range(1, next_group)]
        else:
            ahead = climb(level + 1, low * group, folded)
        extra = list(beside[1]) if level == 1 else []
        inputs = [rates] + states + ahead + extra
        outs = call(
            functools.partial(spread_kernel, sizes, level, span, forward),
            inputs,
            [jax.ShapeDtypeStruct((heads,) + state, BF16)] * group,
            anywhere=range(1 + group + len(ahead), len(inputs)),
            name="spread_states",
        )
        return [outs[0]] + [swap(outs[k], k * low, devices) for k in range(1, group)]

    return climb(0, 1, [kept, sent])


def local(devices, queries, key_vectors, value_vectors, output_grad, decay_rate, norm_gain):
    length, heads, size = queries.shape
    half = heads // 2
    rates = jnp.broadcast_to(decay_rate[:, None], (heads, size))

    def shaped(*shape, dtype=BF16):
        return jax.ShapeDtypeStruct(shape, dtype)

    per_head = shaped(half, length, size)
    per_head_wide = shaped(half, length, size, dtype=F32)
    states = shaped(half, size, size)
    whole = shaped(length, heads, size)
    flat = pltpu.VMEM((length * half, size), F32)
    stage = pltpu.VMEM((length, half, size), BF16)
    sems = pltpu.SemaphoreType.DMA((2, CHUNKS))
    unit = 2 * half * length * size * size

    keys, values, local_states = [None, None], [None, None], [None, None]
    for s in (1, 0):
        keys[s], values[s], local_states[s] = call(
            functools.partial(local_kernel, s == 0),
            [key_vectors, value_vectors, rates],
            [per_head, per_head, states],
            [stage, stage, flat, flat, sems],
            anywhere=(0, 1),
            flops=unit,
            name="local_states",
        )
    query, grad, attention, inner = [None, None], [None, None], [None, None], [None, None]
    for s in (0, 1):
        query[s], grad[s], attention[s], inner[s] = call(
            functools.partial(attention_kernel, s == 0),
            [queries, output_grad, keys[s], values[s], rates],
            [per_head, per_head, shaped(half, length, length), per_head_wide],
            [flat, flat],
            flops=2 * unit,
            name="attention",
        )
    incoming = carry_states(
        local_states[0], local_states[1], devices, rates, length, True, [inner[:1], inner[1:]]
    )
    normed, grad_out, state_grad = [None, None], [None, None], [None, None]
    for s in (0, 1):
        normed[s], grad_out[s], state_grad[s] = call(
            functools.partial(norm_kernel, s == 0),
            [query[s], grad[s], inner[s], incoming[s], rates, norm_gain],
            [per_head, per_head, states],
            flops=2 * unit,
            name="norm",
        )
    normed_out, query_out, key_part, value_part = None, None, [None, None], [None, None]
    for s in (0, 1):
        inputs = [query[s], keys[s], values[s], attention[s], grad_out[s], incoming[s], normed[s], rates]
        count = len(inputs)
        aliases = {}
        if s:
            aliases = {count: 0, count + 1: 1}
            inputs += [normed_out, query_out]
        normed_out, query_out, key_part[s], value_part[s] = call(
            functools.partial(grad_kernel, s == 0),
            inputs,
            [whole, whole, per_head_wide, per_head_wide],
            [flat, flat, stage, stage, sems],
            anywhere=(count, count + 1),
            out_anywhere=(0, 1),
            aliases=aliases,
            flops=5 * unit,
            name="stretch_gradients",
        )
    later = carry_states(
        state_grad[1], state_grad[0], devices, rates, length, False, [key_part[:1], key_part[1:]]
    )
    key_out, value_out = None, None
    for s in (1, 0):
        inputs = [keys[s], values[s], later[1 - s], key_part[s], value_part[s], rates]
        count = len(inputs)
        aliases = {}
        if s == 0:
            aliases = {count: 0, count + 1: 1}
            inputs += [key_out, value_out]
        key_out, value_out = call(
            functools.partial(later_kernel, s == 0),
            inputs,
            [whole, whole],
            [flat, flat, stage, stage, sems],
            anywhere=(count, count + 1),
            out_anywhere=(0, 1),
            aliases=aliases,
            flops=2 * unit,
            name="later_gradients",
        )
    return normed_out, query_out, key_out, value_out


def solution(mesh):
    devices = mesh.shape["ctx"] * mesh.shape["head"]
    spread = P(AXES, None, None)
    return jax.shard_map(
        functools.partial(local, devices),
        mesh=mesh,
        in_specs=(spread, spread, spread, spread, P(), P()),
        out_specs=(spread, spread, spread, spread),
        check_vma=False,
    )
```

time: 123 us -> 83.1 us (0.68)
  Pallas kernels: 48.3 us -> 22 us
  local copies, waits for them, and re-layouts: 10.9 us -> 3.28 us
  waiting for transfers between devices: 37.3 us -> 31.4 us
    pallas_call x18, Pallas kernels: 48.3 us -> 22 us  [call(): pl.pallas_call(body, in_specs=[ANYWHERE if n in anywhere else WHOLE for n...]
    unnamed x62 -> x12, local copies, waits for them, and re-layouts: 10.8 us -> 2.55 us
    ppermute x22, waiting for transfers between devices: 37.3 us -> 31.4 us  [swap(): lax.ppermute(array, AXES, [(i, i ^ distance) for i in range(devices)])]
  transfers between devices with their start and end apart: 22 -> 22, of which waited for: 11 -> 13; matrix products, arithmetic and copies ran while one was open for 0% -> 0% of each run, Pallas kernels for 21% -> 19%
where the time goes in v2:
time: 83.1 us; the launch traced here: 82.8 us
  waiting for transfers between devices  31.4 us (38%)
  starting transfers between devices  25.2 us (30%)
  Pallas kernels  22 us (26%)
  local copies, waits for them, and re-layouts  3.28 us (4%)
  between operations  0.97 us (1%)
    ppermute x22, waiting for transfers between devices, swap(): lax.ppermute(array, AXES, [(i, i ^ distance) for i in range(devices)])  31.4 us
    ppermute x22, starting transfers between devices, swap(): lax.ppermute(array, AXES, [(i, i ^ distance) for i in range(devices)])  25.2 us
    pallas_call x18, Pallas kernels, call(): pl.pallas_call(body, in_specs=[ANYWHERE if n in anywhere else WHOLE for n...  22 us
    unnamed x12, local copies, waits for them, and re-layouts  2.55 us
  transfers between devices with their start and end apart: 22, of which 13 were waited for; matrix products, arithmetic and copies ran while one was open for 0% of the time, Pallas kernels for 19%

profile of v2, /device:TPU:0, one launch (start us, length us, event | category | flops | bytes accessed | tf_op | source)
XLA Modules:
  0.0 82.8 jit_solution(17066052746761795117)
XLA Ops:
  7.3 2.9 %collective-permute-start.1 = (bf16[4,128,128]{2,1,0:T(8,128)(2,1)S(1)}, bf16[4,128,128]{2,1,0:T(8,128)(2,1)S(1)}, u32[]{:S(2)}, u32[]{:S(2)}) collective-permute-start(bf16[4,128,128]{2,1,0:T(8,128)(2,1)S(1)} %get-tuple-element.65), channel_id=1, source_target_pairs={{0,2},{1,3},{2,0},{3,1},{4,6},{5,7},{6,4},{7,5},{8,10},{9,11},{10,... | collective-permute-start | bytes 393224 | tf_op jit(solution)/shard_map/ppermute | solution.py:308
  10.2 1.5 %collective-permute-start.2 = (bf16[4,128,128]{2,1,0:T(8,128)(2,1)S(1)}, bf16[4,128,128]{2,1,0:T(8,128)(2,1)S(1)}, u32[]{:S(2)}, u32[]{:S(2)}) collective-permute-start(bf16[4,128,128]{2,1,0:T(8,128)(2,1)S(1)} %get-tuple-element.66), channel_id=1, source_target_pairs={{0,4},{1,5},{2,6},{3,7},{4,0},{5,1},{6,2},{7,3},{8,12},{9,13},{10,... | collective-permute-start | bytes 393224 | tf_op jit(solution)/shard_map/ppermute | solution.py:308
  14.1 4.2 %collective-permute-done.2.refs_2_ = bf16[4,128,128]{2,1,0:T(8,128)(2,1)S(1)} collective-permute-done((bf16[4,128,128]{2,1,0:T(8,128)(2,1)S(1)}, bf16[4,128,128]{2,1,0:T(8,128)(2,1)S(1)}, u32[]{:S(2)}, u32[]{:S(2)}) %collective-permute-start.2) | collective-permute-done | bytes 131104 | tf_op jit(solution)/shard_map/ppermute | solution.py:308
  18.5 1.6 %collective-permute-start.4 = (bf16[4,128,128]{2,1,0:T(8,128)(2,1)S(1)}, bf16[4,128,128]{2,1,0:T(8,128)(2,1)S(1)}, u32[]{:S(2)}, u32[]{:S(2)}) collective-permute-start(bf16[4,128,128]{2,1,0:T(8,128)(2,1)S(1)} %fold_states.5), channel_id=1, source_target_pairs={{0,8},{1,9},{2,10},{3,11},{4,12},{5,13},{6,14},{7,15},{8,0},{9,1},... | collective-permute-start | bytes 393224 | tf_op jit(solution)/shard_map/ppermute | solution.py:308
  20.1 2.6 %collective-permute-start.5 = (bf16[4,128,128]{2,1,0:T(8,128)(2,1)S(1)}, bf16[4,128,128]{2,1,0:T(8,128)(2,1)S(1)}, u32[]{:S(2)}, u32[]{:S(2)}) collective-permute-start(bf16[4,128,128]{2,1,0:T(8,128)(2,1)S(1)} %fold_states.5), channel_id=1, source_target_pairs={{0,16},{1,17},{2,18},{3,19},{4,20},{5,21},{6,22},{7,23},{8,24},{9,... | collective-permute-start | bytes 393224 | tf_op jit(solution)/shard_map/ppermute | solution.py:308
  25.0 7.1 %collective-permute-done.5.refs_5_ = bf16[4,128,128]{2,1,0:T(8,128)(2,1)S(1)} collective-permute-done((bf16[4,128,128]{2,1,0:T(8,128)(2,1)S(1)}, bf16[4,128,128]{2,1,0:T(8,128)(2,1)S(1)}, u32[]{:S(2)}, u32[]{:S(2)}) %collective-permute-start.5) | collective-permute-done | bytes 131104 | tf_op jit(solution)/shard_map/ppermute | solution.py:308
  32.5 1.7 %collective-permute-start.7 = (bf16[4,128,128]{2,1,0:T(8,128)(2,1)S(1)}, bf16[4,128,128]{2,1,0:T(8,128)(2,1)S(1)}, u32[]{:S(2)}, u32[]{:S(2)}) collective-permute-start(bf16[4,128,128]{2,1,0:T(8,128)(2,1)S(1)} %get-tuple-element.72), channel_id=1, source_target_pairs={{0,2},{1,3},{2,0},{3,1},{4,6},{5,7},{6,4},{7,5},{8,10},{9,11},{10,... | collective-permute-start | bytes 393224 | tf_op jit(solution)/shard_map/ppermute | solution.py:308
  36.1 1.5 %collective-permute-done.7.refs_3_ = bf16[4,128,128]{2,1,0:T(8,128)(2,1)S(1)} collective-permute-done((bf16[4,128,128]{2,1,0:T(8,128)(2,1)S(1)}, bf16[4,128,128]{2,1,0:T(8,128)(2,1)S(1)}, u32[]{:S(2)}, u32[]{:S(2)}) %collective-permute-start.7) | collective-permute-done | bytes 131104 | tf_op jit(solution)/shard_map/ppermute | solution.py:308
  37.6 1.7 %collective-permute-done.8.refs_4_ = bf16[4,128,128]{2,1,0:T(8,128)(2,1)S(1)} collective-permute-done((bf16[4,128,128]{2,1,0:T(8,128)(2,1)S(1)}, bf16[4,128,128]{2,1,0:T(8,128)(2,1)S(1)}, u32[]{:S(2)}, u32[]{:S(2)}) %collective-permute-start.8) | collective-permute-done | bytes 131104 | tf_op jit(solution)/shard_map/ppermute | solution.py:308
  41.4 1.7 %norm.3 = (bf16[16,128,128]{2,1,0:T(8,128)(2,1)S(1)}, bf16[16,128,128]{2,1,0:T(8,128)(2,1)S(1)}, bf16[16,128,128]{2,1,0:T(8,128)(2,1)S(1)}) custom-call(bf16[16,128,128]{2,1,0:T(8,128)(2,1)S(1)} %get-tuple-element.78.qt_ref, bf16[16,128,128]{2,1,0:T(8,128)(2,1)S(1)} %get-tuple-element.80.gt_ref, f32[16,128,128]{2,1,0:T(8,128)S(1)} %get-tuple-element.70.refs_4_.o_ref, ...), custom_call_target="tpu_custom_call" | custom-call | flops 134217728 | bytes 4227072 | tf_op jit(solution)/shard_map/norm/pallas_call | solution.py:285
  43.6 1.7 %norm.2 = (bf16[16,128,128]{2,1,0:T(8,128)(2,1)S(1)}, bf16[16,128,128]{2,1,0:T(8,128)(2,1)S(1)}, bf16[16,128,128]{2,1,0:T(8,128)(2,1)S(1)}) custom-call(bf16[16,128,128]{2,1,0:T(8,128)(2,1)S(1)} %get-tuple-element.58.qt_ref, bf16[16,128,128]{2,1,0:T(8,128)(2,1)S(1)} %get-tuple-element.60.gt_ref, f32[16,128,128]{2,1,0:T(8,128)S(1)} %get-tuple-element.61.refs_7_.o_ref, ...), custom_call_target="tpu_custom_call" | custom-call | flops 134217728 | bytes 4227072 | tf_op jit(solution)/shard_map/norm/pallas_call | solution.py:285
  45.6 1.5 %collective-permute-start.12 = (bf16[4,128,128]{2,1,0:T(8,128)(2,1)S(1)}, bf16[4,128,128]{2,1,0:T(8,128)(2,1)S(1)}, u32[]{:S(2)}, u32[]{:S(2)}) collective-permute-start(bf16[4,128,128]{2,1,0:T(8,128)(2,1)S(1)} %get-tuple-element.91), channel_id=1, source_target_pairs={{0,2},{1,3},{2,0},{3,1},{4,6},{5,7},{6,4},{7,5},{8,10},{9,11},{10,... | collective-permute-start | bytes 393224 | tf_op jit(solution)/shard_map/ppermute | solution.py:308
  47.6 1.5 %collective-permute-start.14 = (bf16[4,128,128]{2,1,0:T(8,128)(2,1)S(1)}, bf16[4,128,128]{2,1,0:T(8,128)(2,1)S(1)}, u32[]{:S(2)}, u32[]{:S(2)}) collective-permute-start(bf16[4,128,128]{2,1,0:T(8,128)(2,1)S(1)} %get-tuple-element.93), channel_id=1, source_target_pairs={{0,6},{1,7},{2,4},{3,5},{4,2},{5,3},{6,0},{7,1},{8,14},{9,15},{10,... | collective-permute-start | bytes 393224 | tf_op jit(solution)/shard_map/ppermute | solution.py:308
  49.2 3.1 %stretch_gradients.2 = (bf16[128,32,128]{2,1,0:T(8,128)(2,1)}, bf16[128,32,128]{2,1,0:T(8,128)(2,1)}, f32[16,128,128]{2,1,0:T(8,128)S(1)}, f32[16,128,128]{2,1,0:T(8,128)S(1)}) custom-call(bf16[16,128,128]{2,1,0:T(8,128)(2,1)S(1)} %get-tuple-element.78.qt_ref, bf16[16,128,128]{2,1,0:T(8,128)(2,1)S(1)} %get-tuple-element.68.kt_ref, ...), custom_call_target="tpu_custom_call" | custom-call | flops 335544320 | bytes 7880704 | tf_op jit(solution)/shard_map/stretch_gradients/pallas_call | solution.py:285
  52.3 2.9 %collective-permute-done.13.refs_2_ = bf16[4,128,128]{2,1,0:T(8,128)(2,1)S(1)} collective-permute-done((bf16[4,128,128]{2,1,0:T(8,128)(2,1)S(1)}, bf16[4,128,128]{2,1,0:T(8,128)(2,1)S(1)}, u32[]{:S(2)}, u32[]{:S(2)}) %collective-permute-start.13) | collective-permute-done | bytes 131104 | tf_op jit(solution)/shard_map/ppermute | solution.py:308
  55.4 2.0 %collective-permute-start.15 = (bf16[4,128,128]{2,1,0:T(8,128)(2,1)S(1)}, bf16[4,128,128]{2,1,0:T(8,128)(2,1)S(1)}, u32[]{:S(2)}, u32[]{:S(2)}) collective-permute-start(bf16[4,128,128]{2,1,0:T(8,128)(2,1)S(1)} %fold_states.7), channel_id=1, source_target_pairs={{0,8},{1,9},{2,10},{3,11},{4,12},{5,13},{6,14},{7,15},{8,0},{9,1},... | collective-permute-start | bytes 393224 | tf_op jit(solution)/shard_map/ppermute | solution.py:308
  59.9 3.3 %stretch_gradients.3 = (bf16[128,32,128]{2,1,0:T(8,128)(2,1)}, bf16[128,32,128]{2,1,0:T(8,128)(2,1)}, f32[16,128,128]{2,1,0:T(8,128)S(1)}, f32[16,128,128]{2,1,0:T(8,128)S(1)}) custom-call(bf16[16,128,128]{2,1,0:T(8,128)(2,1)S(1)} %get-tuple-element.58.qt_ref, ...), custom_call_target="tpu_custom_call", output_to_operand_aliasing={{0}: (8, {}), {1}: (9, {})} | custom-call | flops 335544320 | bytes 9977856 | tf_op jit(solution)/shard_map/stretch_gradients/pallas_call | solution.py:285
  63.2 6.4 %collective-permute-done.16.refs_5_ = bf16[4,128,128]{2,1,0:T(8,128)(2,1)S(1)} collective-permute-done((bf16[4,128,128]{2,1,0:T(8,128)(2,1)S(1)}, bf16[4,128,128]{2,1,0:T(8,128)(2,1)S(1)}, u32[]{:S(2)}, u32[]{:S(2)}) %collective-permute-start.16) | collective-permute-done | bytes 131104 | tf_op jit(solution)/shard_map/ppermute | solution.py:308
  70.3 1.8 %collective-permute-start.19 = (bf16[4,128,128]{2,1,0:T(8,128)(2,1)S(1)}, bf16[4,128,128]{2,1,0:T(8,128)(2,1)S(1)}, u32[]{:S(2)}, u32[]{:S(2)}) collective-permute-start(bf16[4,128,128]{2,1,0:T(8,128)(2,1)S(1)} %get-tuple-element.98), channel_id=1, source_target_pairs={{0,4},{1,5},{2,6},{3,7},{4,0},{5,1},{6,2},{7,3},{8,12},{9,13},{10,... | collective-permute-start | bytes 393224 | tf_op jit(solution)/shard_map/ppermute | solution.py:308
  72.1 1.5 %collective-permute-start.20 = (bf16[4,128,128]{2,1,0:T(8,128)(2,1)S(1)}, bf16[4,128,128]{2,1,0:T(8,128)(2,1)S(1)}, u32[]{:S(2)}, u32[]{:S(2)}) collective-permute-start(bf16[4,128,128]{2,1,0:T(8,128)(2,1)S(1)} %get-tuple-element.99), channel_id=1, source_target_pairs={{0,6},{1,7},{2,4},{3,5},{4,2},{5,3},{6,0},{7,1},{8,14},{9,15},{10,... | collective-permute-start | bytes 393224 | tf_op jit(solution)/shard_map/ppermute | solution.py:308
  73.6 1.5 %collective-permute-done.18.refs_3_ = bf16[4,128,128]{2,1,0:T(8,128)(2,1)S(1)} collective-permute-done((bf16[4,128,128]{2,1,0:T(8,128)(2,1)S(1)}, bf16[4,128,128]{2,1,0:T(8,128)(2,1)S(1)}, u32[]{:S(2)}, u32[]{:S(2)}) %collective-permute-start.18) | collective-permute-done | bytes 131104 | tf_op jit(solution)/shard_map/ppermute | solution.py:308
  76.0 1.9 %collective-permute-done.20.refs_5_ = bf16[4,128,128]{2,1,0:T(8,128)(2,1)S(1)} collective-permute-done((bf16[4,128,128]{2,1,0:T(8,128)(2,1)S(1)}, bf16[4,128,128]{2,1,0:T(8,128)(2,1)S(1)}, u32[]{:S(2)}, u32[]{:S(2)}) %collective-permute-start.20) | collective-permute-done | bytes 131104 | tf_op jit(solution)/shard_map/ppermute | solution.py:308
  78.6 2.0 %later_gradients.2 = (bf16[128,32,128]{2,1,0:T(8,128)(2,1)}, bf16[128,32,128]{2,1,0:T(8,128)(2,1)}) custom-call(bf16[16,128,128]{2,1,0:T(8,128)(2,1)S(1)} %get-tuple-element.56.kt_ref, bf16[16,128,128]{2,1,0:T(8,128)(2,1)S(1)} %get-tuple-element.57.vt_ref, bf16[16,128,128]{2,1,0:T(8,128)(2,1)S(1)} %get-tuple-element.102.later_ref, ...), custom_call_target="tpu_custom_call" | custom-call | flops 134217728 | bytes 5783552 | tf_op jit(solution)/shard_map/later_gradients/pallas_call | solution.py:285
  80.6 2.0 %later_gradients.3 = (bf16[128,32,128]{2,1,0:T(8,128)(2,1)}, bf16[128,32,128]{2,1,0:T(8,128)(2,1)}) custom-call(bf16[16,128,128]{2,1,0:T(8,128)(2,1)S(1)} %get-tuple-element.68.kt_ref, bf16[16,128,128]{2,1,0:T(8,128)(2,1)S(1)} %get-tuple-element.69.vt_ref, ...), custom_call_target="tpu_custom_call", output_to_operand_aliasing={{0}: (6, {}), {1}: (7, {})} | custom-call | flops 134217728 | bytes 7880704 | tf_op jit(solution)/shard_map/later_gradients/pallas_call | solution.py:285
  (51 shorter events, 21.9 us)
Async XLA Ops:
  5.0 2.1 %collective-permute-start = (bf16[16,128,128]{2,1,0:T(8,128)(2,1)S(1)}, bf16[16,128,128]{2,1,0:T(8,128)(2,1)S(1)}, u32[]{:S(2)}, u32[]{:S(2)}) collective-permute-start(bf16[16,128,128]{2,1,0:T(8,128)(2,1)S(1)} %get-tuple-element.63), channel_id=1, source_target_pairs={{0,1},{1,0},{2,3},{3,2},{4,5},{5,4},{6,7},{7,6},{8,9},{9,8},{10,11... | collective-permute-start | bytes 1572872 | tf_op jit(solution)/shard_map/ppermute | solution.py:308
  5.5 6.3 %copy-start.1 = (bf16[128,32,128]{2,1,0:T(8,128)(2,1)S(1)}, bf16[128,32,128]{2,1,0:T(8,128)(2,1)}, u32[]{:S(2)}) copy-start(bf16[128,32,128]{2,1,0:T(8,128)(2,1)} %g_ref.3) | copy-start | bytes 3145732
  6.7 5.1 %copy-start = (bf16[128,32,128]{2,1,0:T(8,128)(2,1)S(1)}, bf16[128,32,128]{2,1,0:T(8,128)(2,1)}, u32[]{:S(2)}) copy-start(bf16[128,32,128]{2,1,0:T(8,128)(2,1)} %q_ref.3) | copy-start | bytes 3145732
  7.3 6.8 %collective-permute-start.1 = (bf16[4,128,128]{2,1,0:T(8,128)(2,1)S(1)}, bf16[4,128,128]{2,1,0:T(8,128)(2,1)S(1)}, u32[]{:S(2)}, u32[]{:S(2)}) collective-permute-start(bf16[4,128,128]{2,1,0:T(8,128)(2,1)S(1)} %get-tuple-element.65), channel_id=1, source_target_pairs={{0,2},{1,3},{2,0},{3,1},{4,6},{5,7},{6,4},{7,5},{8,10},{9,11},{10,... | collective-permute-start | bytes 393224 | tf_op jit(solution)/shard_map/ppermute | solution.py:308
  10.2 8.1 %collective-permute-start.2 = (bf16[4,128,128]{2,1,0:T(8,128)(2,1)S(1)}, bf16[4,128,128]{2,1,0:T(8,128)(2,1)S(1)}, u32[]{:S(2)}, u32[]{:S(2)}) collective-permute-start(bf16[4,128,128]{2,1,0:T(8,128)(2,1)S(1)} %get-tuple-element.66), channel_id=1, source_target_pairs={{0,4},{1,5},{2,6},{3,7},{4,0},{5,1},{6,2},{7,3},{8,12},{9,13},{10,... | collective-permute-start | bytes 393224 | tf_op jit(solution)/shard_map/ppermute | solution.py:308
  11.7 6.6 %collective-permute-start.3 = (bf16[4,128,128]{2,1,0:T(8,128)(2,1)S(1)}, bf16[4,128,128]{2,1,0:T(8,128)(2,1)S(1)}, u32[]{:S(2)}, u32[]{:S(2)}) collective-permute-start(bf16[4,128,128]{2,1,0:T(8,128)(2,1)S(1)} %get-tuple-element.67), channel_id=1, source_target_pairs={{0,6},{1,7},{2,4},{3,5},{4,2},{5,3},{6,0},{7,1},{8,14},{9,15},{10,... | collective-permute-start | bytes 393224 | tf_op jit(solution)/shard_map/ppermute | solution.py:308
  18.5 6.5 %collective-permute-start.4 = (bf16[4,128,128]{2,1,0:T(8,128)(2,1)S(1)}, bf16[4,128,128]{2,1,0:T(8,128)(2,1)S(1)}, u32[]{:S(2)}, u32[]{:S(2)}) collective-permute-start(bf16[4,128,128]{2,1,0:T(8,128)(2,1)S(1)} %fold_states.5), channel_id=1, source_target_pairs={{0,8},{1,9},{2,10},{3,11},{4,12},{5,13},{6,14},{7,15},{8,0},{9,1},... | collective-permute-start | bytes 393224 | tf_op jit(solution)/shard_map/ppermute | solution.py:308
  20.1 12.0 %collective-permute-start.5 = (bf16[4,128,128]{2,1,0:T(8,128)(2,1)S(1)}, bf16[4,128,128]{2,1,0:T(8,128)(2,1)S(1)}, u32[]{:S(2)}, u32[]{:S(2)}) collective-permute-start(bf16[4,128,128]{2,1,0:T(8,128)(2,1)S(1)} %fold_states.5), channel_id=1, source_target_pairs={{0,16},{1,17},{2,18},{3,19},{4,20},{5,21},{6,22},{7,23},{8,24},{9,... | collective-permute-start | bytes 393224 | tf_op jit(solution)/shard_map/ppermute | solution.py:308
  22.7 9.4 %collective-permute-start.6 = (bf16[4,128,128]{2,1,0:T(8,128)(2,1)S(1)}, bf16[4,128,128]{2,1,0:T(8,128)(2,1)S(1)}, u32[]{:S(2)}, u32[]{:S(2)}) collective-permute-start(bf16[4,128,128]{2,1,0:T(8,128)(2,1)S(1)} %fold_states.5), channel_id=1, source_target_pairs={{0,24},{1,25},{2,26},{3,27},{4,28},{5,29},{6,30},{7,31},{8,16},{9,... | collective-permute-start | bytes 393224 | tf_op jit(solution)/shard_map/ppermute | solution.py:308
  32.5 5.0 %collective-permute-start.7 = (bf16[4,128,128]{2,1,0:T(8,128)(2,1)S(1)}, bf16[4,128,128]{2,1,0:T(8,128)(2,1)S(1)}, u32[]{:S(2)}, u32[]{:S(2)}) collective-permute-start(bf16[4,128,128]{2,1,0:T(8,128)(2,1)S(1)} %get-tuple-element.72), channel_id=1, source_target_pairs={{0,2},{1,3},{2,0},{3,1},{4,6},{5,7},{6,4},{7,5},{8,10},{9,11},{10,... | collective-permute-start | bytes 393224 | tf_op jit(solution)/shard_map/ppermute | solution.py:308
  34.3 5.0 %collective-permute-start.8 = (bf16[4,128,128]{2,1,0:T(8,128)(2,1)S(1)}, bf16[4,128,128]{2,1,0:T(8,128)(2,1)S(1)}, u32[]{:S(2)}, u32[]{:S(2)}) collective-permute-start(bf16[4,128,128]{2,1,0:T(8,128)(2,1)S(1)} %get-tuple-element.73), channel_id=1, source_target_pairs={{0,4},{1,5},{2,6},{3,7},{4,0},{5,1},{6,2},{7,3},{8,12},{9,13},{10,... | collective-permute-start | bytes 393224 | tf_op jit(solution)/shard_map/ppermute | solution.py:308
  34.8 5.9 %collective-permute-start.9 = (bf16[4,128,128]{2,1,0:T(8,128)(2,1)S(1)}, bf16[4,128,128]{2,1,0:T(8,128)(2,1)S(1)}, u32[]{:S(2)}, u32[]{:S(2)}) collective-permute-start(bf16[4,128,128]{2,1,0:T(8,128)(2,1)S(1)} %get-tuple-element.74), channel_id=1, source_target_pairs={{0,6},{1,7},{2,4},{3,5},{4,2},{5,3},{6,0},{7,1},{8,14},{9,15},{10,... | collective-permute-start | bytes 393224 | tf_op jit(solution)/shard_map/ppermute | solution.py:308
  41.2 2.4 %collective-permute-start.10 = (bf16[16,128,128]{2,1,0:T(8,128)(2,1)S(1)}, bf16[16,128,128]{2,1,0:T(8,128)(2,1)S(1)}, u32[]{:S(2)}, u32[]{:S(2)}) collective-permute-start(bf16[16,128,128]{2,1,0:T(8,128)(2,1)S(1)} %get-tuple-element.75), channel_id=1, source_target_pairs={{0,1},{1,0},{2,3},{3,2},{4,5},{5,4},{6,7},{7,6},{8,9},{9,8},{10,11... | collective-permute-start | bytes 1572872 | tf_op jit(solution)/shard_map/ppermute | solution.py:308
  43.1 2.2 %collective-permute-start.11 = (bf16[16,128,128]{2,1,0:T(8,128)(2,1)S(1)}, bf16[16,128,128]{2,1,0:T(8,128)(2,1)S(1)}, u32[]{:S(2)}, u32[]{:S(2)}) collective-permute-start(bf16[16,128,128]{2,1,0:T(8,128)(2,1)S(1)} %get-tuple-element.89), channel_id=1, source_target_pairs={{0,1},{1,0},{2,3},{3,2},{4,5},{5,4},{6,7},{7,6},{8,9},{9,8},{10,11... | collective-permute-start | bytes 1572872 | tf_op jit(solution)/shard_map/ppermute | solution.py:308
  45.6 6.7 %collective-permute-start.12 = (bf16[4,128,128]{2,1,0:T(8,128)(2,1)S(1)}, bf16[4,128,128]{2,1,0:T(8,128)(2,1)S(1)}, u32[]{:S(2)}, u32[]{:S(2)}) collective-permute-start(bf16[4,128,128]{2,1,0:T(8,128)(2,1)S(1)} %get-tuple-element.91), channel_id=1, source_target_pairs={{0,2},{1,3},{2,0},{3,1},{4,6},{5,7},{6,4},{7,5},{8,10},{9,11},{10,... | collective-permute-start | bytes 393224 | tf_op jit(solution)/shard_map/ppermute | solution.py:308
  47.1 8.1 %collective-permute-start.13 = (bf16[4,128,128]{2,1,0:T(8,128)(2,1)S(1)}, bf16[4,128,128]{2,1,0:T(8,128)(2,1)S(1)}, u32[]{:S(2)}, u32[]{:S(2)}) collective-permute-start(bf16[4,128,128]{2,1,0:T(8,128)(2,1)S(1)} %get-tuple-element.92), channel_id=1, source_target_pairs={{0,4},{1,5},{2,6},{3,7},{4,0},{5,1},{6,2},{7,3},{8,12},{9,13},{10,... | collective-permute-start | bytes 393224 | tf_op jit(solution)/shard_map/ppermute | solution.py:308
  47.6 7.6 %collective-permute-start.14 = (bf16[4,128,128]{2,1,0:T(8,128)(2,1)S(1)}, bf16[4,128,128]{2,1,0:T(8,128)(2,1)S(1)}, u32[]{:S(2)}, u32[]{:S(2)}) collective-permute-start(bf16[4,128,128]{2,1,0:T(8,128)(2,1)S(1)} %get-tuple-element.93), channel_id=1, source_target_pairs={{0,6},{1,7},{2,4},{3,5},{4,2},{5,3},{6,0},{7,1},{8,14},{9,15},{10,... | collective-permute-start | bytes 393224 | tf_op jit(solution)/shard_map/ppermute | solution.py:308
  55.4 7.8 %collective-permute-start.15 = (bf16[4,128,128]{2,1,0:T(8,128)(2,1)S(1)}, bf16[4,128,128]{2,1,0:T(8,128)(2,1)S(1)}, u32[]{:S(2)}, u32[]{:S(2)}) collective-permute-start(bf16[4,128,128]{2,1,0:T(8,128)(2,1)S(1)} %fold_states.7), channel_id=1, source_target_pairs={{0,8},{1,9},{2,10},{3,11},{4,12},{5,13},{6,14},{7,15},{8,0},{9,1},... | collective-permute-start | bytes 393224 | tf_op jit(solution)/shard_map/ppermute | solution.py:308
  57.4 12.2 %collective-permute-start.16 = (bf16[4,128,128]{2,1,0:T(8,128)(2,1)S(1)}, bf16[4,128,128]{2,1,0:T(8,128)(2,1)S(1)}, u32[]{:S(2)}, u32[]{:S(2)}) collective-permute-start(bf16[4,128,128]{2,1,0:T(8,128)(2,1)S(1)} %fold_states.7), channel_id=1, source_target_pairs={{0,16},{1,17},{2,18},{3,19},{4,20},{5,21},{6,22},{7,23},{8,24},{9,... | collective-permute-start | bytes 393224 | tf_op jit(solution)/shard_map/ppermute | solution.py:308
  58.5 11.1 %collective-permute-start.17 = (bf16[4,128,128]{2,1,0:T(8,128)(2,1)S(1)}, bf16[4,128,128]{2,1,0:T(8,128)(2,1)S(1)}, u32[]{:S(2)}, u32[]{:S(2)}) collective-permute-start(bf16[4,128,128]{2,1,0:T(8,128)(2,1)S(1)} %fold_states.7), channel_id=1, source_target_pairs={{0,24},{1,25},{2,26},{3,27},{4,28},{5,29},{6,30},{7,31},{8,16},{9,... | collective-permute-start | bytes 393224 | tf_op jit(solution)/shard_map/ppermute | solution.py:308
  70.1 5.0 %collective-permute-start.18 = (bf16[4,128,128]{2,1,0:T(8,128)(2,1)S(1)}, bf16[4,128,128]{2,1,0:T(8,128)(2,1)S(1)}, u32[]{:S(2)}, u32[]{:S(2)}) collective-permute-start(bf16[4,128,128]{2,1,0:T(8,128)(2,1)S(1)} %get-tuple-element.97), channel_id=1, source_target_pairs={{0,2},{1,3},{2,0},{3,1},{4,6},{5,7},{6,4},{7,5},{8,10},{9,11},{10,... | collective-permute-start | bytes 393224 | tf_op jit(solution)/shard_map/ppermute | solution.py:308
  70.3 5.8 %collective-permute-start.19 = (bf16[4,128,128]{2,1,0:T(8,128)(2,1)S(1)}, bf16[4,128,128]{2,1,0:T(8,128)(2,1)S(1)}, u32[]{:S(2)}, u32[]{:S(2)}) collective-permute-start(bf16[4,128,128]{2,1,0:T(8,128)(2,1)S(1)} %get-tuple-element.98), channel_id=1, source_target_pairs={{0,4},{1,5},{2,6},{3,7},{4,0},{5,1},{6,2},{7,3},{8,12},{9,13},{10,... | collective-permute-start | bytes 393224 | tf_op jit(solution)/shard_map/ppermute | solution.py:308
  72.1 5.9 %collective-permute-start.20 = (bf16[4,128,128]{2,1,0:T(8,128)(2,1)S(1)}, bf16[4,128,128]{2,1,0:T(8,128)(2,1)S(1)}, u32[]{:S(2)}, u32[]{:S(2)}) collective-permute-start(bf16[4,128,128]{2,1,0:T(8,128)(2,1)S(1)} %get-tuple-element.99), channel_id=1, source_target_pairs={{0,6},{1,7},{2,4},{3,5},{4,2},{5,3},{6,0},{7,1},{8,14},{9,15},{10,... | collective-permute-start | bytes 393224 | tf_op jit(solution)/shard_map/ppermute | solution.py:308
  78.5 2.1 %collective-permute-start.21 = (bf16[16,128,128]{2,1,0:T(8,128)(2,1)S(1)}, bf16[16,128,128]{2,1,0:T(8,128)(2,1)S(1)}, u32[]{:S(2)}, u32[]{:S(2)}) collective-permute-start(bf16[16,128,128]{2,1,0:T(8,128)(2,1)S(1)} %get-tuple-element.100), channel_id=1, source_target_pairs={{0,1},{1,0},{2,3},{3,2},{4,5},{5,4},{6,7},{7,6},{8,9},{9,8},{10,11... | collective-permute-start | bytes 1572872 | tf_op jit(solution)/shard_map/ppermute | solution.py:308
  (4 other events, 4.9 us)

commit v3 on v2

--- a/solution.py
+++ b/solution.py
@@ -10,8 +10,11 @@
 F32 = jnp.float32
 BF16 = jnp.bfloat16
 VMEM_LIMIT = 16 * 1024 * 1024
-BATCH = 4
+LOCAL_LIMIT = 51 * 1024 * 1024
+BATCH = 16
 CHUNKS = 4
+PIECES = 1
+DOUBLING = True
 
 
 def dot(a, b, dims):
@@ -77,13 +80,31 @@
     return [range(start, start + size) for start in range(0, heads, size)]
 
 
-def local_kernel(own, k_ref, v_ref, rate_ref, kt_ref, vt_ref, s_ref, kb, vb, ks, vs, sems):
+def local_states(ks, vs, rates, kt_ref, vt_ref, s_ref):
+    heads, length, size = kt_ref.shape
+    tail_steps = length - 1.0 - positions((length, size))
+    for batch in batches(heads):
+        key = [one_head(ks, h, length, heads) for h in batch]
+        value = [one_head(vs, h, length, heads).astype(BF16) for h in batch]
+        tail = [decay(rates[h], tail_steps) for h in batch]
+        decayed = [(k * t).astype(BF16) for k, t in zip(key, tail)]
+        state = [dot(k, v, ATB) for k, v in zip(decayed, value)]
+        for i, h in enumerate(batch):
+            kt_ref[h] = key[i].astype(BF16)
+            vt_ref[h] = value[i]
+            s_ref[h] = state[i].astype(BF16)
+
+
+def first_local_kernel(k_ref, v_ref, rates_ref, kt_ref, vt_ref, s_ref, k_rest, v_rest, rates_out, *scratch):
+    kb, vb, ks, vs, rates, sems, rest_sems, rate_sem = scratch
     length, heads, size = kb.shape
-    half = head_half(own)
-    first = half * heads
-    start = pl.multiple_of(first, heads)
+    half = head_half(False)
+    start = pl.multiple_of(half * heads, heads)
+    rest = pl.multiple_of((1 - half) * heads, heads)
     chunks = sems.shape[1]
     rows = length // chunks
+    rate_copy = pltpu.make_async_copy(rates_ref, rates, rate_sem)
+    rate_copy.start()
     copies = []
     for c in range(chunks):
         piece = pl.ds(c * rows, rows)
@@ -91,6 +112,11 @@
             copy = pltpu.make_async_copy(ref.at[piece, pl.ds(start, heads), :], buffer.at[piece], sems.at[n, c])
             copy.start()
             copies.append(copy)
+    rest_copies = []
+    for n, (ref, buffer) in enumerate(((k_ref, k_rest), (v_ref, v_rest))):
+        copy = pltpu.make_async_copy(ref.at[:, pl.ds(rest, heads), :], buffer, rest_sems.at[n])
+        copy.start()
+        rest_copies.append(copy)
     for c in range(chunks):
         piece = pl.ds(c * rows, rows)
         flat = pl.ds(c * rows * heads, rows * heads)
@@ -98,17 +124,21 @@
         ks[flat, :] = kb[piece].astype(F32).reshape(rows * heads, size)
         copies[2 * c + 1].wait()
         vs[flat, :] = vb[piece].astype(F32).reshape(rows * heads, size)
-    tail_steps = length - 1.0 - positions((length, size))
-    for batch in batches(heads):
-        key = [one_head(ks, h, length, heads) for h in batch]
-        value = [one_head(vs, h, length, heads).astype(BF16) for h in batch]
-        tail = [decay(rate_ref[pl.ds(first + h, 1), :], tail_steps) for h in batch]
-        decayed = [(k * t).astype(BF16) for k, t in zip(key, tail)]
-        state = [dot(k, v, ATB) for k, v in zip(decayed, value)]
-        for i, h in enumerate(batch):
-            kt_ref[h] = key[i].astype(BF16)
-            vt_ref[h] = value[i]
-            s_ref[h] = state[i].astype(BF16)
+    rate_copy.wait()
+    for h in range(rates.shape[0]):
+        rates_out[pl.ds(h, 1), :] = jnp.full((1, size), rates[h], F32)
+    local_states(ks, vs, [rates[start + h] for h in range(heads)], kt_ref, vt_ref, s_ref)
+    for copy in rest_copies:
+        copy.wait()
+
+
+def second_local_kernel(k_ref, v_ref, rate_ref, kt_ref, vt_ref, s_ref, ks, vs):
+    heads, length, size = kt_ref.shape
+    first = head_half(True) * heads
+    ks[...] = k_ref[...].astype(F32).reshape(length * heads, size)
+    vs[...] = v_ref[...].astype(F32).reshape(length * heads, size)
+    rates = [rate_ref[pl.ds(first + h, 1), :] for h in range(heads)]
+    local_states(ks, vs, rates, kt_ref, vt_ref, s_ref)
 
 
 def attention_kernel(own, q_ref, g_ref, kt_ref, vt_ref, rate_ref, qt_ref, gt_ref, a_ref, o_ref, qs, gs):
@@ -154,9 +184,25 @@
             sg_ref[h] = state[i].astype(BF16)
 
 
-def grad_kernel(own, qt_ref, kt_ref, vt_ref, a_ref, go_ref, in_ref, n_ref, rate_ref, *rest):
-    n_out, dq_out, dk_ref, dv_ref, ns, ds, nb, db, sems = rest[-9:]
+def inner_kernel(own, qt_ref, vt_ref, a_ref, go_ref, rate_ref, gs_ref, dk_ref, dv_ref):
     heads, length, size = qt_ref.shape
+    first = head_half(own) * heads
+    for batch in batches(heads):
+        inner = [dot(go_ref[h], vt_ref[h], ABT) for h in batch]
+        value = [dot(a_ref[h], go_ref[h], ATB) for h in batch]
+        weights = [causal_weights(rate_ref[pl.ds(first + h, 1), :], length) for h in batch]
+        scores = [(s * w).astype(BF16) for s, w in zip(inner, weights)]
+        key = [dot(s, qt_ref[h], ATB) for s, h in zip(scores, batch)]
+        for i, h in enumerate(batch):
+            gs_ref[h] = scores[i]
+            dv_ref[h] = value[i]
+            dk_ref[h] = key[i]
+
+
+def query_kernel(own, kt_ref, gs_ref, go_ref, in_ref, n_ref, rate_ref, *rest):
+    n_out, dq_out, mark_ref, ns, ds, nb, db, sems = rest[-8:]
+    mark_ref[...] = jnp.zeros(mark_ref.shape, F32)
+    heads, length, size = kt_ref.shape
     half = head_half(own)
     first = half * heads
     head_steps = positions((length, size)) + 1.0
@@ -164,17 +210,11 @@
         ns[pl.ds(h, length, stride=heads), :] = n_ref[h].astype(F32)
     copies = start_output(ns, nb, n_out, sems.at[0], half)
     for batch in batches(heads):
-        inner = [dot(go_ref[h], vt_ref[h], ABT) for h in batch]
         through = [dot(go_ref[h], in_ref[h], ABT) for h in batch]
-        value = [dot(a_ref[h], go_ref[h], ATB) for h in batch]
-        rate = [rate_ref[pl.ds(first + h, 1), :] for h in batch]
-        scores = [(s * causal_weights(r, length)).astype(BF16) for s, r in zip(inner, rate)]
-        query = [dot(s, kt_ref[h], AB) for s, h in zip(scores, batch)]
-        key = [dot(s, qt_ref[h], ATB) for s, h in zip(scores, batch)]
+        query = [dot(gs_ref[h], kt_ref[h], AB) for h in batch]
         for i, h in enumerate(batch):
-            dv_ref[h] = value[i]
-            dk_ref[h] = key[i]
-            ds[pl.ds(h, length, stride=heads), :] = query[i] + decay(rate[i], head_steps) * through[i]
+            head_decay = decay(rate_ref[pl.ds(first + h, 1), :], head_steps)
+            ds[pl.ds(h, length, stride=heads), :] = query[i] + head_decay * through[i]
     copies += start_output(ds, db, dq_out, sems.at[1], half)
     for copy in copies:
         copy.wait()
@@ -223,73 +263,94 @@
     return first
 
 
-def fold_kernel(sizes, level, span, forward, rate_ref, *refs):
+def fold_kernel(sizes, level, shift, pieces, span, forward, rate_ref, *refs):
     group = sizes[level]
     top = level + 2 == len(sizes)
-    states = refs[:group]
-    parts = refs[group : group + 1] if top else refs[-sizes[level + 1] :]
-    if top:
-        parts = refs[-1:]
+    count = 1 if top else sizes[level + 1]
+    states, parts = refs[:group], refs[len(refs) - count * pieces :]
     heads = parts[0].shape[0]
-    first = first_head(sizes, level, rate_ref.shape[0], forward)
+    first = first_head(sizes, level, rate_ref.shape[0], forward) + shift
     place = place_at(sizes, level, forward)
     weigh = [group - 1 - (place ^ j) for j in range(group)]
-    for k in range(len(parts)):
-        start = 0 if top else (place_at(sizes, level + 1) ^ k) * heads
-        for i in range(heads):
-            rate = rate_ref[pl.ds(first + start + i, 1), :]
-            total = None
-            for j in range(group):
-                term = row_weight(rate, span, weigh[j]) * states[j][start + i].astype(F32)
-                total = term if total is None else total + term
-            parts[k][i] = total.astype(BF16)
-
-
-def spread_kernel(sizes, level, span, forward, rate_ref, *refs):
+    for k in range(count):
+        part = 0 if top else place_at(sizes, level + 1) ^ k
+        for g in range(pieces):
+            start = (part * pieces + g) * heads
+            for i in range(heads):
+                rate = rate_ref[pl.ds(first + start + i, 1), :]
+                total = None
+                for j in range(group):
+                    term = row_weight(rate, span, weigh[j]) * states[j][start + i].astype(F32)
+                    total = term if total is None else total + term
+                parts[g * count + k][i] = total.astype(BF16)
+
+
+def double_kernel(sizes, level, shift, step, span, forward, rate_ref, state_ref, other_ref, *rest):
+    out_ref = rest[-1]
+    first = first_head(sizes, level - 1, rate_ref.shape[0], forward) + shift
+    upper = (place_at(sizes, level, forward) // step) % 2
+    for i in range(out_ref.shape[0]):
+        rate = rate_ref[pl.ds(first + i, 1), :]
+        total = row_weight(rate, span * step, 1 - upper) * state_ref[i].astype(F32)
+        total = total + row_weight(rate, span * step, upper) * other_ref[i].astype(F32)
+        out_ref[i] = total.astype(BF16)
+
+
+def spread_kernel(sizes, level, shift, pieces, span, forward, rate_ref, *refs):
     group, next_group = sizes[level], sizes[level + 1]
     top = level + 2 == len(sizes)
-    ahead_count = next_group - 1 if top else next_group
-    states, ahead, outs = refs[:group], refs[group : group + ahead_count], refs[-group:]
+    count = 1 if top else next_group
+    ahead_count = next_group * pieces
+    if top:
+        ahead_count = next_group.bit_length() - 1 if DOUBLING else next_group - 1
+    states, ahead, outs = refs[:group], refs[group : group + ahead_count], refs[len(refs) - group :]
     heads = states[0].shape[0]
-    part_heads = heads if top else heads // next_group
-    first = first_head(sizes, level, rate_ref.shape[0], forward)
+    part_heads = heads if top else heads // (next_group * pieces)
+    first = first_head(sizes, level, rate_ref.shape[0], forward) + shift
     place = place_at(sizes, level, forward)
     top_place = place_at(sizes, level + 1, forward)
-    for k in range(1 if top else next_group):
-        start = 0 if top else (place_at(sizes, level + 1) ^ k) * part_heads
-        for i in range(part_heads):
-            rate = rate_ref[pl.ds(first + start + i, 1), :]
-            if top:
-                before = None
-                for j in range(1, next_group):
-                    weight = row_weight(rate, span * group, top_place - 1 - (top_place ^ j))
-                    term = weight * ahead[j - 1][i].astype(F32)
-                    before = term if before is None else before + term
-            else:
-                before = ahead[k][i].astype(F32)
-            own = [states[j][start + i].astype(F32) for j in range(group)]
-            for j in range(group):
-                total = row_weight(rate, span, place ^ j) * before
-                for q in range(group):
-                    if q != j:
-                        total = total + row_weight(rate, span, (place ^ j) - 1 - (place ^ q)) * own[q]
-                outs[j][start + i] = total.astype(BF16)
+    for k in range(count):
+        part = 0 if top else place_at(sizes, level + 1) ^ k
+        for g in range(pieces):
+            start = (part * pieces + g) * part_heads
+            for i in range(part_heads):
+                rate = rate_ref[pl.ds(first + start + i, 1), :]
+                if top:
+                    before = None
+                    for j in range(ahead_count):
+                        steps = top_place - 1 - (top_place ^ (j + 1))
+                        if DOUBLING:
+                            step = 1 << j
+                            steps = jnp.where((top_place // step) % 2 == 1, top_place % step, -1)
+                        term = row_weight(rate, span * group, steps) * ahead[j][i].astype(F32)
+                        before = term if before is None else before + term
+                else:
+                    before = ahead[g * count + k][i].astype(F32)
+                own = [states[j][start + i].astype(F32) for j in range(group)]
+                for j in range(group):
+                    total = row_weight(rate, span, place ^ j) * before
+                    for q in range(group):
+                        if q != j:
+                            total = total + row_weight(rate, span, (place ^ j) - 1 - (place ^ q)) * own[q]
+                    outs[j][start + i] = total.astype(BF16)
 
 
 WHOLE = pl.BlockSpec(memory_space=pltpu.VMEM)
 ANYWHERE = pl.BlockSpec(memory_space=pl.ANY)
-
-
-def call(body, inputs, outputs, scratch=(), anywhere=(), out_anywhere=(), aliases=None, flops=0, name=None):
+OUTSIDE = pl.BlockSpec(memory_space=pltpu.HBM)
+
+
+def call(body, inputs, outputs, scratch=(), anywhere=(), outside=(), out_outside=(), aliases=None, flops=0, name=None, limit=VMEM_LIMIT, count_bytes=True):
     nbytes = sum(a.size * a.dtype.itemsize for a in inputs) + sum(s.size * s.dtype.itemsize for s in outputs)
+    nbytes = nbytes if count_bytes else 0
     return pl.pallas_call(
         body,
-        in_specs=[ANYWHERE if n in anywhere else WHOLE for n in range(len(inputs))],
-        out_specs=[ANYWHERE if n in out_anywhere else WHOLE for n in range(len(outputs))],
+        in_specs=[ANYWHERE if n in anywhere else OUTSIDE if n in outside else WHOLE for n in range(len(inputs))],
+        out_specs=[OUTSIDE if n in out_outside else WHOLE for n in range(len(outputs))],
         scratch_shapes=list(scratch),
         out_shape=list(outputs),
         input_output_aliases=aliases or {},
-        compiler_params=pltpu.CompilerParams(vmem_limit_bytes=VMEM_LIMIT),
+        compiler_params=pltpu.CompilerParams(vmem_limit_bytes=limit),
         cost_estimate=pl.CostEstimate(flops=flops, bytes_accessed=nbytes, transcendentals=0),
         name=name,
     )(*inputs)
@@ -311,32 +372,58 @@
 def carry_states(kept, sent, devices, rates, length, forward, beside):
     sizes = level_sizes(devices)
     state = kept.shape[1:]
-
-    def climb(level, low, parts):
+    left = kept.shape[0]
+    for size in sizes[1:-1]:
+        left //= size
+    pieces = min(PIECES, left) if len(sizes) > 2 else 1
+
+    def climb(level, low, parts, shift, piece):
         group, next_group = sizes[level], sizes[level + 1]
         top = level + 2 == len(sizes)
+        cut = pieces if level == 0 else 1
         span = float(length * low)
         states = [parts[0]] + [swap(parts[k], k * low, devices) for k in range(1, group)]
         heads = parts[0].shape[0]
         count = 1 if top else next_group
-        part_heads = heads if top else heads // next_group
-        extra = list(beside[0]) if level == 1 else []
+        part_heads = heads if top else heads // (next_group * cut)
+        extra = list(beside.get(("fold", piece), ())) if level == 1 else []
         inputs = [rates] + states + extra
         folded = call(
-            functools.partial(fold_kernel, sizes, level, span, forward),
+            functools.partial(fold_kernel, sizes, level, shift, cut, span, forward),
             inputs,
-            [jax.ShapeDtypeStruct((part_heads,) + state, BF16)] * count,
+            [jax.ShapeDtypeStruct((part_heads,) + state, BF16)] * (count * cut),
             anywhere=range(1 + group, len(inputs)),
             name="fold_states",
         )
-        if top:
+        if top and not DOUBLING:
             ahead = [swap(folded[0], k * low * group, devices) for k in range(1, next_group)]
+        elif top:
+            total, ahead, step = folded[0], [], 1
+            while step < next_group:
+                if step > 1:
+                    extra = list(beside.get(("double", piece), ()))
+                    inputs = [rates, total, ahead[-1]] + extra
+                    (total,) = call(
+                        functools.partial(
+                            double_kernel, sizes, level + 1, shift, step // 2, span * group, forward
+                        ),
+                        inputs,
+                        [jax.ShapeDtypeStruct((part_heads,) + state, BF16)],
+                        anywhere=range(3, len(inputs)),
+                        name="double_states",
+                    )
+                ahead.append(swap(total, step * low * group, devices))
+                step *= 2
         else:
-            ahead = climb(level + 1, low * group, folded)
-        extra = list(beside[1]) if level == 1 else []
+            ahead = []
+            for g in range(cut):
+                ahead += climb(
+                    level + 1, low * group, folded[g * count : (g + 1) * count], shift + g * part_heads, g
+                )
+        extra = list(beside.get(("spread", piece if level else -1), ())) if level < 2 else []
         inputs = [rates] + states + ahead + extra
         outs = call(
-            functools.partial(spread_kernel, sizes, level, span, forward),
+            functools.partial(spread_kernel, sizes, level, shift, cut, span, forward),
             inputs,
             [jax.ShapeDtypeStruct((heads,) + state, BF16)] * group,
             anywhere=range(1 + group + len(ahead), len(inputs)),
@@ -344,13 +431,12 @@
         )
         return [outs[0]] + [swap(outs[k], k * low, devices) for k in range(1, group)]
 
-    return climb(0, 1, [kept, sent])
+    return climb(0, 1, [kept, sent], 0, 0)
 
 
 def local(devices, queries, key_vectors, value_vectors, output_grad, decay_rate, norm_gain):
     length, heads, size = queries.shape
     half = heads // 2
-    rates = jnp.broadcast_to(decay_rate[:, None], (heads, size))
 
     def shaped(*shape, dtype=BF16):
         return jax.ShapeDtypeStruct(shape, dtype)
@@ -364,17 +450,29 @@
     sems = pltpu.SemaphoreType.DMA((2, CHUNKS))
     unit = 2 * half * length * size * size
 
-    keys, values, local_states = [None, None], [None, None], [None, None]
-    for s in (1, 0):
-        keys[s], values[s], local_states[s] = call(
-            functools.partial(local_kernel, s == 0),
-            [key_vectors, value_vectors, rates],
-            [per_head, per_head, states],
-            [stage, stage, flat, flat, sems],
-            anywhere=(0, 1),
-            flops=unit,
-            name="local_states",
-        )
+    rate_rows = shaped(heads, size, dtype=F32)
+    block = shaped(length, half, size)
+    copy_sem = pltpu.SemaphoreType.DMA
+    sent_key, sent_value, sent_state, key_rest, value_rest, rates = call(
+        first_local_kernel,
+        [key_vectors, value_vectors, decay_rate],
+        [per_head, per_head, states, block, block, rate_rows],
+        [stage, stage, flat, flat, pltpu.SMEM((heads,), F32), sems, copy_sem((2,)), copy_sem],
+        outside=(0, 1, 2),
+        limit=LOCAL_LIMIT,
+        count_bytes=False,
+        flops=unit,
+        name="local_states",
+    )
+    kept_key, kept_value, kept_state = call(
+        second_local_kernel,
+        [key_rest, value_rest, rates],
+        [per_head, per_head, states],
+        [flat, flat],
+        flops=unit,
+        name="local_states",
+    )
+    keys, values = [kept_key, sent_key], [kept_value, sent_value]
     query, grad, attention, inner = [None, None], [None, None], [None, None], [None, None]
     for s in (0, 1):
         query[s], grad[s], attention[s], inner[s] = call(
@@ -386,7 +484,7 @@
             name="attention",
         )
     incoming = carry_states(
-        local_states[0], local_states[1], devices, rates, length, True, [inner[:1], inner[1:]]
+        kept_state, sent_state, devices, rates, length, True, {("fold", 0): inner[:1], ("spread", 0): inner[1:]}
     )
     normed, grad_out, state_grad = [None, None], [None, None], [None, None]
     for s in (0, 1):
@@ -397,27 +495,38 @@
             flops=2 * unit,
             name="norm",
         )
-    normed_out, query_out, key_part, value_part = None, None, [None, None], [None, None]
+    normed_out, query_out = None, None
+    scores, key_part, value_part, marks = [None, None], [None, None], [None, None], []
     for s in (0, 1):
-        inputs = [query[s], keys[s], values[s], attention[s], grad_out[s], incoming[s], normed[s], rates]
+        scores[s], key_part[s], value_part[s] = call(
+            functools.partial(inner_kernel, s == 0),
+            [query[s], values[s], attention[s], grad_out[s], rates],
+            [shaped(half, length, length), per_head_wide, per_head_wide],
+            flops=3 * unit,
+            name="inner_gradients",
+        )
+        inputs = [keys[s], scores[s], grad_out[s], incoming[s], normed[s], rates]
         count = len(inputs)
         aliases = {}
         if s:
             aliases = {count: 0, count + 1: 1}
             inputs += [normed_out, query_out]
-        normed_out, query_out, key_part[s], value_part[s] = call(
-            functools.partial(grad_kernel, s == 0),
+        normed_out, query_out, mark = call(
+            functools.partial(query_kernel, s == 0),
             inputs,
-            [whole, whole, per_head_wide, per_head_wide],
+            [whole, whole, shaped(8, size, dtype=F32)],
             [flat, flat, stage, stage, sems],
-            anywhere=(count, count + 1),
-            out_anywhere=(0, 1),
+            outside=(count, count + 1),
+            out_outside=(0, 1),
             aliases=aliases,
-            flops=5 * unit,
-            name="stretch_gradients",
-        )
+            flops=2 * unit,
+            name="query_gradient",
+        )
+        marks += [key_part[s], mark]
     later = carry_states(
-        state_grad[1], state_grad[0], devices, rates, length, False, [key_part[:1], key_part[1:]]
+        state_grad[1], state_grad[0], devices, rates, length, False,
+        {("fold", 0): marks[:1] + marks[2:3], ("spread", 0): marks[1:2], ("spread", -1): marks[3:]},
+
     )
     key_out, value_out = None, None
     for s in (1, 0):
@@ -432,8 +541,8 @@
             inputs,
             [whole, whole],
             [flat, flat, stage, stage, sems],
-            anywhere=(count, count + 1),
-            out_anywhere=(0, 1),
+            outside=(count, count + 1),
+            out_outside=(0, 1),
             aliases=aliases,
             flops=2 * unit,
             name="later_gradients",

time: 83.1 us -> 78.9 us (0.949)
  local copies, waits for them, and re-layouts: 3.28 us -> 0.74 us
  starting transfers between devices: 25.2 us -> 23.4 us
    unnamed x12 -> x8, local copies, waits for them, and re-layouts: 2.55 us -> 0.74 us
    ppermute x22 -> x20, starting transfers between devices: 25.2 us -> 23.4 us  [swap(): lax.ppermute(array, AXES, [(i, i ^ distance) for i in range(devices)])]
    ppermute x22 -> x20, waiting for transfers between devices: 31.4 us -> 31.6 us  [swap(): lax.ppermute(array, AXES, [(i, i ^ distance) for i in range(devices)])]
    pallas_call x18 -> x22, Pallas kernels: 22 us -> 21.8 us  [call(): pl.pallas_call(body, in_specs=[ANYWHERE if n in anywhere else OUTSIDE if...]
  transfers between devices with their start and end apart: 22 -> 20, of which waited for: 13 -> 15; matrix products, arithmetic and copies ran while one was open for 0% -> 0% of each run, Pallas kernels for 19% -> 18%
where the time goes in v3:
time: 78.9 us; the launch traced here: 78.5 us
  waiting for transfers between devices  31.6 us (40%)
  starting transfers between devices  23.4 us (30%)
  Pallas kernels  21.8 us (28%)
  between operations  0.97 us (1%)
    ppermute x20, waiting for transfers between devices, swap(): lax.ppermute(array, AXES, [(i, i ^ distance) for i in range(devices)])  31.6 us
    ppermute x20, starting transfers between devices, swap(): lax.ppermute(array, AXES, [(i, i ^ distance) for i in range(devices)])  23.4 us
    pallas_call x22, Pallas kernels, call(): pl.pallas_call(body, in_specs=[ANYWHERE if n in anywhere else OUTSIDE if...  21.8 us
  transfers between devices with their start and end apart: 20, of which 15 were waited for; matrix products, arithmetic and copies ran while one was open for 0% of the time, Pallas kernels for 18%

profile of v3, /device:TPU:0, one launch (start us, length us, event | category | flops | bytes accessed | tf_op | source)
XLA Modules:
  0.0 78.5 jit_solution(4108135029536273014)
XLA Ops:
  1.3 2.4 %local_states.2 = (bf16[16,128,128]{2,1,0:T(8,128)(2,1)S(1)}, bf16[16,128,128]{2,1,0:T(8,128)(2,1)S(1)}, bf16[16,128,128]{2,1,0:T(8,128)(2,1)S(1)}, bf16[128,16,...) custom-call(bf16[128,32,128]{2,1,0:T(8,128)(2,1)} %k_ref.1, ...), custom_call_target="tpu_custom_call" | custom-call | flops 67108864 | tf_op jit(solution)/shard_map/local_states/pallas_call | solution.py:346
  6.1 2.9 %collective-permute-start.1 = (bf16[4,128,128]{2,1,0:T(8,128)(2,1)S(1)}, bf16[4,128,128]{2,1,0:T(8,128)(2,1)S(1)}, u32[]{:S(2)}, u32[]{:S(2)}) collective-permute-start(bf16[4,128,128]{2,1,0:T(8,128)(2,1)S(1)} %get-tuple-element.75), channel_id=1, source_target_pairs={{0,2},{1,3},{2,0},{3,1},{4,6},{5,7},{6,4},{7,5},{8,10},{9,11},{10,... | collective-permute-start | bytes 393224 | tf_op jit(solution)/shard_map/ppermute | solution.py:369
  9.0 1.5 %collective-permute-start.2 = (bf16[4,128,128]{2,1,0:T(8,128)(2,1)S(1)}, bf16[4,128,128]{2,1,0:T(8,128)(2,1)S(1)}, u32[]{:S(2)}, u32[]{:S(2)}) collective-permute-start(bf16[4,128,128]{2,1,0:T(8,128)(2,1)S(1)} %get-tuple-element.76), channel_id=1, source_target_pairs={{0,4},{1,5},{2,6},{3,7},{4,0},{5,1},{6,2},{7,3},{8,12},{9,13},{10,... | collective-permute-start | bytes 393224 | tf_op jit(solution)/shard_map/ppermute | solution.py:369
  12.9 4.2 %collective-permute-done.2.refs_2_ = bf16[4,128,128]{2,1,0:T(8,128)(2,1)S(1)} collective-permute-done((bf16[4,128,128]{2,1,0:T(8,128)(2,1)S(1)}, bf16[4,128,128]{2,1,0:T(8,128)(2,1)S(1)}, u32[]{:S(2)}, u32[]{:S(2)}) %collective-permute-start.2) | collective-permute-done | bytes 131104 | tf_op jit(solution)/shard_map/ppermute | solution.py:369
  17.2 1.6 %collective-permute-start.4 = (bf16[4,128,128]{2,1,0:T(8,128)(2,1)S(1)}, bf16[4,128,128]{2,1,0:T(8,128)(2,1)S(1)}, u32[]{:S(2)}, u32[]{:S(2)}) collective-permute-start(bf16[4,128,128]{2,1,0:T(8,128)(2,1)S(1)} %fold_states.5.state_ref), channel_id=1, source_target_pairs={{0,8},{1,9},{2,10},{3,11},{4,12},{5,13},{6,14},{7,15},{8,0},{9,1},... | collective-permute-start | bytes 393224 | tf_op jit(solution)/shard_map/ppermute | solution.py:369
  18.8 3.4 %collective-permute-done.4.other_ref.refs_4_ = bf16[4,128,128]{2,1,0:T(8,128)(2,1)S(1)} collective-permute-done((bf16[4,128,128]{2,1,0:T(8,128)(2,1)S(1)}, bf16[4,128,128]{2,1,0:T(8,128)(2,1)S(1)}, u32[]{:S(2)}, u32[]{:S(2)}) %collective-permute-start.4) | collective-permute-done | bytes 131104 | tf_op jit(solution)/shard_map/ppermute | solution.py:369
  22.3 2.7 %collective-permute-start.5 = (bf16[4,128,128]{2,1,0:T(8,128)(2,1)S(1)}, bf16[4,128,128]{2,1,0:T(8,128)(2,1)S(1)}, u32[]{:S(2)}, u32[]{:S(2)}) collective-permute-start(bf16[4,128,128]{2,1,0:T(8,128)(2,1)S(1)} %double_states.2), channel_id=1, source_target_pairs={{0,16},{1,17},{2,18},{3,19},{4,20},{5,21},{6,22},{7,23},{8,24},{9,... | collective-permute-start | bytes 393224 | tf_op jit(solution)/shard_map/ppermute | solution.py:369
  26.2 3.5 %collective-permute-done.5.refs_5_ = bf16[4,128,128]{2,1,0:T(8,128)(2,1)S(1)} collective-permute-done((bf16[4,128,128]{2,1,0:T(8,128)(2,1)S(1)}, bf16[4,128,128]{2,1,0:T(8,128)(2,1)S(1)}, u32[]{:S(2)}, u32[]{:S(2)}) %collective-permute-start.5) | collective-permute-done | bytes 131104 | tf_op jit(solution)/shard_map/ppermute | solution.py:369
  30.1 1.3 %collective-permute-start.6 = (bf16[4,128,128]{2,1,0:T(8,128)(2,1)S(1)}, bf16[4,128,128]{2,1,0:T(8,128)(2,1)S(1)}, u32[]{:S(2)}, u32[]{:S(2)}) collective-permute-start(bf16[4,128,128]{2,1,0:T(8,128)(2,1)S(1)} %get-tuple-element.82), channel_id=1, source_target_pairs={{0,2},{1,3},{2,0},{3,1},{4,6},{5,7},{6,4},{7,5},{8,10},{9,11},{10,... | collective-permute-start | bytes 393224 | tf_op jit(solution)/shard_map/ppermute | solution.py:369
  32.2 1.4 %collective-permute-start.8 = (bf16[4,128,128]{2,1,0:T(8,128)(2,1)S(1)}, bf16[4,128,128]{2,1,0:T(8,128)(2,1)S(1)}, u32[]{:S(2)}, u32[]{:S(2)}) collective-permute-start(bf16[4,128,128]{2,1,0:T(8,128)(2,1)S(1)} %get-tuple-element.84), channel_id=1, source_target_pairs={{0,6},{1,7},{2,4},{3,5},{4,2},{5,3},{6,0},{7,1},{8,14},{9,15},{10,... | collective-permute-start | bytes 393224 | tf_op jit(solution)/shard_map/ppermute | solution.py:369
  33.7 1.5 %collective-permute-done.6.refs_3_ = bf16[4,128,128]{2,1,0:T(8,128)(2,1)S(1)} collective-permute-done((bf16[4,128,128]{2,1,0:T(8,128)(2,1)S(1)}, bf16[4,128,128]{2,1,0:T(8,128)(2,1)S(1)}, u32[]{:S(2)}, u32[]{:S(2)}) %collective-permute-start.6) | collective-permute-done | bytes 131104 | tf_op jit(solution)/shard_map/ppermute | solution.py:369
  36.4 1.7 %collective-permute-done.8.refs_5_ = bf16[4,128,128]{2,1,0:T(8,128)(2,1)S(1)} collective-permute-done((bf16[4,128,128]{2,1,0:T(8,128)(2,1)S(1)}, bf16[4,128,128]{2,1,0:T(8,128)(2,1)S(1)}, u32[]{:S(2)}, u32[]{:S(2)}) %collective-permute-start.8) | collective-permute-done | bytes 131104 | tf_op jit(solution)/shard_map/ppermute | solution.py:369
  42.3 1.6 %collective-permute-start.11 = (bf16[4,128,128]{2,1,0:T(8,128)(2,1)S(1)}, bf16[4,128,128]{2,1,0:T(8,128)(2,1)S(1)}, u32[]{:S(2)}, u32[]{:S(2)}) collective-permute-start(bf16[4,128,128]{2,1,0:T(8,128)(2,1)S(1)} %get-tuple-element.103), channel_id=1, source_target_pairs={{0,2},{1,3},{2,0},{3,1},{4,6},{5,7},{6,4},{7,5},{8,10},{9,11},{10,... | collective-permute-start | bytes 393224 | tf_op jit(solution)/shard_map/ppermute | solution.py:369
  44.4 1.5 %collective-permute-start.13 = (bf16[4,128,128]{2,1,0:T(8,128)(2,1)S(1)}, bf16[4,128,128]{2,1,0:T(8,128)(2,1)S(1)}, u32[]{:S(2)}, u32[]{:S(2)}) collective-permute-start(bf16[4,128,128]{2,1,0:T(8,128)(2,1)S(1)} %get-tuple-element.105), channel_id=1, source_target_pairs={{0,6},{1,7},{2,4},{3,5},{4,2},{5,3},{6,0},{7,1},{8,14},{9,15},{10,... | collective-permute-start | bytes 393224 | tf_op jit(solution)/shard_map/ppermute | solution.py:369
  48.5 3.7 %collective-permute-done.12.refs_2_ = bf16[4,128,128]{2,1,0:T(8,128)(2,1)S(1)} collective-permute-done((bf16[4,128,128]{2,1,0:T(8,128)(2,1)S(1)}, bf16[4,128,128]{2,1,0:T(8,128)(2,1)S(1)}, u32[]{:S(2)}, u32[]{:S(2)}) %collective-permute-start.12) | collective-permute-done | bytes 131104 | tf_op jit(solution)/shard_map/ppermute | solution.py:369
  53.0 4.3 %collective-permute-done.14.other_ref.refs_4_ = bf16[4,128,128]{2,1,0:T(8,128)(2,1)S(1)} collective-permute-done((bf16[4,128,128]{2,1,0:T(8,128)(2,1)S(1)}, bf16[4,128,128]{2,1,0:T(8,128)(2,1)S(1)}, u32[]{:S(2)}, u32[]{:S(2)}) %collective-permute-start.14) | collective-permute-done | bytes 131104 | tf_op jit(solution)/shard_map/ppermute | solution.py:369
  57.4 2.1 %collective-permute-start.15 = (bf16[4,128,128]{2,1,0:T(8,128)(2,1)S(1)}, bf16[4,128,128]{2,1,0:T(8,128)(2,1)S(1)}, u32[]{:S(2)}, u32[]{:S(2)}) collective-permute-start(bf16[4,128,128]{2,1,0:T(8,128)(2,1)S(1)} %double_states.3), channel_id=1, source_target_pairs={{0,16},{1,17},{2,18},{3,19},{4,20},{5,21},{6,22},{7,23},{8,24},{9,... | collective-permute-start | bytes 393224 | tf_op jit(solution)/shard_map/ppermute | solution.py:369
  59.5 2.5 %query_gradient.2 = (bf16[128,32,128]{2,1,0:T(8,128)(2,1)}, bf16[128,32,128]{2,1,0:T(8,128)(2,1)}, f32[8,128]{1,0:T(8,128)S(1)}) custom-call(bf16[16,128,128]{2,1,0:T(8,128)(2,1)S(1)} %get-tuple-element.78.kt_ref, bf16[16,128,128]{2,1,0:T(8,128)(2,1)S(1)} %get-tuple-element.94.gs_ref, bf16[16,128,128]{2,1,0:T(8,128)(2,1)S(1)} %get-tuple-element.93.go_ref, ...), custom_call_target="tpu_custom_call" | custom-call | flops 134217728 | bytes 4739072 | tf_op jit(solution)/shard_map/query_gradient/pallas_call | solution.py:346
  62.1 2.7 %collective-permute-done.15.refs_5_ = bf16[4,128,128]{2,1,0:T(8,128)(2,1)S(1)} collective-permute-done((bf16[4,128,128]{2,1,0:T(8,128)(2,1)S(1)}, bf16[4,128,128]{2,1,0:T(8,128)(2,1)S(1)}, u32[]{:S(2)}, u32[]{:S(2)}) %collective-permute-start.15) | collective-permute-done | bytes 131104 | tf_op jit(solution)/shard_map/ppermute | solution.py:369
  65.8 1.7 %collective-permute-start.17 = (bf16[4,128,128]{2,1,0:T(8,128)(2,1)S(1)}, bf16[4,128,128]{2,1,0:T(8,128)(2,1)S(1)}, u32[]{:S(2)}, u32[]{:S(2)}) collective-permute-start(bf16[4,128,128]{2,1,0:T(8,128)(2,1)S(1)} %get-tuple-element.111), channel_id=1, source_target_pairs={{0,4},{1,5},{2,6},{3,7},{4,0},{5,1},{6,2},{7,3},{8,12},{9,13},{10,... | collective-permute-start | bytes 393224 | tf_op jit(solution)/shard_map/ppermute | solution.py:369
  68.8 2.4 %query_gradient.3 = (bf16[128,32,128]{2,1,0:T(8,128)(2,1)}, bf16[128,32,128]{2,1,0:T(8,128)(2,1)}, f32[8,128]{1,0:T(8,128)S(1)}) custom-call(bf16[16,128,128]{2,1,0:T(8,128)(2,1)S(1)} %get-tuple-element.63.kt_ref, bf16[16,128,128]{2,1,0:T(8,128)(2,1)S(1)} %get-tuple-element.87.gs_ref, ...), custom_call_target="tpu_custom_call", output_to_operand_aliasing={{0}: (6, {}), {1}: (7, {})} | custom-call | flops 134217728 | bytes 6836224 | tf_op jit(solution)/shard_map/query_gradient/pallas_call | solution.py:346
  71.2 2.4 %collective-permute-done.17.refs_4_ = bf16[4,128,128]{2,1,0:T(8,128)(2,1)S(1)} collective-permute-done((bf16[4,128,128]{2,1,0:T(8,128)(2,1)S(1)}, bf16[4,128,128]{2,1,0:T(8,128)(2,1)S(1)}, u32[]{:S(2)}, u32[]{:S(2)}) %collective-permute-start.17) | collective-permute-done | bytes 131104 | tf_op jit(solution)/shard_map/ppermute | solution.py:369
  74.2 2.1 %later_gradients.2 = (bf16[128,32,128]{2,1,0:T(8,128)(2,1)}, bf16[128,32,128]{2,1,0:T(8,128)(2,1)}) custom-call(bf16[16,128,128]{2,1,0:T(8,128)(2,1)S(1)} %get-tuple-element.63.kt_ref, bf16[16,128,128]{2,1,0:T(8,128)(2,1)S(1)} %get-tuple-element.64.vt_ref, bf16[16,128,128]{2,1,0:T(8,128)(2,1)S(1)} %get-tuple-element.116.later_ref, ...), custom_call_target="tpu_custom_call" | custom-call | flops 134217728 | bytes 5783552 | tf_op jit(solution)/shard_map/later_gradients/pallas_call | solution.py:346
  76.3 2.1 %later_gradients.3 = (bf16[128,32,128]{2,1,0:T(8,128)(2,1)}, bf16[128,32,128]{2,1,0:T(8,128)(2,1)}) custom-call(bf16[16,128,128]{2,1,0:T(8,128)(2,1)S(1)} %get-tuple-element.78.kt_ref, bf16[16,128,128]{2,1,0:T(8,128)(2,1)S(1)} %get-tuple-element.79.vt_ref, ...), custom_call_target="tpu_custom_call", output_to_operand_aliasing={{0}: (6, {}), {1}: (7, {})} | custom-call | flops 134217728 | bytes 7880704 | tf_op jit(solution)/shard_map/later_gradients/pallas_call | solution.py:346
  (46 shorter events, 20.5 us)
Async XLA Ops:
  0.6 0.7 copy-start.3
  3.7 2.1 %collective-permute-start = (bf16[16,128,128]{2,1,0:T(8,128)(2,1)S(1)}, bf16[16,128,128]{2,1,0:T(8,128)(2,1)S(1)}, u32[]{:S(2)}, u32[]{:S(2)}) collective-permute-start(bf16[16,128,128]{2,1,0:T(8,128)(2,1)S(1)} %get-tuple-element.73), channel_id=1, source_target_pairs={{0,1},{1,0},{2,3},{3,2},{4,5},{5,4},{6,7},{7,6},{8,9},{9,8},{10,11... | collective-permute-start | bytes 1572872 | tf_op jit(solution)/shard_map/ppermute | solution.py:369
  4.3 6.3 %copy-start = (bf16[128,32,128]{2,1,0:T(8,128)(2,1)S(1)}, bf16[128,32,128]{2,1,0:T(8,128)(2,1)}, u32[]{:S(2)}) copy-start(bf16[128,32,128]{2,1,0:T(8,128)(2,1)} %q_ref.3) | copy-start | bytes 3145732
  4.3 6.3 %copy-start.1 = (bf16[128,32,128]{2,1,0:T(8,128)(2,1)S(1)}, bf16[128,32,128]{2,1,0:T(8,128)(2,1)}, u32[]{:S(2)}) copy-start(bf16[128,32,128]{2,1,0:T(8,128)(2,1)} %g_ref.3) | copy-start | bytes 3145732
  6.1 6.8 %collective-permute-start.1 = (bf16[4,128,128]{2,1,0:T(8,128)(2,1)S(1)}, bf16[4,128,128]{2,1,0:T(8,128)(2,1)S(1)}, u32[]{:S(2)}, u32[]{:S(2)}) collective-permute-start(bf16[4,128,128]{2,1,0:T(8,128)(2,1)S(1)} %get-tuple-element.75), channel_id=1, source_target_pairs={{0,2},{1,3},{2,0},{3,1},{4,6},{5,7},{6,4},{7,5},{8,10},{9,11},{10,... | collective-permute-start | bytes 393224 | tf_op jit(solution)/shard_map/ppermute | solution.py:369
  9.0 8.1 %collective-permute-start.2 = (bf16[4,128,128]{2,1,0:T(8,128)(2,1)S(1)}, bf16[4,128,128]{2,1,0:T(8,128)(2,1)S(1)}, u32[]{:S(2)}, u32[]{:S(2)}) collective-permute-start(bf16[4,128,128]{2,1,0:T(8,128)(2,1)S(1)} %get-tuple-element.76), channel_id=1, source_target_pairs={{0,4},{1,5},{2,6},{3,7},{4,0},{5,1},{6,2},{7,3},{8,12},{9,13},{10,... | collective-permute-start | bytes 393224 | tf_op jit(solution)/shard_map/ppermute | solution.py:369
  10.5 6.6 %collective-permute-start.3 = (bf16[4,128,128]{2,1,0:T(8,128)(2,1)S(1)}, bf16[4,128,128]{2,1,0:T(8,128)(2,1)S(1)}, u32[]{:S(2)}, u32[]{:S(2)}) collective-permute-start(bf16[4,128,128]{2,1,0:T(8,128)(2,1)S(1)} %get-tuple-element.77), channel_id=1, source_target_pairs={{0,6},{1,7},{2,4},{3,5},{4,2},{5,3},{6,0},{7,1},{8,14},{9,15},{10,... | collective-permute-start | bytes 393224 | tf_op jit(solution)/shard_map/ppermute | solution.py:369
  17.2 5.0 %collective-permute-start.4 = (bf16[4,128,128]{2,1,0:T(8,128)(2,1)S(1)}, bf16[4,128,128]{2,1,0:T(8,128)(2,1)S(1)}, u32[]{:S(2)}, u32[]{:S(2)}) collective-permute-start(bf16[4,128,128]{2,1,0:T(8,128)(2,1)S(1)} %fold_states.5.state_ref), channel_id=1, source_target_pairs={{0,8},{1,9},{2,10},{3,11},{4,12},{5,13},{6,14},{7,15},{8,0},{9,1},... | collective-permute-start | bytes 393224 | tf_op jit(solution)/shard_map/ppermute | solution.py:369
  22.3 7.3 %collective-permute-start.5 = (bf16[4,128,128]{2,1,0:T(8,128)(2,1)S(1)}, bf16[4,128,128]{2,1,0:T(8,128)(2,1)S(1)}, u32[]{:S(2)}, u32[]{:S(2)}) collective-permute-start(bf16[4,128,128]{2,1,0:T(8,128)(2,1)S(1)} %double_states.2), channel_id=1, source_target_pairs={{0,16},{1,17},{2,18},{3,19},{4,20},{5,21},{6,22},{7,23},{8,24},{9,... | collective-permute-start | bytes 393224 | tf_op jit(solution)/shard_map/ppermute | solution.py:369
  30.1 5.0 %collective-permute-start.6 = (bf16[4,128,128]{2,1,0:T(8,128)(2,1)S(1)}, bf16[4,128,128]{2,1,0:T(8,128)(2,1)S(1)}, u32[]{:S(2)}, u32[]{:S(2)}) collective-permute-start(bf16[4,128,128]{2,1,0:T(8,128)(2,1)S(1)} %get-tuple-element.82), channel_id=1, source_target_pairs={{0,2},{1,3},{2,0},{3,1},{4,6},{5,7},{6,4},{7,5},{8,10},{9,11},{10,... | collective-permute-start | bytes 393224 | tf_op jit(solution)/shard_map/ppermute | solution.py:369
  31.4 5.0 %collective-permute-start.7 = (bf16[4,128,128]{2,1,0:T(8,128)(2,1)S(1)}, bf16[4,128,128]{2,1,0:T(8,128)(2,1)S(1)}, u32[]{:S(2)}, u32[]{:S(2)}) collective-permute-start(bf16[4,128,128]{2,1,0:T(8,128)(2,1)S(1)} %get-tuple-element.83), channel_id=1, source_target_pairs={{0,4},{1,5},{2,6},{3,7},{4,0},{5,1},{6,2},{7,3},{8,12},{9,13},{10,... | collective-permute-start | bytes 393224 | tf_op jit(solution)/shard_map/ppermute | solution.py:369
  32.2 5.9 %collective-permute-start.8 = (bf16[4,128,128]{2,1,0:T(8,128)(2,1)S(1)}, bf16[4,128,128]{2,1,0:T(8,128)(2,1)S(1)}, u32[]{:S(2)}, u32[]{:S(2)}) collective-permute-start(bf16[4,128,128]{2,1,0:T(8,128)(2,1)S(1)} %get-tuple-element.84), channel_id=1, source_target_pairs={{0,6},{1,7},{2,4},{3,5},{4,2},{5,3},{6,0},{7,1},{8,14},{9,15},{10,... | collective-permute-start | bytes 393224 | tf_op jit(solution)/shard_map/ppermute | solution.py:369
  38.1 0.7 copy-start.2
  38.6 2.0 %collective-permute-start.9 = (bf16[16,128,128]{2,1,0:T(8,128)(2,1)S(1)}, bf16[16,128,128]{2,1,0:T(8,128)(2,1)S(1)}, u32[]{:S(2)}, u32[]{:S(2)}) collective-permute-start(bf16[16,128,128]{2,1,0:T(8,128)(2,1)S(1)} %get-tuple-element.85), channel_id=1, source_target_pairs={{0,1},{1,0},{2,3},{3,2},{4,5},{5,4},{6,7},{7,6},{8,9},{9,8},{10,11... | collective-permute-start | bytes 1572872 | tf_op jit(solution)/shard_map/ppermute | solution.py:369
  40.0 2.0 %collective-permute-start.10 = (bf16[16,128,128]{2,1,0:T(8,128)(2,1)S(1)}, bf16[16,128,128]{2,1,0:T(8,128)(2,1)S(1)}, u32[]{:S(2)}, u32[]{:S(2)}) collective-permute-start(bf16[16,128,128]{2,1,0:T(8,128)(2,1)S(1)} %get-tuple-element.101), channel_id=1, source_target_pairs={{0,1},{1,0},{2,3},{3,2},{4,5},{5,4},{6,7},{7,6},{8,9},{9,8},{10,11... | collective-permute-start | bytes 1572872 | tf_op jit(solution)/shard_map/ppermute | solution.py:369
  42.3 6.2 %collective-permute-start.11 = (bf16[4,128,128]{2,1,0:T(8,128)(2,1)S(1)}, bf16[4,128,128]{2,1,0:T(8,128)(2,1)S(1)}, u32[]{:S(2)}, u32[]{:S(2)}) collective-permute-start(bf16[4,128,128]{2,1,0:T(8,128)(2,1)S(1)} %get-tuple-element.103), channel_id=1, source_target_pairs={{0,2},{1,3},{2,0},{3,1},{4,6},{5,7},{6,4},{7,5},{8,10},{9,11},{10,... | collective-permute-start | bytes 393224 | tf_op jit(solution)/shard_map/ppermute | solution.py:369
  43.9 8.3 %collective-permute-start.12 = (bf16[4,128,128]{2,1,0:T(8,128)(2,1)S(1)}, bf16[4,128,128]{2,1,0:T(8,128)(2,1)S(1)}, u32[]{:S(2)}, u32[]{:S(2)}) collective-permute-start(bf16[4,128,128]{2,1,0:T(8,128)(2,1)S(1)} %get-tuple-element.104), channel_id=1, source_target_pairs={{0,4},{1,5},{2,6},{3,7},{4,0},{5,1},{6,2},{7,3},{8,12},{9,13},{10,... | collective-permute-start | bytes 393224 | tf_op jit(solution)/shard_map/ppermute | solution.py:369
  44.4 7.8 %collective-permute-start.13 = (bf16[4,128,128]{2,1,0:T(8,128)(2,1)S(1)}, bf16[4,128,128]{2,1,0:T(8,128)(2,1)S(1)}, u32[]{:S(2)}, u32[]{:S(2)}) collective-permute-start(bf16[4,128,128]{2,1,0:T(8,128)(2,1)S(1)} %get-tuple-element.105), channel_id=1, source_target_pairs={{0,6},{1,7},{2,4},{3,5},{4,2},{5,3},{6,0},{7,1},{8,14},{9,15},{10,... | collective-permute-start | bytes 393224 | tf_op jit(solution)/shard_map/ppermute | solution.py:369
  52.3 5.0 %collective-permute-start.14 = (bf16[4,128,128]{2,1,0:T(8,128)(2,1)S(1)}, bf16[4,128,128]{2,1,0:T(8,128)(2,1)S(1)}, u32[]{:S(2)}, u32[]{:S(2)}) collective-permute-start(bf16[4,128,128]{2,1,0:T(8,128)(2,1)S(1)} %fold_states.7.state_ref), channel_id=1, source_target_pairs={{0,8},{1,9},{2,10},{3,11},{4,12},{5,13},{6,14},{7,15},{8,0},{9,1},... | collective-permute-start | bytes 393224 | tf_op jit(solution)/shard_map/ppermute | solution.py:369
  57.4 7.3 %collective-permute-start.15 = (bf16[4,128,128]{2,1,0:T(8,128)(2,1)S(1)}, bf16[4,128,128]{2,1,0:T(8,128)(2,1)S(1)}, u32[]{:S(2)}, u32[]{:S(2)}) collective-permute-start(bf16[4,128,128]{2,1,0:T(8,128)(2,1)S(1)} %double_states.3), channel_id=1, source_target_pairs={{0,16},{1,17},{2,18},{3,19},{4,20},{5,21},{6,22},{7,23},{8,24},{9,... | collective-permute-start | bytes 393224 | tf_op jit(solution)/shard_map/ppermute | solution.py:369
  65.2 5.9 %collective-permute-start.16 = (bf16[4,128,128]{2,1,0:T(8,128)(2,1)S(1)}, bf16[4,128,128]{2,1,0:T(8,128)(2,1)S(1)}, u32[]{:S(2)}, u32[]{:S(2)}) collective-permute-start(bf16[4,128,128]{2,1,0:T(8,128)(2,1)S(1)} %get-tuple-element.110), channel_id=1, source_target_pairs={{0,2},{1,3},{2,0},{3,1},{4,6},{5,7},{6,4},{7,5},{8,10},{9,11},{10,... | collective-permute-start | bytes 393224 | tf_op jit(solution)/shard_map/ppermute | solution.py:369
  65.8 7.8 %collective-permute-start.17 = (bf16[4,128,128]{2,1,0:T(8,128)(2,1)S(1)}, bf16[4,128,128]{2,1,0:T(8,128)(2,1)S(1)}, u32[]{:S(2)}, u32[]{:S(2)}) collective-permute-start(bf16[4,128,128]{2,1,0:T(8,128)(2,1)S(1)} %get-tuple-element.111), channel_id=1, source_target_pairs={{0,4},{1,5},{2,6},{3,7},{4,0},{5,1},{6,2},{7,3},{8,12},{9,13},{10,... | collective-permute-start | bytes 393224 | tf_op jit(solution)/shard_map/ppermute | solution.py:369
  67.5 6.1 %collective-permute-start.18 = (bf16[4,128,128]{2,1,0:T(8,128)(2,1)S(1)}, bf16[4,128,128]{2,1,0:T(8,128)(2,1)S(1)}, u32[]{:S(2)}, u32[]{:S(2)}) collective-permute-start(bf16[4,128,128]{2,1,0:T(8,128)(2,1)S(1)} %get-tuple-element.112), channel_id=1, source_target_pairs={{0,6},{1,7},{2,4},{3,5},{4,2},{5,3},{6,0},{7,1},{8,14},{9,15},{10,... | collective-permute-start | bytes 393224 | tf_op jit(solution)/shard_map/ppermute | solution.py:369
  74.2 2.2 %collective-permute-start.19 = (bf16[16,128,128]{2,1,0:T(8,128)(2,1)S(1)}, bf16[16,128,128]{2,1,0:T(8,128)(2,1)S(1)}, u32[]{:S(2)}, u32[]{:S(2)}) collective-permute-start(bf16[16,128,128]{2,1,0:T(8,128)(2,1)S(1)} %get-tuple-element.114), channel_id=1, source_target_pairs={{0,1},{1,0},{2,3},{3,2},{4,5},{5,4},{6,7},{7,6},{8,9},{9,8},{10,11... | collective-permute-start | bytes 1572872 | tf_op jit(solution)/shard_map/ppermute | solution.py:369

commit v4 on v3

v4 whole, which is shorter than its diff:
```python
import functools
import jax
import jax.numpy as jnp
from jax import lax
from jax.experimental import pallas as pl
from jax.experimental.pallas import tpu as pltpu
from jax.sharding import PartitionSpec as P

AXES = ("ctx", "head")
F32 = jnp.float32
BF16 = jnp.bfloat16
VMEM_LIMIT = 16 * 1024 * 1024
LOCAL_LIMIT = 51 * 1024 * 1024
BATCH = 16
CHUNKS = 4


def dot(a, b, dims):
    return lax.dot_general(a, b, (dims, ((), ())), preferred_element_type=F32)


AB = ((1,), (0,))
ABT = ((1,), (1,))
ATB = ((0,), (0,))


def decay(rate, steps):
    return jnp.exp(-rate * steps)


def positions(shape):
    return lax.broadcasted_iota(jnp.int32, shape, 0).astype(F32)


def causal_weights(rate, length):
    row = lax.broadcasted_iota(jnp.int32, (length, length), 0)
    col = lax.broadcasted_iota(jnp.int32, (length, length), 1)
    offset = (row - col).astype(F32)
    return jnp.where(offset >= 0, jnp.exp(-rate * jnp.maximum(offset, 0.0)), 0.0)


def my_index():
    return lax.axis_index("ctx") * lax.axis_size("head") + lax.axis_index("head")


def head_half(own):
    core = my_index() % 2
    return core if own else 1 - core


def split_heads(block_ref, scratch, half, heads):
    length, _, size = block_ref.shape
    start = pl.multiple_of(half * heads, heads)
    scratch[...] = block_ref[:, pl.ds(start, heads), :].astype(F32).reshape(length * heads, size)


def one_head(scratch, h, length, heads):
    return scratch[pl.ds(h, length, stride=heads), :]


def start_output(scratch, stage, out_ref, sems, half):
    length, heads, size = stage.shape
    chunks = sems.shape[0]
    rows = length // chunks
    start = pl.multiple_of(half * heads, heads)
    copies = []
    for c in range(chunks):
        piece = pl.ds(c * rows, rows)
        stage[piece] = scratch[pl.ds(c * rows * heads, rows * heads), :].reshape(rows, heads, size).astype(BF16)
        copy = pltpu.make_async_copy(stage.at[piece], out_ref.at[piece, pl.ds(start, heads), :], sems.at[c])
        copy.start()
        copies.append(copy)
    return copies


def batches(heads, size=BATCH):
    size = min(size, heads)
    return [range(start, start + size) for start in range(0, heads, size)]


def local_states(ks, vs, rates, kt_ref, vt_ref, s_ref):
    heads, length, size = kt_ref.shape
    tail_steps = length - 1.0 - positions((length, size))
    for batch in batches(heads):
        key = [one_head(ks, h, length, heads) for h in batch]
        value = [one_head(vs, h, length, heads).astype(BF16) for h in batch]
        tail = [decay(rates[h], tail_steps) for h in batch]
        decayed = [(k * t).astype(BF16) for k, t in zip(key, tail)]
        state = [dot(k, v, ATB) for k, v in zip(decayed, value)]
        for i, h in enumerate(batch):
            kt_ref[h] = key[i].astype(BF16)
            vt_ref[h] = value[i]
            s_ref[h] = state[i].astype(BF16)


def first_local_kernel(k_ref, v_ref, rates_ref, kt_ref, vt_ref, s_ref, k_rest, v_rest, rates_out, *scratch):
    kb, vb, ks, vs, rates, sems, rest_sems, rate_sem = scratch
    length, heads, size = kb.shape
    half = head_half(False)
    start = pl.multiple_of(half * heads, heads)
    rest = pl.multiple_of((1 - half) * heads, heads)
    chunks = sems.shape[1]
    rows = length // chunks
    rate_copy = pltpu.make_async_copy(rates_ref, rates, rate_sem)
    rate_copy.start()
    copies = []
    for c in range(chunks):
        piece = pl.ds(c * rows, rows)
        for n, (ref, buffer) in enumerate(((k_ref, kb), (v_ref, vb))):
            copy = pltpu.make_async_copy(ref.at[piece, pl.ds(start, heads), :], buffer.at[piece], sems.at[n, c])
            copy.start()
            copies.append(copy)
    rest_copies = []
    for n, (ref, buffer) in enumerate(((k_ref, k_rest), (v_ref, v_rest))):
        copy = pltpu.make_async_copy(ref.at[:, pl.ds(rest, heads), :], buffer, rest_sems.at[n])
        copy.start()
        rest_copies.append(copy)
    for c in range(chunks):
        piece = pl.ds(c * rows, rows)
        flat = pl.ds(c * rows * heads, rows * heads)
        copies[2 * c].wait()
        ks[flat, :] = kb[piece].astype(F32).reshape(rows * heads, size)
        copies[2 * c + 1].wait()
        vs[flat, :] = vb[piece].astype(F32).reshape(rows * heads, size)
    rate_copy.wait()
    for h in range(rates.shape[0]):
        rates_out[pl.ds(h, 1), :] = jnp.full((1, size), rates[h], F32)
    local_states(ks, vs, [rates[start + h] for h in range(heads)], kt_ref, vt_ref, s_ref)
    for copy in rest_copies:
        copy.wait()


def second_local_kernel(k_ref, v_ref, rate_ref, kt_ref, vt_ref, s_ref, ks, vs):
    heads, length, size = kt_ref.shape
    first = head_half(True) * heads
    ks[...] = k_ref[...].astype(F32).reshape(length * heads, size)
    vs[...] = v_ref[...].astype(F32).reshape(length * heads, size)
    rates = [rate_ref[pl.ds(first + h, 1), :] for h in range(heads)]
    local_states(ks, vs, rates, kt_ref, vt_ref, s_ref)


def attention_kernel(own, q_ref, g_ref, kt_ref, vt_ref, rate_ref, gain_ref, *rest):
    qt_ref, qd_ref, qd_across_ref, scaled_ref, a_ref, o_ref, gain_out, qs, gs = rest
    gain_out[...] = gain_ref[...]
    heads, length, size = kt_ref.shape
    half = head_half(own)
    first = half * heads
    split_heads(q_ref, qs, half, heads)
    split_heads(g_ref, gs, half, heads)
    head_steps = positions((length, size)) + 1.0
    for batch in batches(heads):
        rate = [rate_ref[pl.ds(first + h, 1), :] for h in batch]
        wide = [one_head(qs, h, length, heads) for h in batch]
        query = [q.astype(BF16) for q in wide]
        decayed = [(q * decay(r, head_steps)).astype(BF16) for q, r in zip(wide, rate)]
        scores = [dot(q, kt_ref[h], ABT) for q, h in zip(query, batch)]
        weights = [causal_weights(r, length) for r in rate]
        attention = [(s * w).astype(BF16) for s, w in zip(scores, weights)]
        inner = [dot(a, vt_ref[h], AB) for a, h in zip(attention, batch)]
        for i, h in enumerate(batch):
            qt_ref[h] = query[i]
            qd_ref[h] = decayed[i]
            qd_across_ref[h] = decayed[i].T
            scaled_ref[h] = gain_ref[pl.ds(first + h, 1), :] * one_head(gs, h, length, heads)
            a_ref[h] = attention[i]
            o_ref[h] = inner[i]


def norm_kernel(own, sizes, ks, qd_ref, qd_across_ref, scaled_ref, o_ref, in_ref, gain_ref, *rest):
    n_ref, go_ref, all_in_ref, sg_ref = rest[-4:]
    first = head_half(own) * qd_ref.shape[0]
    places = part_heads_of(sizes, ks, in_ref.shape[0])
    for batch in batches(len(places)):
        out = [o_ref[places[h]] + dot(qd_ref[places[h]], in_ref[h], AB) for h in batch]
        inv_rms = [lax.rsqrt(jnp.mean(o * o, axis=-1, keepdims=True) + 1e-06) for o in out]
        unit = [o * r for o, r in zip(out, inv_rms)]
        gain = [gain_ref[pl.ds(first + places[h], 1), :] for h in batch]
        scaled = [scaled_ref[places[h]] for h in batch]
        along = [jnp.mean(s * u, axis=-1, keepdims=True) for s, u in zip(scaled, unit)]
        grad_out = [
            (r * (s - u * m)).astype(BF16) for r, s, u, m in zip(inv_rms, scaled, unit, along)
        ]
        state = [dot(qd_across_ref[places[h]], g, AB) for h, g in zip(batch, grad_out)]
        for i, h in enumerate(batch):
            n_ref[places[h]] = (unit[i] * gain[i]).astype(BF16)
            go_ref[places[h]] = grad_out[i]
            all_in_ref[places[h]] = in_ref[h]
            sg_ref[h] = state[i].astype(BF16)


def inner_kernel(own, qt_ref, kt_ref, vt_ref, a_ref, go_ref, rate_ref, gs_ref, dk_ref, dv_ref, kd_ref, vd_ref):
    heads, length, size = qt_ref.shape
    tail_steps = length - 1.0 - positions((length, size))
    first = head_half(own) * heads
    for batch in batches(heads):
        inner = [dot(go_ref[h], vt_ref[h], ABT) for h in batch]
        value = [dot(a_ref[h], go_ref[h], ATB) for h in batch]
        weights = [causal_weights(rate_ref[pl.ds(first + h, 1), :], length) for h in batch]
        scores = [(s * w).astype(BF16) for s, w in zip(inner, weights)]
        key = [dot(s, qt_ref[h], ATB) for s, h in zip(scores, batch)]
        for i, h in enumerate(batch):
            gs_ref[h] = scores[i]
            dv_ref[h] = value[i]
            dk_ref[h] = key[i]
            tail = decay(rate_ref[pl.ds(first + h, 1), :], tail_steps)
            kd_ref[h] = (kt_ref[h].astype(F32) * tail).astype(BF16)
            vd_ref[h] = (vt_ref[h].astype(F32) * tail).astype(BF16)


def query_kernel(own, kt_ref, gs_ref, go_ref, in_ref, n_ref, rate_ref, *rest):
    n_out, dq_out, mark_ref, ns, ds, nb, db, sems = rest[-8:]
    mark_ref[...] = jnp.zeros(mark_ref.shape, F32)
    heads, length, size = kt_ref.shape
    half = head_half(own)
    first = half * heads
    head_steps = positions((length, size)) + 1.0
    for h in range(heads):
        ns[pl.ds(h, length, stride=heads), :] = n_ref[h].astype(F32)
    copies = start_output(ns, nb, n_out, sems.at[0], half)
    for batch in batches(heads):
        through = [dot(go_ref[h], in_ref[h], ABT) for h in batch]
        query = [dot(gs_ref[h], kt_ref[h], AB) for h in batch]
        for i, h in enumerate(batch):
            head_decay = decay(rate_ref[pl.ds(first + h, 1), :], head_steps)
            ds[pl.ds(h, length, stride=heads), :] = query[i] + head_decay * through[i]
    copies += start_output(ds, db, dq_out, sems.at[1], half)
    for copy in copies:
        copy.wait()


def add_later(sizes, ks, kd_ref, vd_ref, later_ref, dk_ref, dv_ref, keys, values):
    heads, length, size = kd_ref.shape
    places = part_heads_of(sizes, ks, later_ref.shape[0])
    for batch in batches(len(places)):
        key = [dot(vd_ref[places[h]], later_ref[h], ABT) for h in batch]
        value = [dot(kd_ref[places[h]], later_ref[h], AB) for h in batch]
        for i, h in enumerate(batch):
            at = places[h]
            keys[pl.ds(at, length, stride=heads), :] = dk_ref[at] + key[i]
            values[pl.ds(at, length, stride=heads), :] = dv_ref[at] + value[i]


def later_kernel(sizes, ks, *refs):
    add_later(sizes, ks, *refs[:5], *refs[-2:])


def join_kernel(ks, vs, k_ref, v_ref):
    k_ref[...] = ks[...].reshape(k_ref.shape).astype(BF16)
    v_ref[...] = vs[...].reshape(v_ref.shape).astype(BF16)


def last_kernel(own, sizes, parts, *refs):
    k_rest, v_rest = refs[5:7]
    dk_out, dv_out, ks, vs, kb, vb, sems = refs[-7:]
    heads = kb.shape[1]
    half = head_half(own)
    start = pl.multiple_of((1 - half) * heads, heads)
    copies = []
    for n, (block, out) in enumerate(((k_rest, dk_out), (v_rest, dv_out))):
        copy = pltpu.make_async_copy(block, out.at[:, pl.ds(start, heads), :], sems.at[2, n])
        copy.start()
        copies.append(copy)
    add_later(sizes, parts, *refs[:5], ks, vs)
    copies += start_output(ks, kb, dk_out, sems.at[0], half)
    copies += start_output(vs, vb, dv_out, sems.at[1], half)
    for copy in copies:
        copy.wait()


def row_weight(rate, span, steps):
    weight = jnp.exp(-rate * (span * jnp.maximum(steps, 0).astype(F32)))
    return jnp.where(steps >= 0, weight, 0.0)


def place_at(sizes, level, forward=True):
    low = 1
    for size in sizes[:level]:
        low *= size
    place = (my_index() // low) % sizes[level]
    return place if forward else place ^ (sizes[level] - 1)


def first_head(sizes, level, heads, forward):
    first, count = 0, heads
    for above in range(level + 1):
        count //= sizes[above]
        place = place_at(sizes, above)
        if above == 0 and not forward:
            place = 1 - place
        first = first + place * count
    return first


def part_start(sizes, k, heads):
    return (place_at(sizes, 1) ^ k) * heads


def part_heads_of(sizes, ks, count):
    part = count // len(ks)
    return [part_start(sizes, k, part) + i for k in ks for i in range(part)]


def fold_kernel(sizes, level, span, forward, rate_ref, *refs):
    group = sizes[level]
    top = level + 2 == len(sizes)
    count = 1 if top else sizes[level + 1]
    states, parts = refs[:group], refs[len(refs) - count :]
    heads = parts[0].shape[0]
    first = first_head(sizes, level, rate_ref.shape[0], forward)
    place = place_at(sizes, level, forward)
    weigh = [group - 1 - (place ^ j) for j in range(group)]
    for k in range(count):
        start = 0 if top else (place_at(sizes, level + 1) ^ k) * heads
        for i in range(heads):
            rate = rate_ref[pl.ds(first + start + i, 1), :]
            total = None
            for j in range(group):
                term = row_weight(rate, span, weigh[j]) * states[j][start + i].astype(F32)
                total = term if total is None else total + term
            parts[k][i] = total.astype(BF16)


def pair_fold_kernel(sizes, ks, span, forward, rate_ref, kept_ref, other_ref, *rest):
    out_refs = rest[len(rest) - len(ks) :]
    first = first_head(sizes, 0, rate_ref.shape[0], forward)
    place = place_at(sizes, 0, forward)
    part = out_refs[0].shape[0]
    for i, head in enumerate(part_heads_of(sizes, ks, part * len(ks))):
        at = head if kept_ref.shape[0] > part * len(ks) else i
        rate = rate_ref[pl.ds(first + head, 1), :]
        total = row_weight(rate, span, 1 - place) * kept_ref[at].astype(F32)
        total = total + row_weight(rate, span, place) * other_ref[at].astype(F32)
        out_refs[i // part][i % part] = total.astype(BF16)


def double_kernel(sizes, level, step, span, forward, rate_ref, state_ref, other_ref, *rest):
    out_ref = rest[-1]
    first = first_head(sizes, level - 1, rate_ref.shape[0], forward)
    upper = (place_at(sizes, level, forward) // step) % 2
    for i in range(out_ref.shape[0]):
        rate = rate_ref[pl.ds(first + i, 1), :]
        total = row_weight(rate, span * step, 1 - upper) * state_ref[i].astype(F32)
        total = total + row_weight(rate, span * step, upper) * other_ref[i].astype(F32)
        out_ref[i] = total.astype(BF16)


def spread_kernel(sizes, level, span, forward, rate_ref, *refs):
    group, next_group = sizes[level], sizes[level + 1]
    top = level + 2 == len(sizes)
    count = 1 if top else next_group
    ahead_count = next_group.bit_length() - 1 if top else next_group
    states, ahead, outs = refs[:group], refs[group : group + ahead_count], refs[len(refs) - group :]
    heads = states[0].shape[0]
    part_heads = heads // count
    first = first_head(sizes, level, rate_ref.shape[0], forward)
    place = place_at(sizes, level, forward)
    top_place = place_at(sizes, level + 1, forward)
    for k in range(count):
        start = 0 if top else (place_at(sizes, level + 1) ^ k) * part_heads
        for i in range(part_heads):
            rate = rate_ref[pl.ds(first + start + i, 1), :]
            if top:
                before = None
                for j in range(ahead_count):
                    step = 1 << j
                    steps = jnp.where((top_place // step) % 2 == 1, top_place % step, -1)
                    term = row_weight(rate, span * group, steps) * ahead[j][i].astype(F32)
                    before = term if before is None else before + term
            else:
                before = ahead[k][i].astype(F32)
            own = [states[j][start + i].astype(F32) for j in range(group)]
            for j in range(group):
                total = row_weight(rate, span, place ^ j) * before
                for q in range(group):
                    if q != j:
                        total = total + row_weight(rate, span, (place ^ j) - 1 - (place ^ q)) * own[q]
                outs[j][start + i] = total.astype(BF16)


def pair_spread_kernel(sizes, ks, span, forward, rate_ref, kept_ref, other_ref, *rest):
    before_refs, (send_ref, mine_ref) = rest[: len(ks)], rest[-2:]
    count = send_ref.shape[0]
    part = count // len(ks)
    first = first_head(sizes, 0, rate_ref.shape[0], forward)
    place = place_at(sizes, 0, forward)
    for i, head in enumerate(part_heads_of(sizes, ks, count)):
        at = head if kept_ref.shape[0] > count else i
        rate = rate_ref[pl.ds(first + head, 1), :]
        before = before_refs[i // part][i % part].astype(F32)
        onward = row_weight(rate, span, 1) * before
        send = onward + kept_ref[at].astype(F32)
        send_ref[i] = jnp.where(place == 0, send, before).astype(BF16)
        mine = onward + other_ref[at].astype(F32)
        mine_ref[i] = jnp.where(place == 0, before, mine).astype(BF16)


WHOLE = pl.BlockSpec(memory_space=pltpu.VMEM)
ANYWHERE = pl.BlockSpec(memory_space=pl.ANY)
OUTSIDE = pl.BlockSpec(memory_space=pltpu.HBM)


def call(body, inputs, outputs, scratch=(), anywhere=(), outside=(), out_outside=(), aliases=None, flops=0, name=None, limit=VMEM_LIMIT, count_bytes=True):
    nbytes = sum(a.size * a.dtype.itemsize for a in inputs) + sum(s.size * s.dtype.itemsize for s in outputs)
    nbytes = nbytes if count_bytes else 0
    return list(pl.pallas_call(
        body,
        in_specs=[ANYWHERE if n in anywhere else OUTSIDE if n in outside else WHOLE for n in range(len(inputs))],
        out_specs=[OUTSIDE if n in out_outside else WHOLE for n in range(len(outputs))],
        scratch_shapes=list(scratch),
        out_shape=list(outputs),
        input_output_aliases=aliases or {},
        compiler_params=pltpu.CompilerParams(vmem_limit_bytes=limit),
        cost_estimate=pl.CostEstimate(flops=flops, bytes_accessed=nbytes, transcendentals=0),
        name=name,
    )(*inputs))


def level_sizes(devices):
    sizes = [2]
    left = devices // 2
    while left > 8:
        sizes.append(4)
        left //= 4
    return sizes + [left]


def swap(array, distance, devices):
    return lax.ppermute(array, AXES, [(i, i ^ distance) for i in range(devices)])


def carry_states(parts, sizes, devices, rates, length, forward, beside):
    state = parts[0].shape[1:]

    def climb(level, low, parts):
        group, next_group = sizes[level], sizes[level + 1]
        top = level + 2 == len(sizes)
        span = float(length * low)
        states = [parts[0]] + [swap(parts[k], k * low, devices) for k in range(1, group)]
        heads = parts[0].shape[0]
        count = 1 if top else next_group
        part = jax.ShapeDtypeStruct((heads // count,) + state, BF16)
        inputs = [rates] + states + (beside["fold"] if level == 1 else [])
        folded = call(
            functools.partial(fold_kernel, sizes, level, span, forward),
            inputs,
            [part] * count,
            anywhere=range(1 + group, len(inputs)),
            name="fold_states",
        )
        if top:
            total, ahead, step = folded[0], [], 1
            while step < next_group:
                if step > 1:
                    inputs = [rates, total, ahead[-1]] + (beside["double"] if step == 2 else [])
                    (total,) = call(
                        functools.partial(
                            double_kernel, sizes, level + 1, step // 2, span * group, forward
                        ),
                        inputs,
                        [part],
                        anywhere=range(3, len(inputs)),
                        name="double_states",
                    )
                ahead.append(swap(total, (2 * step - 1) * low * group, devices))
                step *= 2
        else:
            ahead = climb(level + 1, low * group, folded)
        inputs = [rates] + states + ahead + (beside["spread"] if level == 1 else [])
        outs = call(
            functools.partial(spread_kernel, sizes, level, span, forward),
            inputs,
            [jax.ShapeDtypeStruct((heads,) + state, BF16)] * group,
            anywhere=range(1 + group + len(ahead), len(inputs)),
            name="spread_states",
        )
        return [outs[0]] + [swap(outs[k], k * low, devices) for k in range(1, group)]

    return climb(1, sizes[0], parts)


def local(devices, queries, key_vectors, value_vectors, output_grad, decay_rate, norm_gain):
    length, heads, size = queries.shape
    half = heads // 2
    sizes = level_sizes(devices)
    parts = sizes[1]

    def shaped(*shape, dtype=BF16):
        return jax.ShapeDtypeStruct(shape, dtype)

    per_head = shaped(half, length, size)
    per_head_wide = shaped(half, length, size, dtype=F32)
    states = shaped(half, size, size)
    part_states = shaped(half // parts, size, size)
    whole = shaped(length, heads, size)
    block = shaped(length, half, size)
    flat_rows = shaped(length * half, size, dtype=F32)
    flat = pltpu.VMEM((length * half, size), F32)
    stage = pltpu.VMEM((length, half, size), BF16)
    copy_sem = pltpu.SemaphoreType.DMA
    sems = copy_sem((2, CHUNKS))
    unit = 2 * half * length * size * size
    span = float(length)

    sent_key, sent_value, sent_state, key_rest, value_rest, rates = call(
        first_local_kernel,
        [key_vectors, value_vectors, decay_rate],
        [per_head, per_head, states, block, block, shaped(heads, size, dtype=F32)],
        [stage, stage, flat, flat, pltpu.SMEM((heads,), F32), sems, copy_sem((2,)), copy_sem],
        outside=(0, 1, 2),
        limit=LOCAL_LIMIT,
        flops=unit,
        name="local_states",
    )
    kept_key, kept_value, kept_state = call(
        second_local_kernel,
        [key_rest, value_rest, rates],
        [per_head, per_head, states],
        [flat, flat],
        flops=unit,
        name="local_states",
    )
    keys, values = [kept_key, sent_key], [kept_value, sent_value]
    other_state = swap(sent_state, 1, devices)
    query, normal, attention, inner = [None, None], [None, None], [None, None], [None, None]
    gains = norm_gain
    for s in (0, 1):
        query[s], *normal[s], attention[s], inner[s], gains = call(
            functools.partial(attention_kernel, s == 0),
            [queries, output_grad, keys[s], values[s], rates, gains],
            [per_head, per_head, shaped(half, size, length), per_head_wide]
            + [shaped(half, length, length), per_head_wide, shaped(heads, size, dtype=F32)],
            [flat, flat],
            flops=2 * unit,
            name="attention",
        )
    folded = {}
    for ks in ((parts - 1,), range(parts - 1)):
        inputs = [rates, kept_state, other_state] + list(folded.values())
        parts_here = call(
            functools.partial(pair_fold_kernel, sizes, ks, span, True),
            inputs,
            [part_states] * len(ks),
            anywhere=range(3, len(inputs)),
            name="fold_pair",
        )
        folded.update(zip(ks, parts_here))
    before = carry_states(
        folded, sizes, devices, rates, length, True, {"fold": inner[:1], "double": [], "spread": inner[1:]}
    )

    stages = [(0, parts - 1), range(1, parts - 1)]

    def spread_pair(ks, forward, before, kept, other, beside):
        inputs = [rates, kept, other] + [before[k] for k in ks] + beside
        stage_states = shaped(half // parts * len(ks), size, size)
        return call(
            functools.partial(pair_spread_kernel, sizes, ks, span, forward),
            inputs,
            [stage_states] * 2,
            anywhere=range(3 + len(ks), len(inputs)),
            name="spread_pair",
        )

    made, folded, kept_grads, other_grads = [[], []], {}, [], []
    for ks in stages:
        send, mine = spread_pair(ks, True, before, kept_state, other_state, made[0][:1])
        grads = []
        for s, incoming in ((0, mine), (1, swap(send, 1, devices))):
            inputs = [*normal[s], inner[s], incoming, gains]
            *made[s], state_grad = call(
                functools.partial(norm_kernel, s == 0, sizes, ks),
                inputs + made[s],
                [per_head, per_head, states, send],
                aliases={len(inputs) + n: n for n in range(len(made[s]))},
                flops=unit,
                name="norm",
            )
            grads.append(state_grad)
        kept_grads.append(grads[1])
        other_grads.append(swap(grads[0], 1, devices))
        inputs = [rates, kept_grads[-1], other_grads[-1]] + list(folded.values())[-1:]
        parts_here = call(
            functools.partial(pair_fold_kernel, sizes, ks, span, False),
            inputs,
            [part_states] * len(ks),
            anywhere=range(3, len(inputs)),
            name="fold_pair",
        )
        folded.update(zip(ks, parts_here))
    normed_out, query_out = None, None
    key_part, value_part, key_decayed, value_decayed, marks = [None] * 2, [None] * 2, [None] * 2, [None] * 2, []
    for s in (0, 1):
        normed, grad_out, incoming = made[s]
        scores, key_part[s], value_part[s], key_decayed[s], value_decayed[s] = call(
            functools.partial(inner_kernel, s == 0),
            [query[s], keys[s], values[s], attention[s], grad_out, rates],
            [shaped(half, length, length), per_head_wide, per_head_wide, per_head, per_head],
            flops=3 * unit,
            name="inner_gradients",
        )
        inputs = [keys[s], scores, grad_out, incoming, normed, rates]
        count = len(inputs)
        aliases = {}
        if s:
            aliases = {count: 0, count + 1: 1}
            inputs += [normed_out, query_out]
        normed_out, query_out, mark = call(
            functools.partial(query_kernel, s == 0),
            inputs,
            [whole, whole, shaped(8, size, dtype=F32)],
            [flat, flat, stage, stage, sems],
            outside=(count, count + 1),
            out_outside=(0, 1),
            aliases=aliases,
            flops=2 * unit,
            name="query_gradient",
        )
        marks.append(mark)
    after = carry_states(
        folded,
        sizes,
        devices,
        rates,
        length,
        False,
        {"fold": key_part, "double": marks[:1], "spread": marks[1:]},
    )
    flats = [[], []]
    for n, ks in enumerate(stages):
        send, mine = spread_pair(ks, False, after, kept_grads[n], other_grads[n], flats[1][:1])
        for s, later in ((1, mine), (0, swap(send, 1, devices))):
            inputs = [key_decayed[s], value_decayed[s], later, key_part[s], value_part[s]]
            if s == 0 and n:
                break
            flats[s] = call(
                functools.partial(later_kernel, sizes, ks),
                inputs + flats[s],
                [flat_rows, flat_rows],
                aliases={len(inputs) + m: m for m in range(len(flats[s]))},
                flops=unit,
                name="later_gradients",
            )
    inputs += call(join_kernel, flats[1], [block, block], name="join_heads")
    key_out, value_out, *_ = call(
        functools.partial(last_kernel, True, sizes, stages[-1]),
        inputs + flats[0],
        [whole, whole, flat_rows, flat_rows],
        [stage, stage, copy_sem((3, CHUNKS))],
        out_outside=(0, 1),
        aliases={len(inputs) + n: 2 + n for n in range(2)},
        flops=unit,
        name="last_gradients",
    )
    return normed_out, query_out, key_out, value_out


def solution(mesh):
    devices = mesh.shape["ctx"] * mesh.shape["head"]
    spread = P(AXES, None, None)
    return jax.shard_map(
        functools.partial(local, devices),
        mesh=mesh,
        in_specs=(spread, spread, spread, spread, P(), P()),
        out_specs=(spread, spread, spread, spread),
        check_vma=False,
    )
```

time: 78.9 us -> 74.8 us (0.948)
  waiting for transfers between devices: 31.6 us -> 22.4 us
  starting transfers between devices: 23.4 us -> 28.1 us
    ppermute x20 -> x23, waiting for transfers between devices: 31.6 us -> 22.4 us  [swap(): lax.ppermute(array, AXES, [(i, i ^ distance) for i in range(devices)])]
    ppermute x20 -> x23, starting transfers between devices: 23.4 us -> 28.1 us  [swap(): lax.ppermute(array, AXES, [(i, i ^ distance) for i in range(devices)])]
    pallas_call x22 -> x31, Pallas kernels: 21.8 us -> 22.5 us  [call(): pl.pallas_call(body, in_specs=[ANYWHERE if n in anywhere else OUTSIDE if...]
  transfers between devices with their start and end apart: 20 -> 23, of which waited for: 15 -> 17; matrix products, arithmetic and copies ran while one was open for 0% -> 0% of each run, Pallas kernels for 18% -> 23%
where the time goes in v4:
time: 74.8 us; the launch traced here: 74.7 us
  starting transfers between devices  28.1 us (38%)
  Pallas kernels  22.5 us (30%)
  waiting for transfers between devices  22.4 us (30%)
  between operations  1.08 us (1%)
    ppermute x23, starting transfers between devices, swap(): lax.ppermute(array, AXES, [(i, i ^ distance) for i in range(devices)])  28.1 us
    pallas_call x31, Pallas kernels, call(): pl.pallas_call(body, in_specs=[ANYWHERE if n in anywhere else OUTSIDE if...  22.5 us
    ppermute x23, waiting for transfers between devices, swap(): lax.ppermute(array, AXES, [(i, i ^ distance) for i in range(devices)])  22.4 us
  transfers between devices with their start and end apart: 23, of which 17 were waited for; matrix products, arithmetic and copies ran while one was open for 0% of the time, Pallas kernels for 23%

profile of v4, /device:TPU:0, one launch (start us, length us, event | category | flops | bytes accessed | tf_op | source)
XLA Modules:
  0.0 74.7 jit_solution(3335633362949556000)
XLA Ops:
  1.3 2.4 %local_states.2 = (bf16[16,128,128]{2,1,0:T(8,128)(2,1)S(1)}, bf16[16,128,128]{2,1,0:T(8,128)(2,1)S(1)}, bf16[16,128,128]{2,1,0:T(8,128)(2,1)S(1)}, bf16[128,16,...) custom-call(bf16[128,32,128]{2,1,0:T(8,128)(2,1)} %k_ref.1, ...), custom_call_target="tpu_custom_call" | custom-call | flops 67108864 | bytes 4735104 | tf_op jit(solution)/shard_map/local_states/pallas_call | solution.py:405
  5.9 3.9 %collective-permute-start.3 = (bf16[4,128,128]{2,1,0:T(8,128)(2,1)S(1)}, bf16[4,128,128]{2,1,0:T(8,128)(2,1)S(1)}, u32[]{:S(2)}, u32[]{:S(2)}) collective-permute-start(bf16[4,128,128]{2,1,0:T(8,128)(2,1)S(1)} %fold_pair.4.rest_0_), channel_id=1, source_target_pairs={{0,6},{1,7},{2,4},{3,5},{4,2},{5,3},{6,0},{7,1},{8,14},{9,15},{10,... | collective-permute-start | bytes 393224 | tf_op jit(solution)/shard_map/ppermute | solution.py:428
  10.6 1.4 %attention.2 = (bf16[16,128,128]{2,1,0:T(8,128)(2,1)S(1)}, bf16[16,128,128]{2,1,0:T(8,128)(2,1)S(1)}, bf16[16,128,128]{2,1,0:T(8,128)(2,1)S(1)}, f32[16,128,128]...) custom-call(bf16[128,32,128]{2,1,0:T(8,128)(2,1)S(1)} %copy-done, ...), custom_call_target="tpu_custom_call" | custom-call | flops 134217728 | bytes 7389184 | tf_op jit(solution)/shard_map/attention/pallas_call | solution.py:405
  12.0 2.0 %collective-permute-done.3.refs_3_ = bf16[4,128,128]{2,1,0:T(8,128)(2,1)S(1)} collective-permute-done((bf16[4,128,128]{2,1,0:T(8,128)(2,1)S(1)}, bf16[4,128,128]{2,1,0:T(8,128)(2,1)S(1)}, u32[]{:S(2)}, u32[]{:S(2)}) %collective-permute-start.3) | collective-permute-done | bytes 131104 | tf_op jit(solution)/shard_map/ppermute | solution.py:428
  14.0 2.6 %collective-permute-done.1.refs_1_ = bf16[4,128,128]{2,1,0:T(8,128)(2,1)S(1)} collective-permute-done((bf16[4,128,128]{2,1,0:T(8,128)(2,1)S(1)}, bf16[4,128,128]{2,1,0:T(8,128)(2,1)S(1)}, u32[]{:S(2)}, u32[]{:S(2)}) %collective-permute-start.1) | collective-permute-done | bytes 131104 | tf_op jit(solution)/shard_map/ppermute | solution.py:428
  16.8 1.6 %collective-permute-start.4 = (bf16[4,128,128]{2,1,0:T(8,128)(2,1)S(1)}, bf16[4,128,128]{2,1,0:T(8,128)(2,1)S(1)}, u32[]{:S(2)}, u32[]{:S(2)}) collective-permute-start(bf16[4,128,128]{2,1,0:T(8,128)(2,1)S(1)} %fold_states.2.state_ref), channel_id=1, source_target_pairs={{0,8},{1,9},{2,10},{3,11},{4,12},{5,13},{6,14},{7,15},{8,0},{9,1},... | collective-permute-start | bytes 393224 | tf_op jit(solution)/shard_map/ppermute | solution.py:428
  18.4 3.4 %collective-permute-done.4.other_ref.refs_4_ = bf16[4,128,128]{2,1,0:T(8,128)(2,1)S(1)} collective-permute-done((bf16[4,128,128]{2,1,0:T(8,128)(2,1)S(1)}, bf16[4,128,128]{2,1,0:T(8,128)(2,1)S(1)}, u32[]{:S(2)}, u32[]{:S(2)}) %collective-permute-start.4) | collective-permute-done | bytes 131104 | tf_op jit(solution)/shard_map/ppermute | solution.py:428
  21.9 3.7 %collective-permute-start.5 = (bf16[4,128,128]{2,1,0:T(8,128)(2,1)S(1)}, bf16[4,128,128]{2,1,0:T(8,128)(2,1)S(1)}, u32[]{:S(2)}, u32[]{:S(2)}) collective-permute-start(bf16[4,128,128]{2,1,0:T(8,128)(2,1)S(1)} %double_states.2), channel_id=1, source_target_pairs={{0,24},{1,25},{2,26},{3,27},{4,28},{5,29},{6,30},{7,31},{8,16},{9,... | collective-permute-start | bytes 393224 | tf_op jit(solution)/shard_map/ppermute | solution.py:428
  25.6 1.4 %attention.3 = (bf16[16,128,128]{2,1,0:T(8,128)(2,1)S(1)}, bf16[16,128,128]{2,1,0:T(8,128)(2,1)S(1)}, bf16[16,128,128]{2,1,0:T(8,128)(2,1)S(1)}, f32[16,128,128]...) custom-call(bf16[128,32,128]{2,1,0:T(8,128)(2,1)S(1)} %copy-done, ...), custom_call_target="tpu_custom_call" | custom-call | flops 134217728 | bytes 7389184 | tf_op jit(solution)/shard_map/attention/pallas_call | solution.py:405
  27.0 1.8 %collective-permute-done.5.refs_5_ = bf16[4,128,128]{2,1,0:T(8,128)(2,1)S(1)} collective-permute-done((bf16[4,128,128]{2,1,0:T(8,128)(2,1)S(1)}, bf16[4,128,128]{2,1,0:T(8,128)(2,1)S(1)}, u32[]{:S(2)}, u32[]{:S(2)}) %collective-permute-start.5) | collective-permute-done | bytes 131104 | tf_op jit(solution)/shard_map/ppermute | solution.py:428
  29.3 2.8 %collective-permute-start.8 = (bf16[4,128,128]{2,1,0:T(8,128)(2,1)S(1)}, bf16[4,128,128]{2,1,0:T(8,128)(2,1)S(1)}, u32[]{:S(2)}, u32[]{:S(2)}) collective-permute-start(bf16[4,128,128]{2,1,0:T(8,128)(2,1)S(1)} %get-tuple-element.118), channel_id=1, source_target_pairs={{0,6},{1,7},{2,4},{3,5},{4,2},{5,3},{6,0},{7,1},{8,14},{9,15},{10,... | collective-permute-start | bytes 393224 | tf_op jit(solution)/shard_map/ppermute | solution.py:428
  32.8 2.6 %collective-permute-done.8.rest_1_ = bf16[4,128,128]{2,1,0:T(8,128)(2,1)S(1)} collective-permute-done((bf16[4,128,128]{2,1,0:T(8,128)(2,1)S(1)}, bf16[4,128,128]{2,1,0:T(8,128)(2,1)S(1)}, u32[]{:S(2)}, u32[]{:S(2)}) %collective-permute-start.8) | collective-permute-done | bytes 131104 | tf_op jit(solution)/shard_map/ppermute | solution.py:428
  40.1 2.1 %collective-permute-start.15 = (bf16[4,128,128]{2,1,0:T(8,128)(2,1)S(1)}, bf16[4,128,128]{2,1,0:T(8,128)(2,1)S(1)}, u32[]{:S(2)}, u32[]{:S(2)}) collective-permute-start(bf16[4,128,128]{2,1,0:T(8,128)(2,1)S(1)} %get-tuple-element.151.rest_0_), channel_id=1, source_target_pairs={{0,6},{1,7},{2,4},{3,5},{4,2},{5,3},{6,0},{7,1},{8,14},{9,15},{10,... | collective-permute-start | bytes 393224 | tf_op jit(solution)/shard_map/ppermute | solution.py:428
  44.6 1.1 %inner_gradients.3 = (bf16[16,128,128]{2,1,0:T(8,128)(2,1)S(1)}, f32[16,128,128]{2,1,0:T(8,128)S(1)}, f32[16,128,128]{2,1,0:T(8,128)S(1)}, bf16[16,128,128]{2,1,0:T(8,128)(2,1)S(1)}, bf16[16,128,128]{2,1,0:T(8,128)(2,1)S(1)}) custom-call(bf16[16,128,128]{2,1,0:T(8,128)(2,1)S(1)} %get-tuple-element.131.qt_ref, ...), custom_call_target="tpu_custom_call" | custom-call | flops 201326592 | bytes 6307840 | tf_op jit(solution)/shard_map/inner_gradients/pallas_call | solution.py:405
  45.7 1.3 %inner_gradients.2 = (bf16[16,128,128]{2,1,0:T(8,128)(2,1)S(1)}, f32[16,128,128]{2,1,0:T(8,128)S(1)}, f32[16,128,128]{2,1,0:T(8,128)S(1)}, bf16[16,128,128]{2,1,0:T(8,128)(2,1)S(1)}, bf16[16,128,128]{2,1,0:T(8,128)(2,1)S(1)}) custom-call(bf16[16,128,128]{2,1,0:T(8,128)(2,1)S(1)} %get-tuple-element.100.qt_ref, ...), custom_call_target="tpu_custom_call" | custom-call | flops 201326592 | bytes 6307840 | tf_op jit(solution)/shard_map/inner_gradients/pallas_call | solution.py:405
  47.1 1.8 %collective-permute-done.13.refs_1_ = bf16[4,128,128]{2,1,0:T(8,128)(2,1)S(1)} collective-permute-done((bf16[4,128,128]{2,1,0:T(8,128)(2,1)S(1)}, bf16[4,128,128]{2,1,0:T(8,128)(2,1)S(1)}, u32[]{:S(2)}, u32[]{:S(2)}) %collective-permute-start.13) | collective-permute-done | bytes 131104 | tf_op jit(solution)/shard_map/ppermute | solution.py:428
  49.4 2.8 %collective-permute-start.16 = (bf16[4,128,128]{2,1,0:T(8,128)(2,1)S(1)}, bf16[4,128,128]{2,1,0:T(8,128)(2,1)S(1)}, u32[]{:S(2)}, u32[]{:S(2)}) collective-permute-start(bf16[4,128,128]{2,1,0:T(8,128)(2,1)S(1)} %fold_states.3.state_ref), channel_id=1, source_target_pairs={{0,8},{1,9},{2,10},{3,11},{4,12},{5,13},{6,14},{7,15},{8,0},{9,1},... | collective-permute-start | bytes 393224 | tf_op jit(solution)/shard_map/ppermute | solution.py:428
  52.2 2.4 %query_gradient.2 = (bf16[128,32,128]{2,1,0:T(8,128)(2,1)}, bf16[128,32,128]{2,1,0:T(8,128)(2,1)}, f32[8,128]{1,0:T(8,128)S(1)}) custom-call(bf16[16,128,128]{2,1,0:T(8,128)(2,1)S(1)} %get-tuple-element.97.kt_ref, bf16[16,128,128]{2,1,0:T(8,128)(2,1)S(1)} %get-tuple-element.137.gs_ref, bf16[16,128,128]{2,1,0:T(8,128)(2,1)S(1)} %get-tuple-element.136.go_ref, ...), custom_call_target="tpu_custom_call" | custom-call | flops 134217728 | bytes 4739072 | tf_op jit(solution)/shard_map/query_gradient/pallas_call | solution.py:405
  55.4 2.8 %collective-permute-start.17 = (bf16[4,128,128]{2,1,0:T(8,128)(2,1)S(1)}, bf16[4,128,128]{2,1,0:T(8,128)(2,1)S(1)}, u32[]{:S(2)}, u32[]{:S(2)}) collective-permute-start(bf16[4,128,128]{2,1,0:T(8,128)(2,1)S(1)} %double_states.3), channel_id=1, source_target_pairs={{0,24},{1,25},{2,26},{3,27},{4,28},{5,29},{6,30},{7,31},{8,16},{9,... | collective-permute-start | bytes 393224 | tf_op jit(solution)/shard_map/ppermute | solution.py:428
  58.2 2.4 %query_gradient.3 = (bf16[128,32,128]{2,1,0:T(8,128)(2,1)}, bf16[128,32,128]{2,1,0:T(8,128)(2,1)}, f32[8,128]{1,0:T(8,128)S(1)}) custom-call(bf16[16,128,128]{2,1,0:T(8,128)(2,1)S(1)} %get-tuple-element.92.kt_ref, bf16[16,128,128]{2,1,0:T(8,128)(2,1)S(1)} %get-tuple-element.128.gs_ref, ...), custom_call_target="tpu_custom_call", output_to_operand_aliasing={{0}: (6, {}), {1}: (7, {})} | custom-call | flops 134217728 | bytes 6836224 | tf_op jit(solution)/shard_map/query_gradient/pallas_call | solution.py:405
  60.6 1.7 %collective-permute-done.17.refs_5_ = bf16[4,128,128]{2,1,0:T(8,128)(2,1)S(1)} collective-permute-done((bf16[4,128,128]{2,1,0:T(8,128)(2,1)S(1)}, bf16[4,128,128]{2,1,0:T(8,128)(2,1)S(1)}, u32[]{:S(2)}, u32[]{:S(2)}) %collective-permute-start.17) | collective-permute-done | bytes 131104 | tf_op jit(solution)/shard_map/ppermute | solution.py:428
  62.8 2.5 %collective-permute-start.20 = (bf16[4,128,128]{2,1,0:T(8,128)(2,1)S(1)}, bf16[4,128,128]{2,1,0:T(8,128)(2,1)S(1)}, u32[]{:S(2)}, u32[]{:S(2)}) collective-permute-start(bf16[4,128,128]{2,1,0:T(8,128)(2,1)S(1)} %get-tuple-element.163), channel_id=1, source_target_pairs={{0,6},{1,7},{2,4},{3,5},{4,2},{5,3},{6,0},{7,1},{8,14},{9,15},{10,... | collective-permute-start | bytes 393224 | tf_op jit(solution)/shard_map/ppermute | solution.py:428
  66.3 2.5 %collective-permute-done.20.rest_1_ = bf16[4,128,128]{2,1,0:T(8,128)(2,1)S(1)} collective-permute-done((bf16[4,128,128]{2,1,0:T(8,128)(2,1)S(1)}, bf16[4,128,128]{2,1,0:T(8,128)(2,1)S(1)}, u32[]{:S(2)}, u32[]{:S(2)}) %collective-permute-start.20) | collective-permute-done | bytes 131104 | tf_op jit(solution)/shard_map/ppermute | solution.py:428
  72.8 1.7 %last_gradients.1 = (bf16[128,32,128]{2,1,0:T(8,128)(2,1)}, bf16[128,32,128]{2,1,0:T(8,128)(2,1)}, f32[2048,128]{1,0:T(8,128)S(1)}, f32[2048,128]{1,0:T(8,128)S(1)}) custom-call(bf16[16,128,128]{2,1,0:T(8,128)(2,1)S(1)} %get-tuple-element.144.refs_0_, ...), custom_call_target="tpu_custom_call", output_to_operand_aliasing={{2}: (7, {}), {3}: (8, {})} | custom-call | flops 67108864 | bytes 10747904 | tf_op jit(solution)/shard_map/last_gradients/pallas_call | solution.py:405
  (61 shorter events, 18.9 us)
Async XLA Ops:
  3.7 2.1 %collective-permute-start = (bf16[16,128,128]{2,1,0:T(8,128)(2,1)S(1)}, bf16[16,128,128]{2,1,0:T(8,128)(2,1)S(1)}, u32[]{:S(2)}, u32[]{:S(2)}) collective-permute-start(bf16[16,128,128]{2,1,0:T(8,128)(2,1)S(1)} %get-tuple-element.107), channel_id=1, source_target_pairs={{0,1},{1,0},{2,3},{3,2},{4,5},{5,4},{6,7},{7,6},{8,9},{9,8},{10,11... | collective-permute-start | bytes 1572872 | tf_op jit(solution)/shard_map/ppermute | solution.py:428
  5.8 4.8 %copy-start.1 = (bf16[128,32,128]{2,1,0:T(8,128)(2,1)S(1)}, bf16[128,32,128]{2,1,0:T(8,128)(2,1)}, u32[]{:S(2)}) copy-start(bf16[128,32,128]{2,1,0:T(8,128)(2,1)} %g_ref.3) | copy-start | bytes 3145732
  5.9 8.2 %collective-permute-start.3 = (bf16[4,128,128]{2,1,0:T(8,128)(2,1)S(1)}, bf16[4,128,128]{2,1,0:T(8,128)(2,1)S(1)}, u32[]{:S(2)}, u32[]{:S(2)}) collective-permute-start(bf16[4,128,128]{2,1,0:T(8,128)(2,1)S(1)} %fold_pair.4.rest_0_), channel_id=1, source_target_pairs={{0,6},{1,7},{2,4},{3,5},{4,2},{5,3},{6,0},{7,1},{8,14},{9,15},{10,... | collective-permute-start | bytes 393224 | tf_op jit(solution)/shard_map/ppermute | solution.py:428
  9.9 6.7 %collective-permute-start.1 = (bf16[4,128,128]{2,1,0:T(8,128)(2,1)S(1)}, bf16[4,128,128]{2,1,0:T(8,128)(2,1)S(1)}, u32[]{:S(2)}, u32[]{:S(2)}) collective-permute-start(bf16[4,128,128]{2,1,0:T(8,128)(2,1)S(1)} %get-tuple-element.109), channel_id=1, source_target_pairs={{0,2},{1,3},{2,0},{3,1},{4,6},{5,7},{6,4},{7,5},{8,10},{9,11},{10,... | collective-permute-start | bytes 393224 | tf_op jit(solution)/shard_map/ppermute | solution.py:428
  10.5 6.1 %collective-permute-start.2 = (bf16[4,128,128]{2,1,0:T(8,128)(2,1)S(1)}, bf16[4,128,128]{2,1,0:T(8,128)(2,1)S(1)}, u32[]{:S(2)}, u32[]{:S(2)}) collective-permute-start(bf16[4,128,128]{2,1,0:T(8,128)(2,1)S(1)} %get-tuple-element.110), channel_id=1, source_target_pairs={{0,4},{1,5},{2,6},{3,7},{4,0},{5,1},{6,2},{7,3},{8,12},{9,13},{10,... | collective-permute-start | bytes 393224 | tf_op jit(solution)/shard_map/ppermute | solution.py:428
  16.8 5.0 %collective-permute-start.4 = (bf16[4,128,128]{2,1,0:T(8,128)(2,1)S(1)}, bf16[4,128,128]{2,1,0:T(8,128)(2,1)S(1)}, u32[]{:S(2)}, u32[]{:S(2)}) collective-permute-start(bf16[4,128,128]{2,1,0:T(8,128)(2,1)S(1)} %fold_states.2.state_ref), channel_id=1, source_target_pairs={{0,8},{1,9},{2,10},{3,11},{4,12},{5,13},{6,14},{7,15},{8,0},{9,1},... | collective-permute-start | bytes 393224 | tf_op jit(solution)/shard_map/ppermute | solution.py:428
  21.9 6.9 %collective-permute-start.5 = (bf16[4,128,128]{2,1,0:T(8,128)(2,1)S(1)}, bf16[4,128,128]{2,1,0:T(8,128)(2,1)S(1)}, u32[]{:S(2)}, u32[]{:S(2)}) collective-permute-start(bf16[4,128,128]{2,1,0:T(8,128)(2,1)S(1)} %double_states.2), channel_id=1, source_target_pairs={{0,24},{1,25},{2,26},{3,27},{4,28},{5,29},{6,30},{7,31},{8,16},{9,... | collective-permute-start | bytes 393224 | tf_op jit(solution)/shard_map/ppermute | solution.py:428
  29.3 6.1 %collective-permute-start.8 = (bf16[4,128,128]{2,1,0:T(8,128)(2,1)S(1)}, bf16[4,128,128]{2,1,0:T(8,128)(2,1)S(1)}, u32[]{:S(2)}, u32[]{:S(2)}) collective-permute-start(bf16[4,128,128]{2,1,0:T(8,128)(2,1)S(1)} %get-tuple-element.118), channel_id=1, source_target_pairs={{0,6},{1,7},{2,4},{3,5},{4,2},{5,3},{6,0},{7,1},{8,14},{9,15},{10,... | collective-permute-start | bytes 393224 | tf_op jit(solution)/shard_map/ppermute | solution.py:428
  32.1 5.0 %collective-permute-start.6 = (bf16[4,128,128]{2,1,0:T(8,128)(2,1)S(1)}, bf16[4,128,128]{2,1,0:T(8,128)(2,1)S(1)}, u32[]{:S(2)}, u32[]{:S(2)}) collective-permute-start(bf16[4,128,128]{2,1,0:T(8,128)(2,1)S(1)} %get-tuple-element.112), channel_id=1, source_target_pairs={{0,2},{1,3},{2,0},{3,1},{4,6},{5,7},{6,4},{7,5},{8,10},{9,11},{10,... | collective-permute-start | bytes 393224 | tf_op jit(solution)/shard_map/ppermute | solution.py:428
  32.6 5.0 %collective-permute-start.7 = (bf16[4,128,128]{2,1,0:T(8,128)(2,1)S(1)}, bf16[4,128,128]{2,1,0:T(8,128)(2,1)S(1)}, u32[]{:S(2)}, u32[]{:S(2)}) collective-permute-start(bf16[4,128,128]{2,1,0:T(8,128)(2,1)S(1)} %get-tuple-element.113), channel_id=1, source_target_pairs={{0,4},{1,5},{2,6},{3,7},{4,0},{5,1},{6,2},{7,3},{8,12},{9,13},{10,... | collective-permute-start | bytes 393224 | tf_op jit(solution)/shard_map/ppermute | solution.py:428
  35.6 3.6 %collective-permute-start.10 = (bf16[8,128,128]{2,1,0:T(8,128)(2,1)S(1)}, bf16[8,128,128]{2,1,0:T(8,128)(2,1)S(1)}, u32[]{:S(2)}, u32[]{:S(2)}) collective-permute-start(bf16[8,128,128]{2,1,0:T(8,128)(2,1)S(1)} %get-tuple-element.123), channel_id=1, source_target_pairs={{0,1},{1,0},{2,3},{3,2},{4,5},{5,4},{6,7},{7,6},{8,9},{9,8},{10,11... | collective-permute-start | bytes 786440 | tf_op jit(solution)/shard_map/ppermute | solution.py:428
  36.4 3.5 %collective-permute-start.12 = (bf16[8,128,128]{2,1,0:T(8,128)(2,1)S(1)}, bf16[8,128,128]{2,1,0:T(8,128)(2,1)S(1)}, u32[]{:S(2)}, u32[]{:S(2)}) collective-permute-start(bf16[8,128,128]{2,1,0:T(8,128)(2,1)S(1)} %get-tuple-element.149), channel_id=1, source_target_pairs={{0,1},{1,0},{2,3},{3,2},{4,5},{5,4},{6,7},{7,6},{8,9},{9,8},{10,11... | collective-permute-start | bytes 786440 | tf_op jit(solution)/shard_map/ppermute | solution.py:428
  37.8 4.3 %collective-permute-start.9 = (bf16[8,128,128]{2,1,0:T(8,128)(2,1)S(1)}, bf16[8,128,128]{2,1,0:T(8,128)(2,1)S(1)}, u32[]{:S(2)}, u32[]{:S(2)}) collective-permute-start(bf16[8,128,128]{2,1,0:T(8,128)(2,1)S(1)} %get-tuple-element.122), channel_id=1, source_target_pairs={{0,1},{1,0},{2,3},{3,2},{4,5},{5,4},{6,7},{7,6},{8,9},{9,8},{10,11... | collective-permute-start | bytes 786440 | tf_op jit(solution)/shard_map/ppermute | solution.py:428
  38.6 4.2 %collective-permute-start.11 = (bf16[8,128,128]{2,1,0:T(8,128)(2,1)S(1)}, bf16[8,128,128]{2,1,0:T(8,128)(2,1)S(1)}, u32[]{:S(2)}, u32[]{:S(2)}) collective-permute-start(bf16[8,128,128]{2,1,0:T(8,128)(2,1)S(1)} %get-tuple-element.147), channel_id=1, source_target_pairs={{0,1},{1,0},{2,3},{3,2},{4,5},{5,4},{6,7},{7,6},{8,9},{9,8},{10,11... | collective-permute-start | bytes 786440 | tf_op jit(solution)/shard_map/ppermute | solution.py:428
  40.1 7.0 %collective-permute-start.15 = (bf16[4,128,128]{2,1,0:T(8,128)(2,1)S(1)}, bf16[4,128,128]{2,1,0:T(8,128)(2,1)S(1)}, u32[]{:S(2)}, u32[]{:S(2)}) collective-permute-start(bf16[4,128,128]{2,1,0:T(8,128)(2,1)S(1)} %get-tuple-element.151.rest_0_), channel_id=1, source_target_pairs={{0,6},{1,7},{2,4},{3,5},{4,2},{5,3},{6,0},{7,1},{8,14},{9,15},{10,... | collective-permute-start | bytes 393224 | tf_op jit(solution)/shard_map/ppermute | solution.py:428
  43.0 5.9 %collective-permute-start.13 = (bf16[4,128,128]{2,1,0:T(8,128)(2,1)S(1)}, bf16[4,128,128]{2,1,0:T(8,128)(2,1)S(1)}, u32[]{:S(2)}, u32[]{:S(2)}) collective-permute-start(bf16[4,128,128]{2,1,0:T(8,128)(2,1)S(1)} %get-tuple-element.152), channel_id=1, source_target_pairs={{0,2},{1,3},{2,0},{3,1},{4,6},{5,7},{6,4},{7,5},{8,10},{9,11},{10,... | collective-permute-start | bytes 393224 | tf_op jit(solution)/shard_map/ppermute | solution.py:428
  43.6 5.6 %collective-permute-start.14 = (bf16[4,128,128]{2,1,0:T(8,128)(2,1)S(1)}, bf16[4,128,128]{2,1,0:T(8,128)(2,1)S(1)}, u32[]{:S(2)}, u32[]{:S(2)}) collective-permute-start(bf16[4,128,128]{2,1,0:T(8,128)(2,1)S(1)} %get-tuple-element.153), channel_id=1, source_target_pairs={{0,4},{1,5},{2,6},{3,7},{4,0},{5,1},{6,2},{7,3},{8,12},{9,13},{10,... | collective-permute-start | bytes 393224 | tf_op jit(solution)/shard_map/ppermute | solution.py:428
  49.4 5.9 %collective-permute-start.16 = (bf16[4,128,128]{2,1,0:T(8,128)(2,1)S(1)}, bf16[4,128,128]{2,1,0:T(8,128)(2,1)S(1)}, u32[]{:S(2)}, u32[]{:S(2)}) collective-permute-start(bf16[4,128,128]{2,1,0:T(8,128)(2,1)S(1)} %fold_states.3.state_ref), channel_id=1, source_target_pairs={{0,8},{1,9},{2,10},{3,11},{4,12},{5,13},{6,14},{7,15},{8,0},{9,1},... | collective-permute-start | bytes 393224 | tf_op jit(solution)/shard_map/ppermute | solution.py:428
  55.4 6.9 %collective-permute-start.17 = (bf16[4,128,128]{2,1,0:T(8,128)(2,1)S(1)}, bf16[4,128,128]{2,1,0:T(8,128)(2,1)S(1)}, u32[]{:S(2)}, u32[]{:S(2)}) collective-permute-start(bf16[4,128,128]{2,1,0:T(8,128)(2,1)S(1)} %double_states.3), channel_id=1, source_target_pairs={{0,24},{1,25},{2,26},{3,27},{4,28},{5,29},{6,30},{7,31},{8,16},{9,... | collective-permute-start | bytes 393224 | tf_op jit(solution)/shard_map/ppermute | solution.py:428
  62.8 6.0 %collective-permute-start.20 = (bf16[4,128,128]{2,1,0:T(8,128)(2,1)S(1)}, bf16[4,128,128]{2,1,0:T(8,128)(2,1)S(1)}, u32[]{:S(2)}, u32[]{:S(2)}) collective-permute-start(bf16[4,128,128]{2,1,0:T(8,128)(2,1)S(1)} %get-tuple-element.163), channel_id=1, source_target_pairs={{0,6},{1,7},{2,4},{3,5},{4,2},{5,3},{6,0},{7,1},{8,14},{9,15},{10,... | collective-permute-start | bytes 393224 | tf_op jit(solution)/shard_map/ppermute | solution.py:428
  65.3 5.0 %collective-permute-start.18 = (bf16[4,128,128]{2,1,0:T(8,128)(2,1)S(1)}, bf16[4,128,128]{2,1,0:T(8,128)(2,1)S(1)}, u32[]{:S(2)}, u32[]{:S(2)}) collective-permute-start(bf16[4,128,128]{2,1,0:T(8,128)(2,1)S(1)} %get-tuple-element.158), channel_id=1, source_target_pairs={{0,2},{1,3},{2,0},{3,1},{4,6},{5,7},{6,4},{7,5},{8,10},{9,11},{10,... | collective-permute-start | bytes 393224 | tf_op jit(solution)/shard_map/ppermute | solution.py:428
  66.0 5.0 %collective-permute-start.19 = (bf16[4,128,128]{2,1,0:T(8,128)(2,1)S(1)}, bf16[4,128,128]{2,1,0:T(8,128)(2,1)S(1)}, u32[]{:S(2)}, u32[]{:S(2)}) collective-permute-start(bf16[4,128,128]{2,1,0:T(8,128)(2,1)S(1)} %get-tuple-element.159), channel_id=1, source_target_pairs={{0,4},{1,5},{2,6},{3,7},{4,0},{5,1},{6,2},{7,3},{8,12},{9,13},{10,... | collective-permute-start | bytes 393224 | tf_op jit(solution)/shard_map/ppermute | solution.py:428
  69.0 3.0 %collective-permute-start.22 = (bf16[8,128,128]{2,1,0:T(8,128)(2,1)S(1)}, bf16[8,128,128]{2,1,0:T(8,128)(2,1)S(1)}, u32[]{:S(2)}, u32[]{:S(2)}) collective-permute-start(bf16[8,128,128]{2,1,0:T(8,128)(2,1)S(1)} %get-tuple-element.175), channel_id=1, source_target_pairs={{0,1},{1,0},{2,3},{3,2},{4,5},{5,4},{6,7},{7,6},{8,9},{9,8},{10,11... | collective-permute-start | bytes 786440 | tf_op jit(solution)/shard_map/ppermute | solution.py:428
  71.2 1.6 %collective-permute-start.21 = (bf16[8,128,128]{2,1,0:T(8,128)(2,1)S(1)}, bf16[8,128,128]{2,1,0:T(8,128)(2,1)S(1)}, u32[]{:S(2)}, u32[]{:S(2)}) collective-permute-start(bf16[8,128,128]{2,1,0:T(8,128)(2,1)S(1)} %get-tuple-element.167), channel_id=1, source_target_pairs={{0,1},{1,0},{2,3},{3,2},{4,5},{5,4},{6,7},{7,6},{8,9},{9,8},{10,11... | collective-permute-start | bytes 786440 | tf_op jit(solution)/shard_map/ppermute | solution.py:428
  (3 other events, 6.4 us)

commit v5 on v4

--- a/solution.py
+++ b/solution.py
@@ -78,31 +78,31 @@
     return [range(start, start + size) for start in range(0, heads, size)]
 
 
-def local_states(ks, vs, rates, kt_ref, vt_ref, s_ref):
-    heads, length, size = kt_ref.shape
+def local_states(key, value, rate_ref, first, s_ref):
+    heads, length, size = key.shape
     tail_steps = length - 1.0 - positions((length, size))
     for batch in batches(heads):
-        key = [one_head(ks, h, length, heads) for h in batch]
-        value = [one_head(vs, h, length, heads).astype(BF16) for h in batch]
-        tail = [decay(rates[h], tail_steps) for h in batch]
-        decayed = [(k * t).astype(BF16) for k, t in zip(key, tail)]
-        state = [dot(k, v, ATB) for k, v in zip(decayed, value)]
+        tail = [decay(rate_ref[pl.ds(first + h, 1), :], tail_steps) for h in batch]
+        decayed = [(key[h].astype(F32) * t).astype(BF16) for h, t in zip(batch, tail)]
+        state = [dot(k, value[h], ATB) for h, k in zip(batch, decayed)]
         for i, h in enumerate(batch):
-            kt_ref[h] = key[i].astype(BF16)
-            vt_ref[h] = value[i]
             s_ref[h] = state[i].astype(BF16)
 
 
-def first_local_kernel(k_ref, v_ref, rates_ref, kt_ref, vt_ref, s_ref, k_rest, v_rest, rates_out, *scratch):
-    kb, vb, ks, vs, rates, sems, rest_sems, rate_sem = scratch
+def to_heads(flat, out_ref):
+    heads, length, _ = out_ref.shape
+    for h in range(heads):
+        out_ref[h] = one_head(flat, h, length, heads).astype(BF16)
+
+
+def bring_kernel(k_ref, v_ref, kt_ref, vt_ref, k_rest, v_rest, *scratch):
+    kb, vb, ks, vs, sems, rest_sems = scratch
     length, heads, size = kb.shape
     half = head_half(False)
     start = pl.multiple_of(half * heads, heads)
     rest = pl.multiple_of((1 - half) * heads, heads)
     chunks = sems.shape[1]
     rows = length // chunks
-    rate_copy = pltpu.make_async_copy(rates_ref, rates, rate_sem)
-    rate_copy.start()
     copies = []
     for c in range(chunks):
         piece = pl.ds(c * rows, rows)
@@ -122,21 +122,23 @@
         ks[flat, :] = kb[piece].astype(F32).reshape(rows * heads, size)
         copies[2 * c + 1].wait()
         vs[flat, :] = vb[piece].astype(F32).reshape(rows * heads, size)
-    rate_copy.wait()
-    for h in range(rates.shape[0]):
-        rates_out[pl.ds(h, 1), :] = jnp.full((1, size), rates[h], F32)
-    local_states(ks, vs, [rates[start + h] for h in range(heads)], kt_ref, vt_ref, s_ref)
+    to_heads(ks, kt_ref)
+    to_heads(vs, vt_ref)
     for copy in rest_copies:
         copy.wait()
 
 
+def first_local_kernel(kt_ref, vt_ref, rate_ref, s_ref):
+    local_states(kt_ref, vt_ref, rate_ref, head_half(False) * kt_ref.shape[0], s_ref)
+
+
 def second_local_kernel(k_ref, v_ref, rate_ref, kt_ref, vt_ref, s_ref, ks, vs):
     heads, length, size = kt_ref.shape
-    first = head_half(True) * heads
     ks[...] = k_ref[...].astype(F32).reshape(length * heads, size)
     vs[...] = v_ref[...].astype(F32).reshape(length * heads, size)
-    rates = [rate_ref[pl.ds(first + h, 1), :] for h in range(heads)]
-    local_states(ks, vs, rates, kt_ref, vt_ref, s_ref)
+    to_heads(ks, kt_ref)
+    to_heads(vs, vt_ref)
+    local_states(kt_ref, vt_ref, rate_ref, head_half(True) * heads, s_ref)
 
 
 def attention_kernel(own, q_ref, g_ref, kt_ref, vt_ref, rate_ref, gain_ref, *rest):
@@ -245,8 +247,9 @@
 
 
 def join_kernel(ks, vs, k_ref, v_ref):
-    k_ref[...] = ks[...].reshape(k_ref.shape).astype(BF16)
-    v_ref[...] = vs[...].reshape(v_ref.shape).astype(BF16)
+    rows = pl.ds(0, k_ref.shape[0] * k_ref.shape[1])
+    k_ref[...] = ks[rows, :].reshape(k_ref.shape).astype(BF16)
+    v_ref[...] = vs[rows, :].reshape(v_ref.shape).astype(BF16)
 
 
 def last_kernel(own, sizes, parts, *refs):
@@ -493,7 +496,7 @@
     part_states = shaped(half // parts, size, size)
     whole = shaped(length, heads, size)
     block = shaped(length, half, size)
-    flat_rows = shaped(length * half, size, dtype=F32)
+    flat_rows = shaped((length + 1) * half, size, dtype=F32)
     flat = pltpu.VMEM((length * half, size), F32)
     stage = pltpu.VMEM((length, half, size), BF16)
     copy_sem = pltpu.SemaphoreType.DMA
@@ -501,13 +504,20 @@
     unit = 2 * half * length * size * size
     span = float(length)
 
-    sent_key, sent_value, sent_state, key_rest, value_rest, rates = call(
+    rates = jnp.broadcast_to(decay_rate[:, None], (heads, size))
+    sent_key, sent_value, key_rest, value_rest = call(
+        bring_kernel,
+        [key_vectors, value_vectors],
+        [per_head, per_head, block, block],
+        [stage, stage, flat, flat, copy_sem((2, 2)), copy_sem((2,))],
+        outside=(0, 1),
+        limit=LOCAL_LIMIT,
+        name="keys_and_values",
+    )
+    (sent_state,) = call(
         first_local_kernel,
-        [key_vectors, value_vectors, decay_rate],
-        [per_head, per_head, states, block, block, shaped(heads, size, dtype=F32)],
-        [stage, stage, flat, flat, pltpu.SMEM((heads,), F32), sems, copy_sem((2,)), copy_sem],
-        outside=(0, 1, 2),
-        limit=LOCAL_LIMIT,
+        [sent_key, sent_value, rates],
+        [states],
         flops=unit,
         name="local_states",
     )
@@ -534,7 +544,7 @@
             name="attention",
         )
     folded = {}
-    for ks in ((parts - 1,), range(parts - 1)):
+    for ks in ((2, 3), (0, 1)):
         inputs = [rates, kept_state, other_state] + list(folded.values())
         parts_here = call(
             functools.partial(pair_fold_kernel, sizes, ks, span, True),

time: 74.8 us -> 72.9 us (0.975)
  waiting for transfers between devices: 22.4 us -> 21.3 us
    ppermute x23, waiting for transfers between devices: 22.4 us -> 21.3 us  [swap(): lax.ppermute(array, AXES, [(i, i ^ distance) for i in range(devices)])]
    pallas_call x31 -> x32, Pallas kernels: 22.5 us -> 22.8 us  [call(): pl.pallas_call(body, in_specs=[ANYWHERE if n in anywhere else OUTSIDE if...]
where the time goes in v5:
time: 72.9 us; the launch traced here: 72.7 us
  starting transfers between devices  27.5 us (38%)
  Pallas kernels  22.8 us (31%)
  waiting for transfers between devices  21.3 us (29%)
  between operations  1.06 us (1%)
    ppermute x23, starting transfers between devices, swap(): lax.ppermute(array, AXES, [(i, i ^ distance) for i in range(devices)])  27.5 us
    pallas_call x32, Pallas kernels, call(): pl.pallas_call(body, in_specs=[ANYWHERE if n in anywhere else OUTSIDE if...  22.8 us
    ppermute x23, waiting for transfers between devices, swap(): lax.ppermute(array, AXES, [(i, i ^ distance) for i in range(devices)])  21.3 us
  transfers between devices with their start and end apart: 23, of which 17 were waited for; matrix products, arithmetic and copies ran while one was open for 0% of the time, Pallas kernels for 23%

profile of v5, /device:TPU:0, one launch (start us, length us, event | category | flops | bytes accessed | tf_op | source)
XLA Modules:
  0.0 72.7 jit_solution(10503757248184099823)
XLA Ops:
  0.6 2.1 %keys_and_values.1 = (bf16[16,128,128]{2,1,0:T(8,128)(2,1)S(1)}, bf16[16,128,128]{2,1,0:T(8,128)(2,1)S(1)}, bf16[128,16,128]{2,1,0:T(8,128)(2,1)S(1)}, bf16[128,16,128]{2,1,0:T(8,128)(2,1)S(1)}) custom-call(bf16[128,32,128]{2,1,0:T(8,128)(2,1)} %k_ref.1, bf16[128,32,128]{2,1,0:T(8,128)(2,1)} %v_ref.1), custom_call_target="tpu_custom_call" | custom-call | bytes 4194304 | tf_op jit(solution)/shard_map/keys_and_values/pallas_call | solution.py:408
  5.4 3.0 %collective-permute-start.2 = (bf16[4,128,128]{2,1,0:T(8,128)(2,1)S(1)}, bf16[4,128,128]{2,1,0:T(8,128)(2,1)S(1)}, u32[]{:S(2)}, u32[]{:S(2)}) collective-permute-start(bf16[4,128,128]{2,1,0:T(8,128)(2,1)S(1)} %get-tuple-element.105.rest_0_), channel_id=1, source_target_pairs={{0,4},{1,5},{2,6},{3,7},{4,0},{5,1},{6,2},{7,3},{8,12},{9,13},{10,... | collective-permute-start | bytes 393224 | tf_op jit(solution)/shard_map/ppermute | solution.py:431
  8.4 1.4 %collective-permute-start.3 = (bf16[4,128,128]{2,1,0:T(8,128)(2,1)S(1)}, bf16[4,128,128]{2,1,0:T(8,128)(2,1)S(1)}, u32[]{:S(2)}, u32[]{:S(2)}) collective-permute-start(bf16[4,128,128]{2,1,0:T(8,128)(2,1)S(1)} %get-tuple-element.106.rest_1_), channel_id=1, source_target_pairs={{0,6},{1,7},{2,4},{3,5},{4,2},{5,3},{6,0},{7,1},{8,14},{9,15},{10,... | collective-permute-start | bytes 393224 | tf_op jit(solution)/shard_map/ppermute | solution.py:431
  10.1 1.4 %attention.2 = (bf16[16,128,128]{2,1,0:T(8,128)(2,1)S(1)}, bf16[16,128,128]{2,1,0:T(8,128)(2,1)S(1)}, bf16[16,128,128]{2,1,0:T(8,128)(2,1)S(1)}, f32[16,128,128]...) custom-call(bf16[128,32,128]{2,1,0:T(8,128)(2,1)S(1)} %copy-done, ...), custom_call_target="tpu_custom_call" | custom-call | flops 134217728 | bytes 7389184 | tf_op jit(solution)/shard_map/attention/pallas_call | solution.py:408
  11.6 2.8 %collective-permute-done.2.refs_2_ = bf16[4,128,128]{2,1,0:T(8,128)(2,1)S(1)} collective-permute-done((bf16[4,128,128]{2,1,0:T(8,128)(2,1)S(1)}, bf16[4,128,128]{2,1,0:T(8,128)(2,1)S(1)}, u32[]{:S(2)}, u32[]{:S(2)}) %collective-permute-start.2) | collective-permute-done | bytes 131104 | tf_op jit(solution)/shard_map/ppermute | solution.py:431
  14.3 1.3 %collective-permute-done.3.refs_3_ = bf16[4,128,128]{2,1,0:T(8,128)(2,1)S(1)} collective-permute-done((bf16[4,128,128]{2,1,0:T(8,128)(2,1)S(1)}, bf16[4,128,128]{2,1,0:T(8,128)(2,1)S(1)}, u32[]{:S(2)}, u32[]{:S(2)}) %collective-permute-start.3) | collective-permute-done | bytes 131104 | tf_op jit(solution)/shard_map/ppermute | solution.py:431
  16.5 1.8 %collective-permute-start.4 = (bf16[4,128,128]{2,1,0:T(8,128)(2,1)S(1)}, bf16[4,128,128]{2,1,0:T(8,128)(2,1)S(1)}, u32[]{:S(2)}, u32[]{:S(2)}) collective-permute-start(bf16[4,128,128]{2,1,0:T(8,128)(2,1)S(1)} %fold_states.2.state_ref), channel_id=1, source_target_pairs={{0,8},{1,9},{2,10},{3,11},{4,12},{5,13},{6,14},{7,15},{8,0},{9,1},... | collective-permute-start | bytes 393224 | tf_op jit(solution)/shard_map/ppermute | solution.py:431
  18.2 3.2 %collective-permute-done.4.other_ref.refs_4_ = bf16[4,128,128]{2,1,0:T(8,128)(2,1)S(1)} collective-permute-done((bf16[4,128,128]{2,1,0:T(8,128)(2,1)S(1)}, bf16[4,128,128]{2,1,0:T(8,128)(2,1)S(1)}, u32[]{:S(2)}, u32[]{:S(2)}) %collective-permute-start.4) | collective-permute-done | bytes 131104 | tf_op jit(solution)/shard_map/ppermute | solution.py:431
  21.6 3.8 %collective-permute-start.5 = (bf16[4,128,128]{2,1,0:T(8,128)(2,1)S(1)}, bf16[4,128,128]{2,1,0:T(8,128)(2,1)S(1)}, u32[]{:S(2)}, u32[]{:S(2)}) collective-permute-start(bf16[4,128,128]{2,1,0:T(8,128)(2,1)S(1)} %double_states.2), channel_id=1, source_target_pairs={{0,24},{1,25},{2,26},{3,27},{4,28},{5,29},{6,30},{7,31},{8,16},{9,... | collective-permute-start | bytes 393224 | tf_op jit(solution)/shard_map/ppermute | solution.py:431
  25.4 1.4 %attention.3 = (bf16[16,128,128]{2,1,0:T(8,128)(2,1)S(1)}, bf16[16,128,128]{2,1,0:T(8,128)(2,1)S(1)}, bf16[16,128,128]{2,1,0:T(8,128)(2,1)S(1)}, f32[16,128,128]...) custom-call(bf16[128,32,128]{2,1,0:T(8,128)(2,1)S(1)} %copy-done, ...), custom_call_target="tpu_custom_call" | custom-call | flops 134217728 | bytes 7389184 | tf_op jit(solution)/shard_map/attention/pallas_call | solution.py:408
  26.8 1.7 %collective-permute-done.5.refs_5_ = bf16[4,128,128]{2,1,0:T(8,128)(2,1)S(1)} collective-permute-done((bf16[4,128,128]{2,1,0:T(8,128)(2,1)S(1)}, bf16[4,128,128]{2,1,0:T(8,128)(2,1)S(1)}, u32[]{:S(2)}, u32[]{:S(2)}) %collective-permute-start.5) | collective-permute-done | bytes 131104 | tf_op jit(solution)/shard_map/ppermute | solution.py:431
  29.0 2.7 %collective-permute-start.8 = (bf16[4,128,128]{2,1,0:T(8,128)(2,1)S(1)}, bf16[4,128,128]{2,1,0:T(8,128)(2,1)S(1)}, u32[]{:S(2)}, u32[]{:S(2)}) collective-permute-start(bf16[4,128,128]{2,1,0:T(8,128)(2,1)S(1)} %get-tuple-element.116), channel_id=1, source_target_pairs={{0,6},{1,7},{2,4},{3,5},{4,2},{5,3},{6,0},{7,1},{8,14},{9,15},{10,... | collective-permute-start | bytes 393224 | tf_op jit(solution)/shard_map/ppermute | solution.py:431
  32.5 2.4 %collective-permute-done.8.rest_1_ = bf16[4,128,128]{2,1,0:T(8,128)(2,1)S(1)} collective-permute-done((bf16[4,128,128]{2,1,0:T(8,128)(2,1)S(1)}, bf16[4,128,128]{2,1,0:T(8,128)(2,1)S(1)}, u32[]{:S(2)}, u32[]{:S(2)}) %collective-permute-start.8) | collective-permute-done | bytes 131104 | tf_op jit(solution)/shard_map/ppermute | solution.py:431
  39.6 2.0 %collective-permute-start.15 = (bf16[4,128,128]{2,1,0:T(8,128)(2,1)S(1)}, bf16[4,128,128]{2,1,0:T(8,128)(2,1)S(1)}, u32[]{:S(2)}, u32[]{:S(2)}) collective-permute-start(bf16[4,128,128]{2,1,0:T(8,128)(2,1)S(1)} %get-tuple-element.149.rest_0_), channel_id=1, source_target_pairs={{0,6},{1,7},{2,4},{3,5},{4,2},{5,3},{6,0},{7,1},{8,14},{9,15},{10,... | collective-permute-start | bytes 393224 | tf_op jit(solution)/shard_map/ppermute | solution.py:431
  45.2 1.3 %inner_gradients.2 = (bf16[16,128,128]{2,1,0:T(8,128)(2,1)S(1)}, f32[16,128,128]{2,1,0:T(8,128)S(1)}, f32[16,128,128]{2,1,0:T(8,128)S(1)}, bf16[16,128,128]{2,1,0:T(8,128)(2,1)S(1)}, bf16[16,128,128]{2,1,0:T(8,128)(2,1)S(1)}) custom-call(bf16[16,128,128]{2,1,0:T(8,128)(2,1)S(1)} %get-tuple-element.98.qt_ref, ...), custom_call_target="tpu_custom_call" | custom-call | flops 201326592 | bytes 6307840 | tf_op jit(solution)/shard_map/inner_gradients/pallas_call | solution.py:408
  46.6 1.8 %collective-permute-done.13.refs_1_ = bf16[4,128,128]{2,1,0:T(8,128)(2,1)S(1)} collective-permute-done((bf16[4,128,128]{2,1,0:T(8,128)(2,1)S(1)}, bf16[4,128,128]{2,1,0:T(8,128)(2,1)S(1)}, u32[]{:S(2)}, u32[]{:S(2)}) %collective-permute-start.13) | collective-permute-done | bytes 131104 | tf_op jit(solution)/shard_map/ppermute | solution.py:431
  49.0 1.1 %collective-permute-start.16 = (bf16[4,128,128]{2,1,0:T(8,128)(2,1)S(1)}, bf16[4,128,128]{2,1,0:T(8,128)(2,1)S(1)}, u32[]{:S(2)}, u32[]{:S(2)}) collective-permute-start(bf16[4,128,128]{2,1,0:T(8,128)(2,1)S(1)} %fold_states.3.state_ref), channel_id=1, source_target_pairs={{0,8},{1,9},{2,10},{3,11},{4,12},{5,13},{6,14},{7,15},{8,0},{9,1},... | collective-permute-start | bytes 393224 | tf_op jit(solution)/shard_map/ppermute | solution.py:431
  50.1 2.4 %query_gradient.2 = (bf16[128,32,128]{2,1,0:T(8,128)(2,1)}, bf16[128,32,128]{2,1,0:T(8,128)(2,1)}, f32[8,128]{1,0:T(8,128)S(1)}) custom-call(bf16[16,128,128]{2,1,0:T(8,128)(2,1)S(1)} %get-tuple-element.95.kt_ref, bf16[16,128,128]{2,1,0:T(8,128)(2,1)S(1)} %get-tuple-element.135.gs_ref, bf16[16,128,128]{2,1,0:T(8,128)(2,1)S(1)} %get-tuple-element.134.go_ref, ...), custom_call_target="tpu_custom_call" | custom-call | flops 134217728 | bytes 4739072 | tf_op jit(solution)/shard_map/query_gradient/pallas_call | solution.py:408
  52.5 1.5 %collective-permute-done.16.other_ref.refs_4_ = bf16[4,128,128]{2,1,0:T(8,128)(2,1)S(1)} collective-permute-done((bf16[4,128,128]{2,1,0:T(8,128)(2,1)S(1)}, bf16[4,128,128]{2,1,0:T(8,128)(2,1)S(1)}, u32[]{:S(2)}, u32[]{:S(2)}) %collective-permute-start.16) | collective-permute-done | bytes 131104 | tf_op jit(solution)/shard_map/ppermute | solution.py:431
  54.1 3.6 %collective-permute-start.17 = (bf16[4,128,128]{2,1,0:T(8,128)(2,1)S(1)}, bf16[4,128,128]{2,1,0:T(8,128)(2,1)S(1)}, u32[]{:S(2)}, u32[]{:S(2)}) collective-permute-start(bf16[4,128,128]{2,1,0:T(8,128)(2,1)S(1)} %double_states.3), channel_id=1, source_target_pairs={{0,24},{1,25},{2,26},{3,27},{4,28},{5,29},{6,30},{7,31},{8,16},{9,... | collective-permute-start | bytes 393224 | tf_op jit(solution)/shard_map/ppermute | solution.py:431
  57.7 2.4 %query_gradient.3 = (bf16[128,32,128]{2,1,0:T(8,128)(2,1)}, bf16[128,32,128]{2,1,0:T(8,128)(2,1)}, f32[8,128]{1,0:T(8,128)S(1)}) custom-call(bf16[16,128,128]{2,1,0:T(8,128)(2,1)S(1)} %get-tuple-element.91.kt_ref, bf16[16,128,128]{2,1,0:T(8,128)(2,1)S(1)} %get-tuple-element.126.gs_ref, ...), custom_call_target="tpu_custom_call", output_to_operand_aliasing={{0}: (6, {}), {1}: (7, {})} | custom-call | flops 134217728 | bytes 6836224 | tf_op jit(solution)/shard_map/query_gradient/pallas_call | solution.py:408
  61.5 2.1 %collective-permute-start.20 = (bf16[4,128,128]{2,1,0:T(8,128)(2,1)S(1)}, bf16[4,128,128]{2,1,0:T(8,128)(2,1)S(1)}, u32[]{:S(2)}, u32[]{:S(2)}) collective-permute-start(bf16[4,128,128]{2,1,0:T(8,128)(2,1)S(1)} %get-tuple-element.161), channel_id=1, source_target_pairs={{0,6},{1,7},{2,4},{3,5},{4,2},{5,3},{6,0},{7,1},{8,14},{9,15},{10,... | collective-permute-start | bytes 393224 | tf_op jit(solution)/shard_map/ppermute | solution.py:431
  65.0 2.4 %collective-permute-done.20.rest_1_ = bf16[4,128,128]{2,1,0:T(8,128)(2,1)S(1)} collective-permute-done((bf16[4,128,128]{2,1,0:T(8,128)(2,1)S(1)}, bf16[4,128,128]{2,1,0:T(8,128)(2,1)S(1)}, u32[]{:S(2)}, u32[]{:S(2)}) %collective-permute-start.20) | collective-permute-done | bytes 131104 | tf_op jit(solution)/shard_map/ppermute | solution.py:431
  70.9 1.7 %last_gradients.1 = (bf16[128,32,128]{2,1,0:T(8,128)(2,1)}, bf16[128,32,128]{2,1,0:T(8,128)(2,1)}, f32[2064,128]{1,0:T(8,128)S(1)}, f32[2064,128]{1,0:T(8,128)S(1)}) custom-call(bf16[16,128,128]{2,1,0:T(8,128)(2,1)S(1)} %get-tuple-element.142.refs_0_, ...), custom_call_target="tpu_custom_call", output_to_operand_aliasing={{2}: (7, {}), {3}: (8, {})} | custom-call | flops 67108864 | bytes 10780672 | tf_op jit(solution)/shard_map/last_gradients/pallas_call | solution.py:408
  (63 shorter events, 20.4 us)
Async XLA Ops:
  3.3 2.1 %collective-permute-start = (bf16[16,128,128]{2,1,0:T(8,128)(2,1)S(1)}, bf16[16,128,128]{2,1,0:T(8,128)(2,1)S(1)}, u32[]{:S(2)}, u32[]{:S(2)}) collective-permute-start(bf16[16,128,128]{2,1,0:T(8,128)(2,1)S(1)} %local_states.3), channel_id=1, source_target_pairs={{0,1},{1,0},{2,3},{3,2},{4,5},{5,4},{6,7},{7,6},{8,9},{9,8},{10,11... | collective-permute-start | bytes 1572872 | tf_op jit(solution)/shard_map/ppermute | solution.py:431
  5.3 4.8 %copy-start.2 = (f32[32,128]{1,0:T(8,128)S(1)}, f32[32,128]{1,0:T(8,128)}, u32[]{:S(2)}) copy-start(f32[32,128]{1,0:T(8,128)} %gain_ref.1) | copy-start | bytes 49156
  5.4 8.9 %collective-permute-start.2 = (bf16[4,128,128]{2,1,0:T(8,128)(2,1)S(1)}, bf16[4,128,128]{2,1,0:T(8,128)(2,1)S(1)}, u32[]{:S(2)}, u32[]{:S(2)}) collective-permute-start(bf16[4,128,128]{2,1,0:T(8,128)(2,1)S(1)} %get-tuple-element.105.rest_0_), channel_id=1, source_target_pairs={{0,4},{1,5},{2,6},{3,7},{4,0},{5,1},{6,2},{7,3},{8,12},{9,13},{10,... | collective-permute-start | bytes 393224 | tf_op jit(solution)/shard_map/ppermute | solution.py:431
  8.4 7.3 %collective-permute-start.3 = (bf16[4,128,128]{2,1,0:T(8,128)(2,1)S(1)}, bf16[4,128,128]{2,1,0:T(8,128)(2,1)S(1)}, u32[]{:S(2)}, u32[]{:S(2)}) collective-permute-start(bf16[4,128,128]{2,1,0:T(8,128)(2,1)S(1)} %get-tuple-element.106.rest_1_), channel_id=1, source_target_pairs={{0,6},{1,7},{2,4},{3,5},{4,2},{5,3},{6,0},{7,1},{8,14},{9,15},{10,... | collective-permute-start | bytes 393224 | tf_op jit(solution)/shard_map/ppermute | solution.py:431
  10.0 6.3 %collective-permute-start.1 = (bf16[4,128,128]{2,1,0:T(8,128)(2,1)S(1)}, bf16[4,128,128]{2,1,0:T(8,128)(2,1)S(1)}, u32[]{:S(2)}, u32[]{:S(2)}) collective-permute-start(bf16[4,128,128]{2,1,0:T(8,128)(2,1)S(1)} %get-tuple-element.108), channel_id=1, source_target_pairs={{0,2},{1,3},{2,0},{3,1},{4,6},{5,7},{6,4},{7,5},{8,10},{9,11},{10,... | collective-permute-start | bytes 393224 | tf_op jit(solution)/shard_map/ppermute | solution.py:431
  16.5 5.0 %collective-permute-start.4 = (bf16[4,128,128]{2,1,0:T(8,128)(2,1)S(1)}, bf16[4,128,128]{2,1,0:T(8,128)(2,1)S(1)}, u32[]{:S(2)}, u32[]{:S(2)}) collective-permute-start(bf16[4,128,128]{2,1,0:T(8,128)(2,1)S(1)} %fold_states.2.state_ref), channel_id=1, source_target_pairs={{0,8},{1,9},{2,10},{3,11},{4,12},{5,13},{6,14},{7,15},{8,0},{9,1},... | collective-permute-start | bytes 393224 | tf_op jit(solution)/shard_map/ppermute | solution.py:431
  21.6 6.9 %collective-permute-start.5 = (bf16[4,128,128]{2,1,0:T(8,128)(2,1)S(1)}, bf16[4,128,128]{2,1,0:T(8,128)(2,1)S(1)}, u32[]{:S(2)}, u32[]{:S(2)}) collective-permute-start(bf16[4,128,128]{2,1,0:T(8,128)(2,1)S(1)} %double_states.2), channel_id=1, source_target_pairs={{0,24},{1,25},{2,26},{3,27},{4,28},{5,29},{6,30},{7,31},{8,16},{9,... | collective-permute-start | bytes 393224 | tf_op jit(solution)/shard_map/ppermute | solution.py:431
  29.0 5.9 %collective-permute-start.8 = (bf16[4,128,128]{2,1,0:T(8,128)(2,1)S(1)}, bf16[4,128,128]{2,1,0:T(8,128)(2,1)S(1)}, u32[]{:S(2)}, u32[]{:S(2)}) collective-permute-start(bf16[4,128,128]{2,1,0:T(8,128)(2,1)S(1)} %get-tuple-element.116), channel_id=1, source_target_pairs={{0,6},{1,7},{2,4},{3,5},{4,2},{5,3},{6,0},{7,1},{8,14},{9,15},{10,... | collective-permute-start | bytes 393224 | tf_op jit(solution)/shard_map/ppermute | solution.py:431
  31.6 5.0 %collective-permute-start.6 = (bf16[4,128,128]{2,1,0:T(8,128)(2,1)S(1)}, bf16[4,128,128]{2,1,0:T(8,128)(2,1)S(1)}, u32[]{:S(2)}, u32[]{:S(2)}) collective-permute-start(bf16[4,128,128]{2,1,0:T(8,128)(2,1)S(1)} %get-tuple-element.110), channel_id=1, source_target_pairs={{0,2},{1,3},{2,0},{3,1},{4,6},{5,7},{6,4},{7,5},{8,10},{9,11},{10,... | collective-permute-start | bytes 393224 | tf_op jit(solution)/shard_map/ppermute | solution.py:431
  32.2 5.0 %collective-permute-start.7 = (bf16[4,128,128]{2,1,0:T(8,128)(2,1)S(1)}, bf16[4,128,128]{2,1,0:T(8,128)(2,1)S(1)}, u32[]{:S(2)}, u32[]{:S(2)}) collective-permute-start(bf16[4,128,128]{2,1,0:T(8,128)(2,1)S(1)} %get-tuple-element.111), channel_id=1, source_target_pairs={{0,4},{1,5},{2,6},{3,7},{4,0},{5,1},{6,2},{7,3},{8,12},{9,13},{10,... | collective-permute-start | bytes 393224 | tf_op jit(solution)/shard_map/ppermute | solution.py:431
  35.1 3.6 %collective-permute-start.10 = (bf16[8,128,128]{2,1,0:T(8,128)(2,1)S(1)}, bf16[8,128,128]{2,1,0:T(8,128)(2,1)S(1)}, u32[]{:S(2)}, u32[]{:S(2)}) collective-permute-start(bf16[8,128,128]{2,1,0:T(8,128)(2,1)S(1)} %get-tuple-element.121), channel_id=1, source_target_pairs={{0,1},{1,0},{2,3},{3,2},{4,5},{5,4},{6,7},{7,6},{8,9},{9,8},{10,11... | collective-permute-start | bytes 786440 | tf_op jit(solution)/shard_map/ppermute | solution.py:431
  35.9 3.6 %collective-permute-start.12 = (bf16[8,128,128]{2,1,0:T(8,128)(2,1)S(1)}, bf16[8,128,128]{2,1,0:T(8,128)(2,1)S(1)}, u32[]{:S(2)}, u32[]{:S(2)}) collective-permute-start(bf16[8,128,128]{2,1,0:T(8,128)(2,1)S(1)} %get-tuple-element.147), channel_id=1, source_target_pairs={{0,1},{1,0},{2,3},{3,2},{4,5},{5,4},{6,7},{7,6},{8,9},{9,8},{10,11... | collective-permute-start | bytes 786440 | tf_op jit(solution)/shard_map/ppermute | solution.py:431
  37.3 4.3 %collective-permute-start.9 = (bf16[8,128,128]{2,1,0:T(8,128)(2,1)S(1)}, bf16[8,128,128]{2,1,0:T(8,128)(2,1)S(1)}, u32[]{:S(2)}, u32[]{:S(2)}) collective-permute-start(bf16[8,128,128]{2,1,0:T(8,128)(2,1)S(1)} %get-tuple-element.120), channel_id=1, source_target_pairs={{0,1},{1,0},{2,3},{3,2},{4,5},{5,4},{6,7},{7,6},{8,9},{9,8},{10,11... | collective-permute-start | bytes 786440 | tf_op jit(solution)/shard_map/ppermute | solution.py:431
  38.2 4.3 %collective-permute-start.11 = (bf16[8,128,128]{2,1,0:T(8,128)(2,1)S(1)}, bf16[8,128,128]{2,1,0:T(8,128)(2,1)S(1)}, u32[]{:S(2)}, u32[]{:S(2)}) collective-permute-start(bf16[8,128,128]{2,1,0:T(8,128)(2,1)S(1)} %get-tuple-element.145), channel_id=1, source_target_pairs={{0,1},{1,0},{2,3},{3,2},{4,5},{5,4},{6,7},{7,6},{8,9},{9,8},{10,11... | collective-permute-start | bytes 786440 | tf_op jit(solution)/shard_map/ppermute | solution.py:431
  39.6 7.0 %collective-permute-start.15 = (bf16[4,128,128]{2,1,0:T(8,128)(2,1)S(1)}, bf16[4,128,128]{2,1,0:T(8,128)(2,1)S(1)}, u32[]{:S(2)}, u32[]{:S(2)}) collective-permute-start(bf16[4,128,128]{2,1,0:T(8,128)(2,1)S(1)} %get-tuple-element.149.rest_0_), channel_id=1, source_target_pairs={{0,6},{1,7},{2,4},{3,5},{4,2},{5,3},{6,0},{7,1},{8,14},{9,15},{10,... | collective-permute-start | bytes 393224 | tf_op jit(solution)/shard_map/ppermute | solution.py:431
  42.6 5.9 %collective-permute-start.13 = (bf16[4,128,128]{2,1,0:T(8,128)(2,1)S(1)}, bf16[4,128,128]{2,1,0:T(8,128)(2,1)S(1)}, u32[]{:S(2)}, u32[]{:S(2)}) collective-permute-start(bf16[4,128,128]{2,1,0:T(8,128)(2,1)S(1)} %get-tuple-element.150), channel_id=1, source_target_pairs={{0,2},{1,3},{2,0},{3,1},{4,6},{5,7},{6,4},{7,5},{8,10},{9,11},{10,... | collective-permute-start | bytes 393224 | tf_op jit(solution)/shard_map/ppermute | solution.py:431
  43.2 5.6 %collective-permute-start.14 = (bf16[4,128,128]{2,1,0:T(8,128)(2,1)S(1)}, bf16[4,128,128]{2,1,0:T(8,128)(2,1)S(1)}, u32[]{:S(2)}, u32[]{:S(2)}) collective-permute-start(bf16[4,128,128]{2,1,0:T(8,128)(2,1)S(1)} %get-tuple-element.151), channel_id=1, source_target_pairs={{0,4},{1,5},{2,6},{3,7},{4,0},{5,1},{6,2},{7,3},{8,12},{9,13},{10,... | collective-permute-start | bytes 393224 | tf_op jit(solution)/shard_map/ppermute | solution.py:431
  49.0 5.0 %collective-permute-start.16 = (bf16[4,128,128]{2,1,0:T(8,128)(2,1)S(1)}, bf16[4,128,128]{2,1,0:T(8,128)(2,1)S(1)}, u32[]{:S(2)}, u32[]{:S(2)}) collective-permute-start(bf16[4,128,128]{2,1,0:T(8,128)(2,1)S(1)} %fold_states.3.state_ref), channel_id=1, source_target_pairs={{0,8},{1,9},{2,10},{3,11},{4,12},{5,13},{6,14},{7,15},{8,0},{9,1},... | collective-permute-start | bytes 393224 | tf_op jit(solution)/shard_map/ppermute | solution.py:431
  54.1 6.9 %collective-permute-start.17 = (bf16[4,128,128]{2,1,0:T(8,128)(2,1)S(1)}, bf16[4,128,128]{2,1,0:T(8,128)(2,1)S(1)}, u32[]{:S(2)}, u32[]{:S(2)}) collective-permute-start(bf16[4,128,128]{2,1,0:T(8,128)(2,1)S(1)} %double_states.3), channel_id=1, source_target_pairs={{0,24},{1,25},{2,26},{3,27},{4,28},{5,29},{6,30},{7,31},{8,16},{9,... | collective-permute-start | bytes 393224 | tf_op jit(solution)/shard_map/ppermute | solution.py:431
  61.5 5.9 %collective-permute-start.20 = (bf16[4,128,128]{2,1,0:T(8,128)(2,1)S(1)}, bf16[4,128,128]{2,1,0:T(8,128)(2,1)S(1)}, u32[]{:S(2)}, u32[]{:S(2)}) collective-permute-start(bf16[4,128,128]{2,1,0:T(8,128)(2,1)S(1)} %get-tuple-element.161), channel_id=1, source_target_pairs={{0,6},{1,7},{2,4},{3,5},{4,2},{5,3},{6,0},{7,1},{8,14},{9,15},{10,... | collective-permute-start | bytes 393224 | tf_op jit(solution)/shard_map/ppermute | solution.py:431
  63.6 5.0 %collective-permute-start.18 = (bf16[4,128,128]{2,1,0:T(8,128)(2,1)S(1)}, bf16[4,128,128]{2,1,0:T(8,128)(2,1)S(1)}, u32[]{:S(2)}, u32[]{:S(2)}) collective-permute-start(bf16[4,128,128]{2,1,0:T(8,128)(2,1)S(1)} %get-tuple-element.156), channel_id=1, source_target_pairs={{0,2},{1,3},{2,0},{3,1},{4,6},{5,7},{6,4},{7,5},{8,10},{9,11},{10,... | collective-permute-start | bytes 393224 | tf_op jit(solution)/shard_map/ppermute | solution.py:431
  64.1 5.0 %collective-permute-start.19 = (bf16[4,128,128]{2,1,0:T(8,128)(2,1)S(1)}, bf16[4,128,128]{2,1,0:T(8,128)(2,1)S(1)}, u32[]{:S(2)}, u32[]{:S(2)}) collective-permute-start(bf16[4,128,128]{2,1,0:T(8,128)(2,1)S(1)} %get-tuple-element.157), channel_id=1, source_target_pairs={{0,4},{1,5},{2,6},{3,7},{4,0},{5,1},{6,2},{7,3},{8,12},{9,13},{10,... | collective-permute-start | bytes 393224 | tf_op jit(solution)/shard_map/ppermute | solution.py:431
  67.6 2.4 %collective-permute-start.22 = (bf16[8,128,128]{2,1,0:T(8,128)(2,1)S(1)}, bf16[8,128,128]{2,1,0:T(8,128)(2,1)S(1)}, u32[]{:S(2)}, u32[]{:S(2)}) collective-permute-start(bf16[8,128,128]{2,1,0:T(8,128)(2,1)S(1)} %get-tuple-element.173), channel_id=1, source_target_pairs={{0,1},{1,0},{2,3},{3,2},{4,5},{5,4},{6,7},{7,6},{8,9},{9,8},{10,11... | collective-permute-start | bytes 786440 | tf_op jit(solution)/shard_map/ppermute | solution.py:431
  69.3 1.6 %collective-permute-start.21 = (bf16[8,128,128]{2,1,0:T(8,128)(2,1)S(1)}, bf16[8,128,128]{2,1,0:T(8,128)(2,1)S(1)}, u32[]{:S(2)}, u32[]{:S(2)}) collective-permute-start(bf16[8,128,128]{2,1,0:T(8,128)(2,1)S(1)} %get-tuple-element.165), channel_id=1, source_target_pairs={{0,1},{1,0},{2,3},{3,2},{4,5},{5,4},{6,7},{7,6},{8,9},{9,8},{10,11... | collective-permute-start | bytes 786440 | tf_op jit(solution)/shard_map/ppermute | solution.py:431
  (3 other events, 11.8 us)

commit v6 on v5

--- a/solution.py
+++ b/solution.py
@@ -104,9 +104,9 @@
     chunks = sems.shape[1]
     rows = length // chunks
     copies = []
-    for c in range(chunks):
-        piece = pl.ds(c * rows, rows)
-        for n, (ref, buffer) in enumerate(((k_ref, kb), (v_ref, vb))):
+    for n, (ref, buffer) in enumerate(((k_ref, kb), (v_ref, vb))):
+        for c in range(chunks):
+            piece = pl.ds(c * rows, rows)
             copy = pltpu.make_async_copy(ref.at[piece, pl.ds(start, heads), :], buffer.at[piece], sems.at[n, c])
             copy.start()
             copies.append(copy)
@@ -115,15 +115,12 @@
         copy = pltpu.make_async_copy(ref.at[:, pl.ds(rest, heads), :], buffer, rest_sems.at[n])
         copy.start()
         rest_copies.append(copy)
-    for c in range(chunks):
-        piece = pl.ds(c * rows, rows)
-        flat = pl.ds(c * rows * heads, rows * heads)
-        copies[2 * c].wait()
-        ks[flat, :] = kb[piece].astype(F32).reshape(rows * heads, size)
-        copies[2 * c + 1].wait()
-        vs[flat, :] = vb[piece].astype(F32).reshape(rows * heads, size)
-    to_heads(ks, kt_ref)
-    to_heads(vs, vt_ref)
+    for n, (buffer, flat, out) in enumerate(((kb, ks, kt_ref), (vb, vs, vt_ref))):
+        for c in range(chunks):
+            copies[n * chunks + c].wait()
+            piece = pl.ds(c * rows, rows)
+            flat[pl.ds(c * rows * heads, rows * heads), :] = buffer[piece].astype(F32).reshape(rows * heads, size)
+        to_heads(flat, out)
     for copy in rest_copies:
         copy.wait()
 

time: 72.9 us -> 72.6 us (level)
  transfers between devices with their start and end apart: 23 -> 23, of which waited for: 17 -> 17; matrix products, arithmetic and copies ran while one was open for 0% -> 0% of each run, Pallas kernels for 23% -> 24%
where the time goes in v6:
time: 72.6 us; the launch traced here: 72.5 us
  starting transfers between devices  27.5 us (38%)
  Pallas kernels  22.5 us (31%)
  waiting for transfers between devices  21.3 us (29%)
  between operations  1.06 us (1%)
    ppermute x23, starting transfers between devices, swap(): lax.ppermute(array, AXES, [(i, i ^ distance) for i in range(devices)])  27.5 us
    pallas_call x32, Pallas kernels, call(): pl.pallas_call(body, in_specs=[ANYWHERE if n in anywhere else OUTSIDE if...  22.5 us
    ppermute x23, waiting for transfers between devices, swap(): lax.ppermute(array, AXES, [(i, i ^ distance) for i in range(devices)])  21.3 us
  transfers between devices with their start and end apart: 23, of which 17 were waited for; matrix products, arithmetic and copies ran while one was open for 0% of the time, Pallas kernels for 24%

profile of v6, /device:TPU:0, one launch (start us, length us, event | category | flops | bytes accessed | tf_op | source)
XLA Modules:
  0.0 72.5 jit_solution(13911315165339351079)
XLA Ops:
  0.6 1.8 %keys_and_values.1 = (bf16[16,128,128]{2,1,0:T(8,128)(2,1)S(1)}, bf16[16,128,128]{2,1,0:T(8,128)(2,1)S(1)}, bf16[128,16,128]{2,1,0:T(8,128)(2,1)S(1)}, bf16[128,16,128]{2,1,0:T(8,128)(2,1)S(1)}) custom-call(bf16[128,32,128]{2,1,0:T(8,128)(2,1)} %k_ref.1, bf16[128,32,128]{2,1,0:T(8,128)(2,1)} %v_ref.1), custom_call_target="tpu_custom_call" | custom-call | bytes 4194304 | tf_op jit(solution)/shard_map/keys_and_values/pallas_call | solution.py:405
  5.2 3.0 %collective-permute-start.2 = (bf16[4,128,128]{2,1,0:T(8,128)(2,1)S(1)}, bf16[4,128,128]{2,1,0:T(8,128)(2,1)S(1)}, u32[]{:S(2)}, u32[]{:S(2)}) collective-permute-start(bf16[4,128,128]{2,1,0:T(8,128)(2,1)S(1)} %get-tuple-element.105.rest_0_), channel_id=1, source_target_pairs={{0,4},{1,5},{2,6},{3,7},{4,0},{5,1},{6,2},{7,3},{8,12},{9,13},{10,... | collective-permute-start | bytes 393224 | tf_op jit(solution)/shard_map/ppermute | solution.py:428
  8.2 1.4 %collective-permute-start.3 = (bf16[4,128,128]{2,1,0:T(8,128)(2,1)S(1)}, bf16[4,128,128]{2,1,0:T(8,128)(2,1)S(1)}, u32[]{:S(2)}, u32[]{:S(2)}) collective-permute-start(bf16[4,128,128]{2,1,0:T(8,128)(2,1)S(1)} %get-tuple-element.106.rest_1_), channel_id=1, source_target_pairs={{0,6},{1,7},{2,4},{3,5},{4,2},{5,3},{6,0},{7,1},{8,14},{9,15},{10,... | collective-permute-start | bytes 393224 | tf_op jit(solution)/shard_map/ppermute | solution.py:428
  9.9 1.4 %attention.2 = (bf16[16,128,128]{2,1,0:T(8,128)(2,1)S(1)}, bf16[16,128,128]{2,1,0:T(8,128)(2,1)S(1)}, bf16[16,128,128]{2,1,0:T(8,128)(2,1)S(1)}, f32[16,128,128]...) custom-call(bf16[128,32,128]{2,1,0:T(8,128)(2,1)S(1)} %copy-done, ...), custom_call_target="tpu_custom_call" | custom-call | flops 134217728 | bytes 7389184 | tf_op jit(solution)/shard_map/attention/pallas_call | solution.py:405
  11.3 2.8 %collective-permute-done.2.refs_2_ = bf16[4,128,128]{2,1,0:T(8,128)(2,1)S(1)} collective-permute-done((bf16[4,128,128]{2,1,0:T(8,128)(2,1)S(1)}, bf16[4,128,128]{2,1,0:T(8,128)(2,1)S(1)}, u32[]{:S(2)}, u32[]{:S(2)}) %collective-permute-start.2) | collective-permute-done | bytes 131104 | tf_op jit(solution)/shard_map/ppermute | solution.py:428
  14.1 1.3 %collective-permute-done.3.refs_3_ = bf16[4,128,128]{2,1,0:T(8,128)(2,1)S(1)} collective-permute-done((bf16[4,128,128]{2,1,0:T(8,128)(2,1)S(1)}, bf16[4,128,128]{2,1,0:T(8,128)(2,1)S(1)}, u32[]{:S(2)}, u32[]{:S(2)}) %collective-permute-start.3) | collective-permute-done | bytes 131104 | tf_op jit(solution)/shard_map/ppermute | solution.py:428
  16.2 1.8 %collective-permute-start.4 = (bf16[4,128,128]{2,1,0:T(8,128)(2,1)S(1)}, bf16[4,128,128]{2,1,0:T(8,128)(2,1)S(1)}, u32[]{:S(2)}, u32[]{:S(2)}) collective-permute-start(bf16[4,128,128]{2,1,0:T(8,128)(2,1)S(1)} %fold_states.2.state_ref), channel_id=1, source_target_pairs={{0,8},{1,9},{2,10},{3,11},{4,12},{5,13},{6,14},{7,15},{8,0},{9,1},... | collective-permute-start | bytes 393224 | tf_op jit(solution)/shard_map/ppermute | solution.py:428
  18.0 3.2 %collective-permute-done.4.other_ref.refs_4_ = bf16[4,128,128]{2,1,0:T(8,128)(2,1)S(1)} collective-permute-done((bf16[4,128,128]{2,1,0:T(8,128)(2,1)S(1)}, bf16[4,128,128]{2,1,0:T(8,128)(2,1)S(1)}, u32[]{:S(2)}, u32[]{:S(2)}) %collective-permute-start.4) | collective-permute-done | bytes 131104 | tf_op jit(solution)/shard_map/ppermute | solution.py:428
  21.3 3.8 %collective-permute-start.5 = (bf16[4,128,128]{2,1,0:T(8,128)(2,1)S(1)}, bf16[4,128,128]{2,1,0:T(8,128)(2,1)S(1)}, u32[]{:S(2)}, u32[]{:S(2)}) collective-permute-start(bf16[4,128,128]{2,1,0:T(8,128)(2,1)S(1)} %double_states.2), channel_id=1, source_target_pairs={{0,24},{1,25},{2,26},{3,27},{4,28},{5,29},{6,30},{7,31},{8,16},{9,... | collective-permute-start | bytes 393224 | tf_op jit(solution)/shard_map/ppermute | solution.py:428
  25.2 1.4 %attention.3 = (bf16[16,128,128]{2,1,0:T(8,128)(2,1)S(1)}, bf16[16,128,128]{2,1,0:T(8,128)(2,1)S(1)}, bf16[16,128,128]{2,1,0:T(8,128)(2,1)S(1)}, f32[16,128,128]...) custom-call(bf16[128,32,128]{2,1,0:T(8,128)(2,1)S(1)} %copy-done, ...), custom_call_target="tpu_custom_call" | custom-call | flops 134217728 | bytes 7389184 | tf_op jit(solution)/shard_map/attention/pallas_call | solution.py:405
  26.6 1.7 %collective-permute-done.5.refs_5_ = bf16[4,128,128]{2,1,0:T(8,128)(2,1)S(1)} collective-permute-done((bf16[4,128,128]{2,1,0:T(8,128)(2,1)S(1)}, bf16[4,128,128]{2,1,0:T(8,128)(2,1)S(1)}, u32[]{:S(2)}, u32[]{:S(2)}) %collective-permute-start.5) | collective-permute-done | bytes 131104 | tf_op jit(solution)/shard_map/ppermute | solution.py:428
  28.7 2.7 %collective-permute-start.8 = (bf16[4,128,128]{2,1,0:T(8,128)(2,1)S(1)}, bf16[4,128,128]{2,1,0:T(8,128)(2,1)S(1)}, u32[]{:S(2)}, u32[]{:S(2)}) collective-permute-start(bf16[4,128,128]{2,1,0:T(8,128)(2,1)S(1)} %get-tuple-element.116), channel_id=1, source_target_pairs={{0,6},{1,7},{2,4},{3,5},{4,2},{5,3},{6,0},{7,1},{8,14},{9,15},{10,... | collective-permute-start | bytes 393224 | tf_op jit(solution)/shard_map/ppermute | solution.py:428
  32.3 2.4 %collective-permute-done.8.rest_1_ = bf16[4,128,128]{2,1,0:T(8,128)(2,1)S(1)} collective-permute-done((bf16[4,128,128]{2,1,0:T(8,128)(2,1)S(1)}, bf16[4,128,128]{2,1,0:T(8,128)(2,1)S(1)}, u32[]{:S(2)}, u32[]{:S(2)}) %collective-permute-start.8) | collective-permute-done | bytes 131104 | tf_op jit(solution)/shard_map/ppermute | solution.py:428
  39.4 2.0 %collective-permute-start.15 = (bf16[4,128,128]{2,1,0:T(8,128)(2,1)S(1)}, bf16[4,128,128]{2,1,0:T(8,128)(2,1)S(1)}, u32[]{:S(2)}, u32[]{:S(2)}) collective-permute-start(bf16[4,128,128]{2,1,0:T(8,128)(2,1)S(1)} %get-tuple-element.149.rest_0_), channel_id=1, source_target_pairs={{0,6},{1,7},{2,4},{3,5},{4,2},{5,3},{6,0},{7,1},{8,14},{9,15},{10,... | collective-permute-start | bytes 393224 | tf_op jit(solution)/shard_map/ppermute | solution.py:428
  45.0 1.3 %inner_gradients.2 = (bf16[16,128,128]{2,1,0:T(8,128)(2,1)S(1)}, f32[16,128,128]{2,1,0:T(8,128)S(1)}, f32[16,128,128]{2,1,0:T(8,128)S(1)}, bf16[16,128,128]{2,1,0:T(8,128)(2,1)S(1)}, bf16[16,128,128]{2,1,0:T(8,128)(2,1)S(1)}) custom-call(bf16[16,128,128]{2,1,0:T(8,128)(2,1)S(1)} %get-tuple-element.98.qt_ref, ...), custom_call_target="tpu_custom_call" | custom-call | flops 201326592 | bytes 6307840 | tf_op jit(solution)/shard_map/inner_gradients/pallas_call | solution.py:405
  46.4 1.8 %collective-permute-done.13.refs_1_ = bf16[4,128,128]{2,1,0:T(8,128)(2,1)S(1)} collective-permute-done((bf16[4,128,128]{2,1,0:T(8,128)(2,1)S(1)}, bf16[4,128,128]{2,1,0:T(8,128)(2,1)S(1)}, u32[]{:S(2)}, u32[]{:S(2)}) %collective-permute-start.13) | collective-permute-done | bytes 131104 | tf_op jit(solution)/shard_map/ppermute | solution.py:428
  48.7 1.1 %collective-permute-start.16 = (bf16[4,128,128]{2,1,0:T(8,128)(2,1)S(1)}, bf16[4,128,128]{2,1,0:T(8,128)(2,1)S(1)}, u32[]{:S(2)}, u32[]{:S(2)}) collective-permute-start(bf16[4,128,128]{2,1,0:T(8,128)(2,1)S(1)} %fold_states.3.state_ref), channel_id=1, source_target_pairs={{0,8},{1,9},{2,10},{3,11},{4,12},{5,13},{6,14},{7,15},{8,0},{9,1},... | collective-permute-start | bytes 393224 | tf_op jit(solution)/shard_map/ppermute | solution.py:428
  49.9 2.4 %query_gradient.2 = (bf16[128,32,128]{2,1,0:T(8,128)(2,1)}, bf16[128,32,128]{2,1,0:T(8,128)(2,1)}, f32[8,128]{1,0:T(8,128)S(1)}) custom-call(bf16[16,128,128]{2,1,0:T(8,128)(2,1)S(1)} %get-tuple-element.95.kt_ref, bf16[16,128,128]{2,1,0:T(8,128)(2,1)S(1)} %get-tuple-element.135.gs_ref, bf16[16,128,128]{2,1,0:T(8,128)(2,1)S(1)} %get-tuple-element.134.go_ref, ...), custom_call_target="tpu_custom_call" | custom-call | flops 134217728 | bytes 4739072 | tf_op jit(solution)/shard_map/query_gradient/pallas_call | solution.py:405
  52.3 1.5 %collective-permute-done.16.other_ref.refs_4_ = bf16[4,128,128]{2,1,0:T(8,128)(2,1)S(1)} collective-permute-done((bf16[4,128,128]{2,1,0:T(8,128)(2,1)S(1)}, bf16[4,128,128]{2,1,0:T(8,128)(2,1)S(1)}, u32[]{:S(2)}, u32[]{:S(2)}) %collective-permute-start.16) | collective-permute-done | bytes 131104 | tf_op jit(solution)/shard_map/ppermute | solution.py:428
  53.9 3.6 %collective-permute-start.17 = (bf16[4,128,128]{2,1,0:T(8,128)(2,1)S(1)}, bf16[4,128,128]{2,1,0:T(8,128)(2,1)S(1)}, u32[]{:S(2)}, u32[]{:S(2)}) collective-permute-start(bf16[4,128,128]{2,1,0:T(8,128)(2,1)S(1)} %double_states.3), channel_id=1, source_target_pairs={{0,24},{1,25},{2,26},{3,27},{4,28},{5,29},{6,30},{7,31},{8,16},{9,... | collective-permute-start | bytes 393224 | tf_op jit(solution)/shard_map/ppermute | solution.py:428
  57.4 2.4 %query_gradient.3 = (bf16[128,32,128]{2,1,0:T(8,128)(2,1)}, bf16[128,32,128]{2,1,0:T(8,128)(2,1)}, f32[8,128]{1,0:T(8,128)S(1)}) custom-call(bf16[16,128,128]{2,1,0:T(8,128)(2,1)S(1)} %get-tuple-element.91.kt_ref, bf16[16,128,128]{2,1,0:T(8,128)(2,1)S(1)} %get-tuple-element.126.gs_ref, ...), custom_call_target="tpu_custom_call", output_to_operand_aliasing={{0}: (6, {}), {1}: (7, {})} | custom-call | flops 134217728 | bytes 6836224 | tf_op jit(solution)/shard_map/query_gradient/pallas_call | solution.py:405
  61.2 2.1 %collective-permute-start.20 = (bf16[4,128,128]{2,1,0:T(8,128)(2,1)S(1)}, bf16[4,128,128]{2,1,0:T(8,128)(2,1)S(1)}, u32[]{:S(2)}, u32[]{:S(2)}) collective-permute-start(bf16[4,128,128]{2,1,0:T(8,128)(2,1)S(1)} %get-tuple-element.161), channel_id=1, source_target_pairs={{0,6},{1,7},{2,4},{3,5},{4,2},{5,3},{6,0},{7,1},{8,14},{9,15},{10,... | collective-permute-start | bytes 393224 | tf_op jit(solution)/shard_map/ppermute | solution.py:428
  64.8 2.4 %collective-permute-done.20.rest_1_ = bf16[4,128,128]{2,1,0:T(8,128)(2,1)S(1)} collective-permute-done((bf16[4,128,128]{2,1,0:T(8,128)(2,1)S(1)}, bf16[4,128,128]{2,1,0:T(8,128)(2,1)S(1)}, u32[]{:S(2)}, u32[]{:S(2)}) %collective-permute-start.20) | collective-permute-done | bytes 131104 | tf_op jit(solution)/shard_map/ppermute | solution.py:428
  70.6 1.7 %last_gradients.1 = (bf16[128,32,128]{2,1,0:T(8,128)(2,1)}, bf16[128,32,128]{2,1,0:T(8,128)(2,1)}, f32[2064,128]{1,0:T(8,128)S(1)}, f32[2064,128]{1,0:T(8,128)S(1)}) custom-call(bf16[16,128,128]{2,1,0:T(8,128)(2,1)S(1)} %get-tuple-element.142.refs_0_, ...), custom_call_target="tpu_custom_call", output_to_operand_aliasing={{2}: (7, {}), {3}: (8, {})} | custom-call | flops 67108864 | bytes 10780672 | tf_op jit(solution)/shard_map/last_gradients/pallas_call | solution.py:405
  (63 shorter events, 20.3 us)
Async XLA Ops:
  3.0 2.1 %collective-permute-start = (bf16[16,128,128]{2,1,0:T(8,128)(2,1)S(1)}, bf16[16,128,128]{2,1,0:T(8,128)(2,1)S(1)}, u32[]{:S(2)}, u32[]{:S(2)}) collective-permute-start(bf16[16,128,128]{2,1,0:T(8,128)(2,1)S(1)} %local_states.3), channel_id=1, source_target_pairs={{0,1},{1,0},{2,3},{3,2},{4,5},{5,4},{6,7},{7,6},{8,9},{9,8},{10,11... | collective-permute-start | bytes 1572872 | tf_op jit(solution)/shard_map/ppermute | solution.py:428
  5.1 4.8 %copy-start.2 = (f32[32,128]{1,0:T(8,128)S(1)}, f32[32,128]{1,0:T(8,128)}, u32[]{:S(2)}) copy-start(f32[32,128]{1,0:T(8,128)} %gain_ref.1) | copy-start | bytes 49156
  5.2 8.9 %collective-permute-start.2 = (bf16[4,128,128]{2,1,0:T(8,128)(2,1)S(1)}, bf16[4,128,128]{2,1,0:T(8,128)(2,1)S(1)}, u32[]{:S(2)}, u32[]{:S(2)}) collective-permute-start(bf16[4,128,128]{2,1,0:T(8,128)(2,1)S(1)} %get-tuple-element.105.rest_0_), channel_id=1, source_target_pairs={{0,4},{1,5},{2,6},{3,7},{4,0},{5,1},{6,2},{7,3},{8,12},{9,13},{10,... | collective-permute-start | bytes 393224 | tf_op jit(solution)/shard_map/ppermute | solution.py:428
  8.2 7.3 %collective-permute-start.3 = (bf16[4,128,128]{2,1,0:T(8,128)(2,1)S(1)}, bf16[4,128,128]{2,1,0:T(8,128)(2,1)S(1)}, u32[]{:S(2)}, u32[]{:S(2)}) collective-permute-start(bf16[4,128,128]{2,1,0:T(8,128)(2,1)S(1)} %get-tuple-element.106.rest_1_), channel_id=1, source_target_pairs={{0,6},{1,7},{2,4},{3,5},{4,2},{5,3},{6,0},{7,1},{8,14},{9,15},{10,... | collective-permute-start | bytes 393224 | tf_op jit(solution)/shard_map/ppermute | solution.py:428
  9.7 6.3 %collective-permute-start.1 = (bf16[4,128,128]{2,1,0:T(8,128)(2,1)S(1)}, bf16[4,128,128]{2,1,0:T(8,128)(2,1)S(1)}, u32[]{:S(2)}, u32[]{:S(2)}) collective-permute-start(bf16[4,128,128]{2,1,0:T(8,128)(2,1)S(1)} %get-tuple-element.108), channel_id=1, source_target_pairs={{0,2},{1,3},{2,0},{3,1},{4,6},{5,7},{6,4},{7,5},{8,10},{9,11},{10,... | collective-permute-start | bytes 393224 | tf_op jit(solution)/shard_map/ppermute | solution.py:428
  16.2 5.0 %collective-permute-start.4 = (bf16[4,128,128]{2,1,0:T(8,128)(2,1)S(1)}, bf16[4,128,128]{2,1,0:T(8,128)(2,1)S(1)}, u32[]{:S(2)}, u32[]{:S(2)}) collective-permute-start(bf16[4,128,128]{2,1,0:T(8,128)(2,1)S(1)} %fold_states.2.state_ref), channel_id=1, source_target_pairs={{0,8},{1,9},{2,10},{3,11},{4,12},{5,13},{6,14},{7,15},{8,0},{9,1},... | collective-permute-start | bytes 393224 | tf_op jit(solution)/shard_map/ppermute | solution.py:428
  21.3 6.9 %collective-permute-start.5 = (bf16[4,128,128]{2,1,0:T(8,128)(2,1)S(1)}, bf16[4,128,128]{2,1,0:T(8,128)(2,1)S(1)}, u32[]{:S(2)}, u32[]{:S(2)}) collective-permute-start(bf16[4,128,128]{2,1,0:T(8,128)(2,1)S(1)} %double_states.2), channel_id=1, source_target_pairs={{0,24},{1,25},{2,26},{3,27},{4,28},{5,29},{6,30},{7,31},{8,16},{9,... | collective-permute-start | bytes 393224 | tf_op jit(solution)/shard_map/ppermute | solution.py:428
  28.7 5.9 %collective-permute-start.8 = (bf16[4,128,128]{2,1,0:T(8,128)(2,1)S(1)}, bf16[4,128,128]{2,1,0:T(8,128)(2,1)S(1)}, u32[]{:S(2)}, u32[]{:S(2)}) collective-permute-start(bf16[4,128,128]{2,1,0:T(8,128)(2,1)S(1)} %get-tuple-element.116), channel_id=1, source_target_pairs={{0,6},{1,7},{2,4},{3,5},{4,2},{5,3},{6,0},{7,1},{8,14},{9,15},{10,... | collective-permute-start | bytes 393224 | tf_op jit(solution)/shard_map/ppermute | solution.py:428
  31.4 5.0 %collective-permute-start.6 = (bf16[4,128,128]{2,1,0:T(8,128)(2,1)S(1)}, bf16[4,128,128]{2,1,0:T(8,128)(2,1)S(1)}, u32[]{:S(2)}, u32[]{:S(2)}) collective-permute-start(bf16[4,128,128]{2,1,0:T(8,128)(2,1)S(1)} %get-tuple-element.110), channel_id=1, source_target_pairs={{0,2},{1,3},{2,0},{3,1},{4,6},{5,7},{6,4},{7,5},{8,10},{9,11},{10,... | collective-permute-start | bytes 393224 | tf_op jit(solution)/shard_map/ppermute | solution.py:428
  31.9 5.0 %collective-permute-start.7 = (bf16[4,128,128]{2,1,0:T(8,128)(2,1)S(1)}, bf16[4,128,128]{2,1,0:T(8,128)(2,1)S(1)}, u32[]{:S(2)}, u32[]{:S(2)}) collective-permute-start(bf16[4,128,128]{2,1,0:T(8,128)(2,1)S(1)} %get-tuple-element.111), channel_id=1, source_target_pairs={{0,4},{1,5},{2,6},{3,7},{4,0},{5,1},{6,2},{7,3},{8,12},{9,13},{10,... | collective-permute-start | bytes 393224 | tf_op jit(solution)/shard_map/ppermute | solution.py:428
  34.8 3.6 %collective-permute-start.10 = (bf16[8,128,128]{2,1,0:T(8,128)(2,1)S(1)}, bf16[8,128,128]{2,1,0:T(8,128)(2,1)S(1)}, u32[]{:S(2)}, u32[]{:S(2)}) collective-permute-start(bf16[8,128,128]{2,1,0:T(8,128)(2,1)S(1)} %get-tuple-element.121), channel_id=1, source_target_pairs={{0,1},{1,0},{2,3},{3,2},{4,5},{5,4},{6,7},{7,6},{8,9},{9,8},{10,11... | collective-permute-start | bytes 786440 | tf_op jit(solution)/shard_map/ppermute | solution.py:428
  35.7 3.6 %collective-permute-start.12 = (bf16[8,128,128]{2,1,0:T(8,128)(2,1)S(1)}, bf16[8,128,128]{2,1,0:T(8,128)(2,1)S(1)}, u32[]{:S(2)}, u32[]{:S(2)}) collective-permute-start(bf16[8,128,128]{2,1,0:T(8,128)(2,1)S(1)} %get-tuple-element.147), channel_id=1, source_target_pairs={{0,1},{1,0},{2,3},{3,2},{4,5},{5,4},{6,7},{7,6},{8,9},{9,8},{10,11... | collective-permute-start | bytes 786440 | tf_op jit(solution)/shard_map/ppermute | solution.py:428
  37.1 4.4 %collective-permute-start.9 = (bf16[8,128,128]{2,1,0:T(8,128)(2,1)S(1)}, bf16[8,128,128]{2,1,0:T(8,128)(2,1)S(1)}, u32[]{:S(2)}, u32[]{:S(2)}) collective-permute-start(bf16[8,128,128]{2,1,0:T(8,128)(2,1)S(1)} %get-tuple-element.120), channel_id=1, source_target_pairs={{0,1},{1,0},{2,3},{3,2},{4,5},{5,4},{6,7},{7,6},{8,9},{9,8},{10,11... | collective-permute-start | bytes 786440 | tf_op jit(solution)/shard_map/ppermute | solution.py:428
  37.9 4.3 %collective-permute-start.11 = (bf16[8,128,128]{2,1,0:T(8,128)(2,1)S(1)}, bf16[8,128,128]{2,1,0:T(8,128)(2,1)S(1)}, u32[]{:S(2)}, u32[]{:S(2)}) collective-permute-start(bf16[8,128,128]{2,1,0:T(8,128)(2,1)S(1)} %get-tuple-element.145), channel_id=1, source_target_pairs={{0,1},{1,0},{2,3},{3,2},{4,5},{5,4},{6,7},{7,6},{8,9},{9,8},{10,11... | collective-permute-start | bytes 786440 | tf_op jit(solution)/shard_map/ppermute | solution.py:428
  39.4 7.0 %collective-permute-start.15 = (bf16[4,128,128]{2,1,0:T(8,128)(2,1)S(1)}, bf16[4,128,128]{2,1,0:T(8,128)(2,1)S(1)}, u32[]{:S(2)}, u32[]{:S(2)}) collective-permute-start(bf16[4,128,128]{2,1,0:T(8,128)(2,1)S(1)} %get-tuple-element.149.rest_0_), channel_id=1, source_target_pairs={{0,6},{1,7},{2,4},{3,5},{4,2},{5,3},{6,0},{7,1},{8,14},{9,15},{10,... | collective-permute-start | bytes 393224 | tf_op jit(solution)/shard_map/ppermute | solution.py:428
  42.3 5.9 %collective-permute-start.13 = (bf16[4,128,128]{2,1,0:T(8,128)(2,1)S(1)}, bf16[4,128,128]{2,1,0:T(8,128)(2,1)S(1)}, u32[]{:S(2)}, u32[]{:S(2)}) collective-permute-start(bf16[4,128,128]{2,1,0:T(8,128)(2,1)S(1)} %get-tuple-element.150), channel_id=1, source_target_pairs={{0,2},{1,3},{2,0},{3,1},{4,6},{5,7},{6,4},{7,5},{8,10},{9,11},{10,... | collective-permute-start | bytes 393224 | tf_op jit(solution)/shard_map/ppermute | solution.py:428
  43.0 5.6 %collective-permute-start.14 = (bf16[4,128,128]{2,1,0:T(8,128)(2,1)S(1)}, bf16[4,128,128]{2,1,0:T(8,128)(2,1)S(1)}, u32[]{:S(2)}, u32[]{:S(2)}) collective-permute-start(bf16[4,128,128]{2,1,0:T(8,128)(2,1)S(1)} %get-tuple-element.151), channel_id=1, source_target_pairs={{0,4},{1,5},{2,6},{3,7},{4,0},{5,1},{6,2},{7,3},{8,12},{9,13},{10,... | collective-permute-start | bytes 393224 | tf_op jit(solution)/shard_map/ppermute | solution.py:428
  48.7 5.0 %collective-permute-start.16 = (bf16[4,128,128]{2,1,0:T(8,128)(2,1)S(1)}, bf16[4,128,128]{2,1,0:T(8,128)(2,1)S(1)}, u32[]{:S(2)}, u32[]{:S(2)}) collective-permute-start(bf16[4,128,128]{2,1,0:T(8,128)(2,1)S(1)} %fold_states.3.state_ref), channel_id=1, source_target_pairs={{0,8},{1,9},{2,10},{3,11},{4,12},{5,13},{6,14},{7,15},{8,0},{9,1},... | collective-permute-start | bytes 393224 | tf_op jit(solution)/shard_map/ppermute | solution.py:428
  53.9 6.9 %collective-permute-start.17 = (bf16[4,128,128]{2,1,0:T(8,128)(2,1)S(1)}, bf16[4,128,128]{2,1,0:T(8,128)(2,1)S(1)}, u32[]{:S(2)}, u32[]{:S(2)}) collective-permute-start(bf16[4,128,128]{2,1,0:T(8,128)(2,1)S(1)} %double_states.3), channel_id=1, source_target_pairs={{0,24},{1,25},{2,26},{3,27},{4,28},{5,29},{6,30},{7,31},{8,16},{9,... | collective-permute-start | bytes 393224 | tf_op jit(solution)/shard_map/ppermute | solution.py:428
  61.2 5.9 %collective-permute-start.20 = (bf16[4,128,128]{2,1,0:T(8,128)(2,1)S(1)}, bf16[4,128,128]{2,1,0:T(8,128)(2,1)S(1)}, u32[]{:S(2)}, u32[]{:S(2)}) collective-permute-start(bf16[4,128,128]{2,1,0:T(8,128)(2,1)S(1)} %get-tuple-element.161), channel_id=1, source_target_pairs={{0,6},{1,7},{2,4},{3,5},{4,2},{5,3},{6,0},{7,1},{8,14},{9,15},{10,... | collective-permute-start | bytes 393224 | tf_op jit(solution)/shard_map/ppermute | solution.py:428
  63.3 5.0 %collective-permute-start.18 = (bf16[4,128,128]{2,1,0:T(8,128)(2,1)S(1)}, bf16[4,128,128]{2,1,0:T(8,128)(2,1)S(1)}, u32[]{:S(2)}, u32[]{:S(2)}) collective-permute-start(bf16[4,128,128]{2,1,0:T(8,128)(2,1)S(1)} %get-tuple-element.156), channel_id=1, source_target_pairs={{0,2},{1,3},{2,0},{3,1},{4,6},{5,7},{6,4},{7,5},{8,10},{9,11},{10,... | collective-permute-start | bytes 393224 | tf_op jit(solution)/shard_map/ppermute | solution.py:428
  63.9 5.0 %collective-permute-start.19 = (bf16[4,128,128]{2,1,0:T(8,128)(2,1)S(1)}, bf16[4,128,128]{2,1,0:T(8,128)(2,1)S(1)}, u32[]{:S(2)}, u32[]{:S(2)}) collective-permute-start(bf16[4,128,128]{2,1,0:T(8,128)(2,1)S(1)} %get-tuple-element.157), channel_id=1, source_target_pairs={{0,4},{1,5},{2,6},{3,7},{4,0},{5,1},{6,2},{7,3},{8,12},{9,13},{10,... | collective-permute-start | bytes 393224 | tf_op jit(solution)/shard_map/ppermute | solution.py:428
  67.4 2.4 %collective-permute-start.22 = (bf16[8,128,128]{2,1,0:T(8,128)(2,1)S(1)}, bf16[8,128,128]{2,1,0:T(8,128)(2,1)S(1)}, u32[]{:S(2)}, u32[]{:S(2)}) collective-permute-start(bf16[8,128,128]{2,1,0:T(8,128)(2,1)S(1)} %get-tuple-element.173), channel_id=1, source_target_pairs={{0,1},{1,0},{2,3},{3,2},{4,5},{5,4},{6,7},{7,6},{8,9},{9,8},{10,11... | collective-permute-start | bytes 786440 | tf_op jit(solution)/shard_map/ppermute | solution.py:428
  69.0 1.6 %collective-permute-start.21 = (bf16[8,128,128]{2,1,0:T(8,128)(2,1)S(1)}, bf16[8,128,128]{2,1,0:T(8,128)(2,1)S(1)}, u32[]{:S(2)}, u32[]{:S(2)}) collective-permute-start(bf16[8,128,128]{2,1,0:T(8,128)(2,1)S(1)} %get-tuple-element.165), channel_id=1, source_target_pairs={{0,1},{1,0},{2,3},{3,2},{4,5},{5,4},{6,7},{7,6},{8,9},{9,8},{10,11... | collective-permute-start | bytes 786440 | tf_op jit(solution)/shard_map/ppermute | solution.py:428
  (3 other events, 11.5 us)
